TPU v7x, 32 devices: a whole 2x2x4 slice. The times are simulated.
32 devices in a mesh: region: 8 (over z, x), tm: 4 (over y, core).
Axes of the slice: x: 2, y: 2, z: 4, core: 2. Of those that a mesh axis runs over, the one named last changes fastest.
Arguments:
- tensor: bfloat16 [2048, 32, 2, 128], P('region'), may hold values from -6 to 6
- g_occ: bfloat16 [4, 1024, 128], P('tm', 'region'), may hold values from -0.375 to 0.375
- g_virt: bfloat16 [4, 1024, 128], P('tm', 'region'), may hold values from -0.375 to 0.375
- offsets: int32 [8, 2], P('region'), may hold values from -1 to 1, as said below
- pattern: int32 [8, 3], P('region'), may hold values from 0 to 1, as said below
Outputs:
- screened: float32 [4, 2048, 768], P('tm', 'region')
Inputs may be any that keep to these rules, and one draw needn't show every extreme that they name: Row r holds 2 distinct offsets in increasing order, and r + offset lies within 0 to 7. `pattern`: row r is (b[r-1], 1, b[r]) for bond bits b with b[-1] = b[7] = 0, so that the kept blocks are symmetric.
All inputs are finite; a program needn't handle non-finite values.
Results may differ from a plain program's by a relative error of at most 0.0039.
Values may be sent and summed in bfloat16 or wider, within the bound.
No kernel may reach another device: no remote copies, remote signals or barrier semaphores. Data moves between devices by JAX's collectives and lax.ppermute only.
A program may use at most 64 MiB of HBM per device.

v0:
```python
import math

import jax
import jax.numpy as jnp
from jax import lax
from jax.sharding import PartitionSpec as P

time_points = (0.1, 0.5, 1.5, 4.0)
time_weights = (0.2, 0.6, 1.2, 2.5)
omega_points = (0.2, 0.9, 2.5, 7.0)


def from_behind(block, axis, distance):
    devices = range(lax.axis_size(axis))
    route = [(i - distance, i) for i in devices if i - distance in devices]
    return lax.ppermute(block, axis, route)


def cosine_table():
    points = jnp.array(time_points, jnp.float32)
    weights = jnp.array(time_weights, jnp.float32)
    omegas = jnp.array(omega_points, jnp.float32)
    return weights[None, :] * jnp.cos(omegas[:, None] * points[None, :])


def contract(first_op, second_op):
    return lax.dot_general(
        first_op, second_op, (((1,), (1,)), ((), ())), preferred_element_type=jnp.float32
    )


def column_block(matrix, position):
    extent = matrix.shape[0]
    return matrix[:, (position + 1) * extent : (position + 2) * extent]


def combine(center_rows, below_rows, above_rows, mask_weights):
    sources = (below_rows, center_rows, above_rows)
    pieces = []
    for target in (-1, 0, 1):
        summed = column_block(center_rows, target)
        for middle in (-1, 0, 1):
            if abs(target - middle) <= 1:
                summed = summed + jnp.dot(
                    column_block(center_rows, middle),
                    column_block(sources[middle + 1], target - middle),
                    precision=lax.Precision.HIGHEST,
                    preferred_element_type=jnp.float32,
                )
        pieces.append(summed * mask_weights[target + 1])
    return jnp.concatenate(pieces, 1)


def local(tensor, g_occ, g_virt, offsets, pattern):
    rows_here = tensor.shape[0]
    mu_width = tensor.shape[1]
    blocks_here = tensor.shape[2]
    nu_width = tensor.shape[3]
    lam_width = g_occ.shape[2]
    prefactor = 1.0 / math.sqrt(2.0 * mu_width * lam_width) / (3.0 * rows_here) ** 0.25
    own_green = jnp.concatenate([g_occ[0], g_virt[0]], 1)
    nearby = {}
    for offset in (1, -1):
        far_occ, far_virt = from_behind((g_occ[0], g_virt[0]), "region", offset)
        nearby[offset] = jnp.concatenate([far_occ, far_virt], 1)
    candidates = jnp.stack([nearby[1], own_green, nearby[-1]], 0)
    wanted = offsets[0] + 1
    matches = wanted[:, None] == jnp.arange(3)[None, :]
    picked = jnp.sum(
        jnp.where(matches[:, :, None, None], candidates[None], jnp.zeros((), candidates.dtype)),
        axis=1,
    )
    rotated = jnp.dot(
        tensor.reshape(rows_here * mu_width, blocks_here * nu_width),
        picked.reshape(blocks_here * nu_width, 2 * lam_width),
        preferred_element_type=jnp.float32,
    )
    rotated = rotated.reshape(rows_here, mu_width, 2, lam_width)
    own_occ = rotated[:, :, 0].reshape(rows_here, mu_width * lam_width).astype(jnp.bfloat16)
    own_virt = rotated[:, :, 1].reshape(rows_here, mu_width * lam_width).astype(jnp.bfloat16)
    mask_weights = pattern[0].astype(jnp.float32)
    center = contract(own_occ, own_virt)
    middle = prefactor * (center + center.T)
    far_occ, far_virt = from_behind((own_occ, own_virt), "region", -1)
    right_block = (
        prefactor * (contract(own_occ, far_virt) + contract(own_virt, far_occ)) * mask_weights[2]
    )
    mirrored = from_behind(right_block, "region", 1)
    left_block = mirrored.T * mask_weights[0]
    pol_band = jnp.concatenate([left_block, middle, right_block], 1)
    cos_table = cosine_table()
    moment = lax.axis_index("tm")
    column = jnp.sum(
        jnp.where(jnp.arange(cos_table.shape[1])[None, :] == moment, cos_table, 0.0), axis=1
    )
    time_terms = column[:, None, None] * pol_band[None]
    freq_rows = lax.psum_scatter(time_terms, "tm", scatter_dimension=0, tiled=True)[0]
    neighbours = {}
    for offset in (1, -1):
        neighbours[offset] = from_behind(freq_rows, "region", offset)
    below_rows = neighbours[1]
    above_rows = neighbours[-1]
    result = combine(freq_rows, below_rows, above_rows, mask_weights)
    return result[None]


def solution(mesh):
    return jax.shard_map(
        local,
        mesh=mesh,
        in_specs=(
            P("region", None, None, None),
            P("tm", "region", None),
            P("tm", "region", None),
            P("region", None),
            P("region", None),
        ),
        out_specs=P("tm", "region", None),
        check_vma=False,
    )
```

profile of v0, /device:TPU:0, one launch (start us, length us, event | category | flops | bytes accessed | tf_op | source)
XLA Modules:
  0.0 256.3 jit_solution(12277495320632541914)
XLA Ops:
  6.5 4.8 %collective-permute-start = (bf16[128,128]{1,0:T(8,128)(2,1)}, bf16[128,128]{1,0:T(8,128)(2,1)S(1)}, u32[]{:S(2)}, u32[]{:S(2)}) collective-permute-start(bf16[128,128]{1,0:T(8,128)(2,1)} %bitcast.61), channel_id=1, source_target_pairs={{0,4},{4,8},{8,12},{12,16},{16,20},{20,24},{24,28},{1,5},{5,9},{9,... | collective-permute-start | bytes 98312 | tf_op jit(solution)/shard_map/ppermute | solution.py:16
  12.7 4.6 %collective-permute-start.1 = (bf16[128,128]{1,0:T(8,128)(2,1)}, bf16[128,128]{1,0:T(8,128)(2,1)S(1)}, u32[]{:S(2)}, u32[]{:S(2)}) collective-permute-start(bf16[128,128]{1,0:T(8,128)(2,1)} %bitcast.64), channel_id=1, source_target_pairs={{0,4},{4,8},{8,12},{12,16},{16,20},{20,24},{24,28},{1,5},{5,9},{9,... | collective-permute-start | bytes 98312 | tf_op jit(solution)/shard_map/ppermute | solution.py:16
  20.1 3.6 %collective-permute-done.3 = bf16[128,128]{1,0:T(8,128)(2,1)S(1)} collective-permute-done((bf16[128,128]{1,0:T(8,128)(2,1)}, bf16[128,128]{1,0:T(8,128)(2,1)S(1)}, u32[]{:S(2)}, u32[]{:S(2)}) %collective-permute-start.3) | collective-permute-done | bytes 32800 | tf_op jit(solution)/shard_map/ppermute | solution.py:16
  23.9 5.5 %convolution_bitcast_fusion = bf16[8192,256]{0,1:T(8,128)(2,1)} fusion(bf16[256,256]{1,0:T(8,128)(2,1)S(1)} %bitcast.60, bf16[1024,8,2,128]{3,2,1,0:T(2,128)(2,1)} %bitcast.54), kind=kOutput, calls=%fused_computation | convolution fusion | flops 1073741824 | bytes 8519680 | tf_op jit(solution)/shard_map/dot_general | solution.py:73
  29.4 6.4 %copy.36 = bf16[8192,256]{1,0:T(8,128)(2,1)} copy(bf16[8192,256]{0,1:T(8,128)(2,1)} %convolution_bitcast_fusion) | data formatting | bytes 8388608 | tf_op jit(solution)/shard_map/dot_general | solution.py:73
  35.7 7.0 %reshape.66 = bf16[256,32,2,128]{3,2,1,0:T(2,128)(2,1)} reshape(bf16[8192,256]{1,0:T(8,128)(2,1)} %copy.36) | data formatting | bytes 8388608 | tf_op jit(solution)/shard_map/reshape | solution.py:78
  42.7 12.5 %fusion.27 = (bf16[256,32,1,128]{3,2,1,0:T(2,128)(2,1)S(1)}, bf16[256,32,1,128]{3,2,1,0:T(2,128)(2,1)}) fusion(bf16[256,32,2,128]{3,2,1,0:T(2,128)(2,1)} %reshape.66), kind=kLoop, calls=%fused_computation.50 | loop fusion | bytes 8388608 | tf_op jit(solution)/shard_map/slice | solution.py:79
  55.2 2.4 copy.68
  57.7 3.0 %copy.38 = bf16[256,32,1,128]{0,3,1,2:T(8,128)(2,1)} copy(bf16[256,32,1,128]{3,0,1,2:T(8,128)(2,1)S(1)} %copy.68) | data formatting | bytes 4194304 | tf_op jit(solution)/shard_map/convert_element_type | solution.py:79
  61.9 5.9 %copy.67 = bf16[256,32,1,128]{3,0,1,2:T(8,128)(2,1)} copy(bf16[256,32,1,128]{3,2,1,0:T(2,128)(2,1)} %get-tuple-element.6) | data formatting | bytes 4194304
  67.9 4.1 %copy.40 = bf16[256,32,1,128]{0,3,1,2:T(8,128)(2,1)} copy(bf16[256,32,1,128]{3,0,1,2:T(8,128)(2,1)} %copy.67) | data formatting | bytes 4194304 | tf_op jit(solution)/shard_map/convert_element_type | solution.py:80
  74.7 37.6 %collective-permute-done.5 = bf16[256,4096]{0,1:T(8,128)(2,1)} collective-permute-done((bf16[256,4096]{0,1:T(8,128)(2,1)}, bf16[256,4096]{0,1:T(8,128)(2,1)}, u32[]{:S(2)}, u32[]{:S(2)}) %collective-permute-start.5) | collective-permute-done | bytes 2097184 | tf_op jit(solution)/shard_map/ppermute | solution.py:16
  112.3 3.1 %fusion.29 = f32[256,256]{0,1:T(8,128)S(1)} fusion(bf16[256,4096]{0,1:T(8,128)(2,1)} %bitcast.59, bf16[256,4096]{0,1:T(8,128)(2,1)} %collective-permute-done.5), kind=kOutput, calls=%fused_computation.52 | convolution fusion | flops 536870912 | bytes 4456448 | tf_op jit(solution)/shard_map/dot_general | solution.py:27
  115.4 38.9 %collective-permute-done.4 = bf16[256,4096]{0,1:T(8,128)(2,1)} collective-permute-done((bf16[256,4096]{0,1:T(8,128)(2,1)}, bf16[256,4096]{0,1:T(8,128)(2,1)}, u32[]{:S(2)}, u32[]{:S(2)}) %collective-permute-start.4) | collective-permute-done | bytes 2097184 | tf_op jit(solution)/shard_map/ppermute | solution.py:16
  154.3 2.5 fusion.10
  157.0 4.7 %collective-permute-start.6 = (f32[256,256]{1,0:T(8,128)S(1)}, f32[256,256]{1,0:T(8,128)S(1)}, u32[]{:S(2)}, u32[]{:S(2)}) collective-permute-start(f32[256,256]{1,0:T(8,128)S(1)} %copy.41), channel_id=1, source_target_pairs={{0,4},{4,8},{8,12},{12,16},{16,20},{20,24},{24,28},{1,5},{5,9},{9,... | collective-permute-start | bytes 786440 | tf_op jit(solution)/shard_map/ppermute | solution.py:16
  161.7 2.3 fusion.2
  166.4 1.9 broadcast_multiply_fusion
  168.4 39.3 %reduce-scatter.2.cloned.1.call-done = f32[1,256,768]{2,1,0:T(8,128)} async-done(((f32[4,256,768]{2,1,0:T(8,128)}), f32[1,256,768]{2,1,0:T(8,128)}) %reduce-scatter.2.cloned.1.call-update) | async-done | bytes 786448 | tf_op jit(solution)/shard_map/reduce_scatter | solution.py:97
  207.7 3.5 %collective-permute-start.7 = (f32[256,768]{1,0:T(8,128)}, f32[256,768]{1,0:T(8,128)S(1)}, u32[]{:S(2)}, u32[]{:S(2)}) collective-permute-start(f32[256,768]{1,0:T(8,128)} %bitcast.45), channel_id=1, source_target_pairs={{0,4},{4,8},{8,12},{12,16},{16,20},{20,24},{24,28},{1,5},{5,9},{9,... | collective-permute-start | bytes 2359304 | tf_op jit(solution)/shard_map/ppermute | solution.py:16
  212.5 1.4 fusion.19
  214.0 1.5 fusion.24
  215.4 1.4 convolution_add_fusion
  216.9 28.3 %collective-permute-done.7 = f32[256,768]{1,0:T(8,128)S(1)} collective-permute-done((f32[256,768]{1,0:T(8,128)}, f32[256,768]{1,0:T(8,128)S(1)}, u32[]{:S(2)}, u32[]{:S(2)}) %collective-permute-start.7) | collective-permute-done | bytes 786464 | tf_op jit(solution)/shard_map/ppermute | solution.py:16
  (46 shorter events, 15.7 us)
Async XLA Ops:
  6.5 201.2 %reduce-scatter.2.cloned.1.call-start = ((), (), s32[]{:S(2)}) async-start(), calls=%async_computation.1 | async-start | bytes 3932160 | tf_op jit(solution)/shard_map/reduce_scatter | solution.py:97
  6.5 13.5 %collective-permute-start = (bf16[128,128]{1,0:T(8,128)(2,1)}, bf16[128,128]{1,0:T(8,128)(2,1)S(1)}, u32[]{:S(2)}, u32[]{:S(2)}) collective-permute-start(bf16[128,128]{1,0:T(8,128)(2,1)} %bitcast.61), channel_id=1, source_target_pairs={{0,4},{4,8},{8,12},{12,16},{16,20},{20,24},{24,28},{1,5},{5,9},{9,... | collective-permute-start | bytes 98312 | tf_op jit(solution)/shard_map/ppermute | solution.py:16
  11.4 8.7 %collective-permute-start.2 = (bf16[128,128]{1,0:T(8,128)(2,1)}, bf16[128,128]{1,0:T(8,128)(2,1)S(1)}, u32[]{:S(2)}, u32[]{:S(2)}) collective-permute-start(bf16[128,128]{1,0:T(8,128)(2,1)} %bitcast.62), channel_id=1, source_target_pairs={{4,0},{8,4},{12,8},{16,12},{20,16},{24,20},{28,24},{5,1},{9,5},{13... | collective-permute-start | bytes 98312 | tf_op jit(solution)/shard_map/ppermute | solution.py:16
  12.7 7.4 %collective-permute-start.1 = (bf16[128,128]{1,0:T(8,128)(2,1)}, bf16[128,128]{1,0:T(8,128)(2,1)S(1)}, u32[]{:S(2)}, u32[]{:S(2)}) collective-permute-start(bf16[128,128]{1,0:T(8,128)(2,1)} %bitcast.64), channel_id=1, source_target_pairs={{0,4},{4,8},{8,12},{12,16},{16,20},{20,24},{24,28},{1,5},{5,9},{9,... | collective-permute-start | bytes 98312 | tf_op jit(solution)/shard_map/ppermute | solution.py:16
  17.2 6.5 %collective-permute-start.3 = (bf16[128,128]{1,0:T(8,128)(2,1)}, bf16[128,128]{1,0:T(8,128)(2,1)S(1)}, u32[]{:S(2)}, u32[]{:S(2)}) collective-permute-start(bf16[128,128]{1,0:T(8,128)(2,1)} %bitcast.65), channel_id=1, source_target_pairs={{4,0},{8,4},{12,8},{16,12},{20,16},{24,20},{28,24},{5,1},{9,5},{13... | collective-permute-start | bytes 98312 | tf_op jit(solution)/shard_map/ppermute | solution.py:16
  60.6 51.7 %collective-permute-start.5 = (bf16[256,4096]{0,1:T(8,128)(2,1)}, bf16[256,4096]{0,1:T(8,128)(2,1)}, u32[]{:S(2)}, u32[]{:S(2)}) collective-permute-start(bf16[256,4096]{0,1:T(8,128)(2,1)} %bitcast.56), channel_id=1, source_target_pairs={{4,0},{8,4},{12,8},{16,12},{20,16},{24,20},{28,24},{5,1},{9,5},{13... | collective-permute-start | bytes 6291464 | tf_op jit(solution)/shard_map/ppermute | solution.py:16
  67.8 5.4 %copy-start.5 = (s32[1,3]{1,0:T(1,128)S(1)}, s32[1,3]{1,0:T(1,128)}, u32[]{:S(2)}) copy-start(s32[1,3]{1,0:T(1,128)} %param.12) | copy-start | bytes 40
  67.8 6.6 %copy-start.2 = (f32[4]{0:T(128)S(1)}, f32[4]{0:T(128)}, u32[]{:S(2)}) copy-start(f32[4]{0:T(128)} %constant.19.clone) | copy-start | bytes 52
  67.8 6.6 %copy-start.3 = (f32[4]{0:T(128)S(1)}, f32[4]{0:T(128)}, u32[]{:S(2)}) copy-start(f32[4]{0:T(128)} %constant.20.clone) | copy-start | bytes 52
  67.9 6.6 %copy-start.4 = (f32[4]{0:T(128)S(1)}, f32[4]{0:T(128)}, u32[]{:S(2)}) copy-start(f32[4]{0:T(128)} %constant.21.clone) | copy-start | bytes 52
  72.0 82.3 %collective-permute-start.4 = (bf16[256,4096]{0,1:T(8,128)(2,1)}, bf16[256,4096]{0,1:T(8,128)(2,1)}, u32[]{:S(2)}, u32[]{:S(2)}) collective-permute-start(bf16[256,4096]{0,1:T(8,128)(2,1)} %bitcast.58), channel_id=1, source_target_pairs={{4,0},{8,4},{12,8},{16,12},{20,16},{24,20},{28,24},{5,1},{9,5},{13... | collective-permute-start | bytes 6291464 | tf_op jit(solution)/shard_map/ppermute | solution.py:16
  74.7 79.6 %copy-start.1 = (bf16[256,32,1,128]{0,3,1,2:T(8,128)(2,1)S(1)}, bf16[256,32,1,128]{0,3,1,2:T(8,128)(2,1)}, u32[]{:S(2)}) copy-start(bf16[256,32,1,128]{0,3,1,2:T(8,128)(2,1)} %copy.38) | copy-start | bytes 6291460
  157.0 8.4 %collective-permute-start.6 = (f32[256,256]{1,0:T(8,128)S(1)}, f32[256,256]{1,0:T(8,128)S(1)}, u32[]{:S(2)}, u32[]{:S(2)}) collective-permute-start(f32[256,256]{1,0:T(8,128)S(1)} %copy.41), channel_id=1, source_target_pairs={{0,4},{4,8},{8,12},{12,16},{16,20},{20,24},{24,28},{1,5},{5,9},{9,... | collective-permute-start | bytes 786440 | tf_op jit(solution)/shard_map/ppermute | solution.py:16
  207.7 37.5 %copy-start = (f32[1,256,768]{2,1,0:T(8,128)S(1)}, f32[1,256,768]{2,1,0:T(8,128)}, u32[]{:S(2)}) copy-start(f32[1,256,768]{2,1,0:T(8,128)} %reduce-scatter.2.cloned.1.call-done) | copy-start | bytes 2359300
  207.7 37.5 %collective-permute-start.7 = (f32[256,768]{1,0:T(8,128)}, f32[256,768]{1,0:T(8,128)S(1)}, u32[]{:S(2)}, u32[]{:S(2)}) collective-permute-start(f32[256,768]{1,0:T(8,128)} %bitcast.45), channel_id=1, source_target_pairs={{0,4},{4,8},{8,12},{12,16},{16,20},{20,24},{24,28},{1,5},{5,9},{9,... | collective-permute-start | bytes 2359304 | tf_op jit(solution)/shard_map/ppermute | solution.py:16
  211.2 35.3 %collective-permute-start.8 = (f32[256,768]{1,0:T(8,128)}, f32[256,768]{1,0:T(8,128)S(1)}, u32[]{:S(2)}, u32[]{:S(2)}) collective-permute-start(f32[256,768]{1,0:T(8,128)} %bitcast.46), channel_id=1, source_target_pairs={{4,0},{8,4},{12,8},{16,12},{20,16},{24,20},{28,24},{5,1},{9,5},{13... | collective-permute-start | bytes 2359304 | tf_op jit(solution)/shard_map/ppermute | solution.py:16
Sparse Core Ops, SparseCore 0:
  168.5 39.1 reduce-scatter.1
where the time goes:
time: 257 us; the launch traced here: 256 us
  waiting for transfers between devices  149 us (58%)
  local copies, waits for them, and re-layouts  42.4 us (16%)
  starting transfers between devices  24.1 us (9%)
  matrix products  21.1 us (8%)
  between operations  14.3 us (6%)
  other arithmetic  5.52 us (2%)
    ppermute x9, waiting for transfers between devices, from_behind(): return lax.ppermute(block, axis, route)  110 us
    reduce_scatter x1, waiting for transfers between devices, local(): lax.psum_scatter(time_terms, 'tm', scatter_dimension=0, tiled=True)[0]  39.3 us
    ppermute x9, starting transfers between devices, from_behind(): return lax.ppermute(block, axis, route)  24.1 us
    slice x1, local copies, waits for them, and re-layouts, local(): rotated[:, :, 0].reshape(rows_here, mu_width * lam_width)  12.5 us
    unnamed x14, local copies, waits for them, and re-layouts  8.4 us
    dot_general x3, matrix products, contract(): lax.dot_general(first_op, second_op, (((1,), (1,)), ((), ())), preferred_...  8.01 us
    dot_general x7, matrix products, combine(): jnp.dot(column_block(center_rows, middle), column_block(sources[middle +...  7.63 us
    reshape x1, local copies, waits for them, and re-layouts, local(): rotated = rotated.reshape(rows_here, mu_width, 2, lam_width)  6.98 us
  transfers between devices with their start and end apart: 10, of which 6 were waited for; matrix products, arithmetic and copies ran while one was open for 9% of the time, Pallas kernels for 0%

commit v1 on v0

v1 whole, which is shorter than its diff:
```python
import functools
import math

import jax
import jax.numpy as jnp
import numpy as np
from jax import lax
from jax.experimental import pallas as pl
from jax.experimental.pallas import tpu as pltpu
from jax.sharding import PartitionSpec as P

time_points = (0.1, 0.5, 1.5, 4.0)
time_weights = (0.2, 0.6, 1.2, 2.5)
omega_points = (0.2, 0.9, 2.5, 7.0)

f32, bf16 = jnp.float32, jnp.bfloat16
VMEM_BYTES = 40 * 2**20


def cosine_table():
    points = np.array(time_points, np.float32)
    weights = np.array(time_weights, np.float32)
    omegas = np.array(omega_points, np.float32)
    return weights[None, :] * np.cos(omegas[:, None] * points[None, :])


def shift(block, distance):
    devices = range(lax.axis_size("region"))
    route = [(i - distance, i) for i in devices if i - distance in devices]
    return lax.ppermute(block, "region", route)


def partner(block, bit):
    return lax.ppermute(block, "tm", [(i, i ^ bit) for i in range(lax.axis_size("tm"))])


def mm(a, b):
    return jnp.dot(a, b, preferred_element_type=f32)


def mm_nt(a, b):
    return lax.dot_general(a, b, (((1,), (1,)), ((), ())), preferred_element_type=f32)


def spec_all(count):
    return [pl.BlockSpec(memory_space=pltpu.VMEM)] * count


SMEM = pl.BlockSpec(memory_space=pltpu.SMEM)


def relayout_kernel(mus, kb, x_ref, out_ref, wide):
    wide[...] = x_ref[...].astype(f32)
    rows = out_ref.shape[1]
    nu = x_ref.shape[1]
    for mu in range(mus):
        for k in range(kb):
            part = wide[pl.ds(mu * kb + k, rows, stride=mus * kb), :]
            out_ref[mu, :, k * nu : (k + 1) * nu] = part.astype(bf16)


def relayout(tensor, steps):
    rows, mus, kb, nu = tensor.shape
    part = rows // steps
    return pl.pallas_call(
        functools.partial(relayout_kernel, mus, kb),
        grid=(steps,),
        out_shape=jax.ShapeDtypeStruct((mus, rows, kb * nu), bf16),
        in_specs=[pl.BlockSpec((part * mus * kb, nu), lambda i: (i, 0))],
        out_specs=pl.BlockSpec((mus, part, kb * nu), lambda i: (0, i, 0)),
        scratch_shapes=[pltpu.VMEM((part * mus * kb, nu), f32)],
        compiler_params=pltpu.CompilerParams(vmem_limit_bytes=VMEM_BYTES),
        cost_estimate=pl.CostEstimate(flops=0, bytes_accessed=4 * tensor.size, transcendentals=0),
        name="relayout",
    )(tensor.reshape(rows * mus * kb, nu))


def weights_kernel(n, where, table, *refs):
    greens, (center_ref, right_ref, terms) = refs[:n], refs[n:]
    nu = greens[0].shape[1] // 2
    me = where[0]
    own = [where[1 + s] + 1 for s in range(2)]
    following = [where[3 + s] + 2 for s in range(2)]

    def pick(green, places):
        occ = jnp.concatenate([green[p, :nu, :] for p in places], 0)
        virt = jnp.concatenate([green[p, nu:, :] for p in places], 0)
        return jnp.concatenate([occ, virt], 1), jnp.concatenate([virt, occ], 1)

    center = None
    for i in range(n):
        first, first_swapped = pick(greens[i], own)
        _, second_swapped = pick(greens[i], following)
        term = table[me, me ^ i] * mm_nt(first, first_swapped)
        center = term if center is None else center + term
        terms[i] = mm_nt(second_swapped, first)
    center_ref[...] = center.astype(bf16)
    size = center_ref.shape[0]
    for q in range(n):
        total = table[me ^ q, me] * terms[0]
        for i in range(1, n):
            total = total + table[me ^ q, me ^ i] * terms[i]
        right_ref[:, q * size : (q + 1) * size] = total.astype(bf16)


def weights(where, greens):
    n = len(greens)
    size = 2 * greens[0].shape[1] // 2
    return pl.pallas_call(
        functools.partial(weights_kernel, n),
        out_shape=[
            jax.ShapeDtypeStruct((size, size), bf16),
            jax.ShapeDtypeStruct((size, n * size), bf16),
        ],
        in_specs=[SMEM, SMEM] + spec_all(n),
        out_specs=spec_all(2),
        scratch_shapes=[pltpu.VMEM((n, size, size), f32)],
        compiler_params=pltpu.CompilerParams(vmem_limit_bytes=VMEM_BYTES),
        cost_estimate=pl.CostEstimate(
            flops=4 * n * size**3, bytes_accessed=n * size**2 * 4, transcendentals=0
        ),
        name="weights",
    )(where, jnp.asarray(cosine_table()), *greens)


def center_kernel(scale, rows_ref, weight_ref, out_ref, low_ref, total):
    step = pl.program_id(0)
    mus, rows, width = rows_ref.shape
    turned = mm(rows_ref[...].reshape(mus * rows, width), weight_ref[...]).astype(bf16)
    acc = mm_nt(rows_ref[0], turned[:rows])
    for mu in range(1, mus):
        acc = acc + mm_nt(rows_ref[mu], turned[mu * rows : (mu + 1) * rows])

    @pl.when(step == 0)
    def _():
        total[...] = acc

    @pl.when(step > 0)
    def _():
        total[...] += acc

    @pl.when(step == pl.num_programs(0) - 1)
    def _():
        out_ref[...] = scale * total[...]
        low_ref[...] = (scale * total[...]).astype(bf16)


def center_block(scale, turned_rows, weight, steps):
    mus, rows, width = turned_rows.shape
    part = mus // steps
    return pl.pallas_call(
        functools.partial(center_kernel, scale),
        grid=(steps,),
        out_shape=[
            jax.ShapeDtypeStruct((rows, rows), f32),
            jax.ShapeDtypeStruct((rows, rows), bf16),
        ],
        in_specs=[
            pl.BlockSpec((part, rows, width), lambda i: (i, 0, 0)),
            pl.BlockSpec((width, width), lambda i: (0, 0)),
        ],
        out_specs=[pl.BlockSpec((rows, rows), lambda i: (0, 0))] * 2,
        scratch_shapes=[pltpu.VMEM((rows, rows), f32)],
        compiler_params=pltpu.CompilerParams(vmem_limit_bytes=VMEM_BYTES),
        cost_estimate=pl.CostEstimate(
            flops=2 * mus * rows * width * (width + rows),
            bytes_accessed=2 * mus * rows * width,
            transcendentals=0,
        ),
        name="center",
    )(turned_rows, weight)


def right_kernel(n, mus, kb, steps, first, last, scale, *refs):
    far_ref, weight_ref, rows_ref = refs[:3]
    refs = refs[3:]
    if not first:
        before_ref, refs = refs[0], refs[1:]
    outs, (wide, total) = refs[:-2], refs[-2:]
    step = pl.program_id(0)
    part = mus // steps
    nu = far_ref.shape[1]
    cols = far_ref.shape[0] // (mus * kb)
    width = kb * nu

    @pl.when(step == 0)
    def _():
        wide[...] = far_ref[...].astype(f32)
        if first:
            total[...] = jnp.zeros_like(total)
        else:
            total[...] = before_ref[...]

    pieces = []
    for mu in range(part):
        line = [
            wide[pl.ds((step * part + mu) * kb + k, cols, stride=mus * kb), :] for k in range(kb)
        ]
        pieces.append(jnp.concatenate(line, 1).astype(bf16))
    turned = mm(jnp.concatenate(pieces, 0), weight_ref[...]).astype(bf16)
    acc = total[...]
    for mu in range(part):
        rows = turned[mu * cols : (mu + 1) * cols]
        stacked = jnp.concatenate([rows[:, q * width : (q + 1) * width] for q in range(n)], 0)
        acc = acc + mm_nt(stacked, rows_ref[mu])
    total[...] = acc

    @pl.when(step == steps - 1)
    def _():
        if last:
            for q in range(n):
                outs[q][...] = (scale * total[q * cols : (q + 1) * cols, :]).astype(bf16)
        else:
            outs[0][...] = total[...]


def right_part(scale, far, weight, turned_rows, before, chunk, last, steps):
    cols, mus, kb, nu = far.shape
    _, rows, width = turned_rows.shape
    n = weight.shape[1] // width
    part = mus // steps
    first = before is None
    whole = lambda *shape: pl.BlockSpec(shape, lambda i: (0,) * len(shape))
    operands = [far.reshape(cols * mus * kb, nu), weight, turned_rows]
    in_specs = [
        whole(cols * mus * kb, nu),
        whole(width, n * width),
        pl.BlockSpec((part, rows, width), lambda i: (chunk * steps + i, 0, 0)),
    ]
    if not first:
        operands.append(before)
        in_specs.append(whole(n * cols, rows))
    if last:
        out_shape = [jax.ShapeDtypeStruct((cols, rows), bf16)] * n
        out_specs = [whole(cols, rows)] * n
    else:
        out_shape = [jax.ShapeDtypeStruct((n * cols, rows), f32)]
        out_specs = [whole(n * cols, rows)]
    return pl.pallas_call(
        functools.partial(right_kernel, n, mus, kb, steps, first, last, scale),
        grid=(steps,),
        out_shape=out_shape,
        in_specs=in_specs,
        out_specs=out_specs,
        scratch_shapes=[
            pltpu.VMEM((cols * mus * kb, nu), f32),
            pltpu.VMEM((n * cols, rows), f32),
        ],
        compiler_params=pltpu.CompilerParams(vmem_limit_bytes=VMEM_BYTES),
        cost_estimate=pl.CostEstimate(
            flops=2 * mus * cols * n * width * (width + rows),
            bytes_accessed=2 * mus * rows * width,
            transcendentals=0,
        ),
        name="right",
    )(*operands)


def split(value):
    high = value.astype(bf16)
    return high, (value - high.astype(f32)).astype(bf16)


def screen_kernel(n, where, center_ref, below_ref, above_ref, left_ref, *refs):
    pieces, (out_ref, left, right_t) = refs[:n], refs[n:]
    me = where[0]
    cols = pieces[0].shape[0]
    size = center_ref.shape[0]
    for i in range(n):
        start = pl.multiple_of((me ^ i) * cols, cols)
        left[pl.ds(start, cols), :] = left_ref[i]
        right_t[pl.ds(start, cols), :] = pieces[i][...]
    masks = [where[1 + e].astype(f32) for e in range(3)]
    lower = left[...] * masks[0].astype(bf16)
    upper = right_t[...].T * masks[2].astype(bf16)
    center = center_ref[...]
    high, low = split(center)
    out_ref[0, :, :size] = masks[0] * (
        lower.astype(f32) + mm(lower, below_ref[...]) + mm(high, lower) + mm(low, lower)
    )
    out_ref[0, :, size : 2 * size] = masks[1] * (
        center
        + mm_nt(lower, lower)
        + mm_nt(upper, upper)
        + mm(high, high)
        + mm(high, low)
        + mm(low, high)
    )
    out_ref[0, :, 2 * size :] = masks[2] * (
        upper.astype(f32) + mm(upper, above_ref[...]) + mm(high, upper) + mm(low, upper)
    )


def screen(where, center, below, above, left, pieces):
    n = len(pieces)
    size = center.shape[0]
    return pl.pallas_call(
        functools.partial(screen_kernel, n),
        out_shape=jax.ShapeDtypeStruct((1, size, 3 * size), f32),
        in_specs=[SMEM] + spec_all(4 + n),
        out_specs=pl.BlockSpec(memory_space=pltpu.VMEM),
        scratch_shapes=[pltpu.VMEM((size, size), bf16)] * 2,
        compiler_params=pltpu.CompilerParams(vmem_limit_bytes=VMEM_BYTES),
        cost_estimate=pl.CostEstimate(
            flops=22 * size**3, bytes_accessed=16 * size**2, transcendentals=0
        ),
        name="screen",
    )(where, center, below, above, left, *pieces)


def local(tensor, g_occ, g_virt, offsets, pattern):
    rows, mus, kb, nu = tensor.shape
    lam = g_occ.shape[2]
    n = lax.axis_size("tm")
    assert n & (n - 1) == 0 and rows % n == 0
    me = lax.axis_index("tm")
    scale = 1.0 / math.sqrt(2.0 * mus * lam) / (3.0 * rows) ** 0.25
    cols = rows // n
    chunks = 2
    far = []
    for c in range(chunks):
        start = (me * cols, c * (mus // chunks), 0, 0)
        slab = lax.dynamic_slice(tensor, start, (cols, mus // chunks, kb, nu))
        far.append(shift(slab, -1))

    note = jnp.zeros((16, lam), bf16).at[:1, :kb].set(offsets.astype(bf16))
    parcel = jnp.concatenate([g_occ[0], g_virt[0], note], 0)
    size = 2 * nu
    above, below, second = shift(parcel, -1), shift(parcel, 1), shift(parcel, -2)
    stack = jnp.stack([below[:size], parcel[:size], above[:size], second[:size]], 0)
    next_offsets = above[size, :kb].astype(jnp.int32)
    greens = {0: stack}
    bit = n // 2
    while bit:
        for i in list(greens):
            greens[i ^ bit] = partner(greens[i], bit)
        bit //= 2
    where = jnp.concatenate([me[None].astype(jnp.int32), offsets[0], next_offsets])
    center_weight, right_weight = weights(where, [greens[i] for i in range(n)])

    turned_rows = relayout(tensor, 8)
    center, center_low = center_block(scale, turned_rows, center_weight, 4)
    center_below, center_above = shift(center_low, 1), shift(center_low, -1)

    before = None
    for c in range(chunks):
        last = c == chunks - 1
        parts = right_part(scale, far[c], right_weight, turned_rows, before, c, last, 2)
        before = parts[0]
    pieces = [parts[0]] + [partner(parts[i], i) for i in range(1, n)]
    left = shift(jnp.stack(pieces, 0), 1)
    places = jnp.concatenate([me[None].astype(jnp.int32), pattern[0]])
    return screen(places, center, center_below, center_above, left, pieces)


def solution(mesh):
    return jax.shard_map(
        local,
        mesh=mesh,
        in_specs=(
            P("region", None, None, None),
            P("tm", "region", None),
            P("tm", "region", None),
            P("region", None),
            P("region", None),
        ),
        out_specs=P("tm", "region", None),
        check_vma=False,
    )
```

time: 257 us -> 69.3 us (0.27)
  waiting for transfers between devices: 149 us -> 18 us
  local copies, waits for them, and re-layouts: 42.4 us -> 4.15 us
  matrix products: 21.1 us -> 0 us
  Pallas kernels: 0 us -> 18.2 us
  between operations: 14.3 us -> 0.23 us
  other arithmetic: 5.52 us -> 2.43 us
    ppermute x9 -> x14, waiting for transfers between devices: 110 us -> 18 us  [the longest x8 16.7 us: shift(): return lax.ppermute(block, 'region', route)]
    reduce_scatter x1 -> x0, waiting for transfers between devices: 39.3 us -> none  [local(): lax.psum_scatter(time_terms, 'tm', scatter_dimension=0, tiled=True)[0]]
    dot_general x11 -> x0, matrix products: 21.1 us -> none  [the longest x3 8.01 us: contract(): lax.dot_general(first_op, second_op, (((1,), (1,)), ((), ())), preferred_...]
    pallas_call x0 -> x6, Pallas kernels: none -> 18.2 us  [the longest x1 5.69 us: relayout(): pl.pallas_call(functools.partial(relayout_kernel, mus, kb), grid=(steps,)...]
    slice x2 -> x0, local copies, waits for them, and re-layouts: 13.1 us -> none  [the longest x1 12.5 us: local(): rotated[:, :, 0].reshape(rows_here, mu_width * lam_width)]
    convert_element_type x2 -> x0, local copies, waits for them, and re-layouts: 7.08 us -> none  [the longest x1 4.12 us: local(): rotated[:, :, 1].reshape(rows_here, mu_width * lam_width)]
    reshape x1 -> x0, local copies, waits for them, and re-layouts: 6.98 us -> none  [local(): rotated = rotated.reshape(rows_here, mu_width, 2, lam_width)]
    dot_general x2 -> x0, local copies, waits for them, and re-layouts: 6.5 us -> none  [the longest x1 6.37 us: local(): jnp.dot(tensor.reshape(rows_here * mu_width, blocks_here * nu_width), pic...]
  transfers between devices with their start and end apart: 10 -> 14, of which waited for: 6 -> 7; matrix products, arithmetic and copies ran while one was open for 9% -> 4% of each run, Pallas kernels for 0% -> 20%
where the time goes in v1:
time: 69.3 us; the launch traced here: 68.8 us
  starting transfers between devices  25.8 us (37%)
  Pallas kernels  18.2 us (26%)
  waiting for transfers between devices  18 us (26%)
  local copies, waits for them, and re-layouts  4.15 us (6%)
  other arithmetic  2.43 us (4%)
    ppermute x8, starting transfers between devices, shift(): return lax.ppermute(block, 'region', route)  21.3 us
    ppermute x8, waiting for transfers between devices, shift(): return lax.ppermute(block, 'region', route)  16.7 us
    pallas_call x1, Pallas kernels, relayout(): pl.pallas_call(functools.partial(relayout_kernel, mus, kb), grid=(steps,)...  5.69 us
    pallas_call x2, Pallas kernels, right_part(): pl.pallas_call(functools.partial(right_kernel, n, mus, kb, steps, first,...  5.5 us
    ppermute x6, starting transfers between devices, partner(): lax.ppermute(block, 'tm', [(i, i ^ bit) for i in range(lax.axis_size('tm'...  4.52 us
    pallas_call x1, Pallas kernels, center_block(): pl.pallas_call(functools.partial(center_kernel, scale), grid=(steps,), ou...  3.85 us
    unnamed x8, local copies, waits for them, and re-layouts  2.2 us
    pallas_call x1, Pallas kernels, screen(): pl.pallas_call(functools.partial(screen_kernel, n), out_shape=jax.ShapeDt...  1.98 us
  transfers between devices with their start and end apart: 14, of which 7 were waited for; matrix products, arithmetic and copies ran while one was open for 4% of the time, Pallas kernels for 20%

profile of v1, /device:TPU:0, one launch (start us, length us, event | category | flops | bytes accessed | tf_op | source)
XLA Modules:
  0.0 68.8 jit_solution(9401810419096856227)
XLA Ops:
  1.4 1.3 %collective-permute-start.2 = (bf16[272,128]{1,0:T(8,128)(2,1)S(1)}, bf16[272,128]{1,0:T(8,128)(2,1)S(1)}, u32[]{:S(2)}, u32[]{:S(2)}) collective-permute-start(bf16[272,128]{1,0:T(8,128)(2,1)S(1)} %fusion.1), channel_id=1, source_target_pairs={{8,0},{12,4},{16,8},{20,12},{24,16},{28,20},{9,1},{13,5},{17,9},{2... | collective-permute-start | bytes 208904 | tf_op jit(solution)/shard_map/ppermute | solution.py:30
  2.7 4.8 %collective-permute-start.1 = (bf16[272,128]{1,0:T(8,128)(2,1)S(1)}, bf16[272,128]{1,0:T(8,128)(2,1)S(1)}, u32[]{:S(2)}, u32[]{:S(2)}) collective-permute-start(bf16[272,128]{1,0:T(8,128)(2,1)S(1)} %fusion.1), channel_id=1, source_target_pairs={{0,4},{4,8},{8,12},{12,16},{16,20},{20,24},{24,28},{1,5},{5,9},{9,... | collective-permute-start | bytes 208904 | tf_op jit(solution)/shard_map/ppermute | solution.py:30
  7.6 1.3 %collective-permute-start = (bf16[272,128]{1,0:T(8,128)(2,1)S(1)}, bf16[272,128]{1,0:T(8,128)(2,1)S(1)}, u32[]{:S(2)}, u32[]{:S(2)}) collective-permute-start(bf16[272,128]{1,0:T(8,128)(2,1)S(1)} %fusion.1), channel_id=1, source_target_pairs={{4,0},{8,4},{12,8},{16,12},{20,16},{24,20},{28,24},{5,1},{9,5},{13... | collective-permute-start | bytes 208904 | tf_op jit(solution)/shard_map/ppermute | solution.py:30
  8.9 0.8 %maximum_bitcast_fusion = bf16[1,256,128]{2,1,0:T(8,128)(2,1)S(1)} fusion(bf16[128,128]{1,0:T(8,128)(2,1)} %bitcast.33, bf16[128,128]{1,0:T(8,128)(2,1)} %bitcast.35), kind=kLoop, calls=%fused_computation.8 | loop fusion | flops 131072 | bytes 131072 | tf_op jit(solution)/shard_map/stack | solution.py:330
  9.7 4.2 %collective-permute-done = bf16[272,128]{1,0:T(8,128)(2,1)S(1)} collective-permute-done((bf16[272,128]{1,0:T(8,128)(2,1)S(1)}, bf16[272,128]{1,0:T(8,128)(2,1)S(1)}, u32[]{:S(2)}, u32[]{:S(2)}) %collective-permute-start) | collective-permute-done | bytes 69664 | tf_op jit(solution)/shard_map/ppermute | solution.py:30
  14.0 2.0 %collective-permute-start.4 = (bf16[4,256,128]{2,1,0:T(8,128)(2,1)S(1)}, bf16[4,256,128]{2,1,0:T(8,128)(2,1)S(1)}, u32[]{:S(2)}, u32[]{:S(2)}) collective-permute-start(bf16[4,256,128]{2,1,0:T(8,128)(2,1)S(1)} %pad_maximum_fusion.refs_0_), channel_id=1, source_target_pairs={{0,2},{1,3},{2,0},{3,1},{4,6},{5,7},{6,4},{7,5},{8,10},{9,11},{10,... | collective-permute-start | bytes 786440 | tf_op jit(solution)/shard_map/ppermute | solution.py:34
  16.0 1.9 %constant_dynamic-slice_fusion.1 = (bf16[64,16,2,128]{3,2,1,0:T(2,128)(2,1)S(1)}, bf16[64,16,2,128]{3,2,1,0:T(2,128)(2,1)S(1)}) fusion(bf16[256,32,2,128]{3,2,1,0:T(2,128)(2,1)} %param.8, s32[]{:T(128)S(6)} %select_n.4), kind=kLoop, calls=%fused_computation.14 | loop fusion | bytes 2097156 | tf_op jit(solution)/shard_map/dynamic_slice | solution.py:323
  18.0 1.3 %collective-permute-start.9 = (bf16[64,16,2,128]{3,2,1,0:T(2,128)(2,1)S(1)}, bf16[64,16,2,128]{3,2,1,0:T(2,128)(2,1)S(1)}, u32[]{:S(2)}, u32[]{:S(2)}) collective-permute-start(bf16[64,16,2,128]{3,2,1,0:T(2,128)(2,1)S(1)} %get-tuple-element.33), channel_id=1, source_target_pairs={{4,0},{8,4},{12,8},{16,12},{20,16},{24,20},{28,24},{5,1},{9,5},{13... | collective-permute-start | bytes 1572872 | tf_op jit(solution)/shard_map/ppermute | solution.py:30
  19.3 1.3 %collective-permute-start.8 = (bf16[64,16,2,128]{3,2,1,0:T(2,128)(2,1)S(1)}, bf16[64,16,2,128]{3,2,1,0:T(2,128)(2,1)S(1)}, u32[]{:S(2)}, u32[]{:S(2)}) collective-permute-start(bf16[64,16,2,128]{3,2,1,0:T(2,128)(2,1)S(1)} %get-tuple-element.34), channel_id=1, source_target_pairs={{4,0},{8,4},{12,8},{16,12},{20,16},{24,20},{28,24},{5,1},{9,5},{13... | collective-permute-start | bytes 1572872 | tf_op jit(solution)/shard_map/ppermute | solution.py:30
  20.6 2.2 %copy-done = bf16[256,32,2,128]{3,2,1,0:T(2,128)(2,1)S(1)} copy-done((bf16[256,32,2,128]{3,2,1,0:T(2,128)(2,1)S(1)}, bf16[256,32,2,128]{3,2,1,0:T(2,128)(2,1)}, u32[]{:S(2)}) %copy-start) | copy-done | bytes 4194328
  22.7 5.7 %relayout.1.rows_ref.refs_2_ = bf16[32,256,256]{2,1,0:T(8,128)(2,1)S(1)} custom-call(bf16[16384,128]{1,0:T(8,128)(2,1)S(1)} %bitcast.25), custom_call_target="tpu_custom_call" | custom-call | bytes 8388608 | tf_op jit(solution)/shard_map/relayout/pallas_call | solution.py:65
  29.1 0.9 %collective-permute-done.3.refs_1_ = bf16[4,256,128]{2,1,0:T(8,128)(2,1)S(1)} collective-permute-done((bf16[4,256,128]{2,1,0:T(8,128)(2,1)S(1)}, bf16[4,256,128]{2,1,0:T(8,128)(2,1)S(1)}, u32[]{:S(2)}, u32[]{:S(2)}) %collective-permute-start.3) | collective-permute-done | bytes 262176 | tf_op jit(solution)/shard_map/ppermute | solution.py:34
  30.4 1.2 %weights.1 = (bf16[256,256]{1,0:T(8,128)(2,1)S(1)}, bf16[256,1024]{1,0:T(8,128)(2,1)S(1)}) custom-call(s32[5]{0:T(128)S(1)} %pad_add_fusion.1.where, f32[4,4]{1,0:T(4,128)S(1)} %copy-done.1, bf16[4,256,128]{2,1,0:T(8,128)(2,1)S(1)} %pad_maximum_fusion.refs_0_, bf16[4,256,128]{2,1,0:T(8,128)(2,1)S(1)} %collective-permute-done.3.refs_1_, ...), custom_call_target="tpu_custom_call" | custom-call | flops 268435456 | bytes 1048576 | tf_op jit(solution)/shard_map/weights/pallas_call | solution.py:109
  31.6 4.0 %collective-permute-done.9 = bf16[64,16,2,128]{3,2,1,0:T(2,128)(2,1)S(1)} collective-permute-done((bf16[64,16,2,128]{3,2,1,0:T(2,128)(2,1)S(1)}, bf16[64,16,2,128]{3,2,1,0:T(2,128)(2,1)S(1)}, u32[]{:S(2)}, u32[]{:S(2)}) %collective-permute-start.9) | collective-permute-done | bytes 524320 | tf_op jit(solution)/shard_map/ppermute | solution.py:30
  35.6 2.7 %right.2.refs_3_ = f32[256,256]{1,0:T(8,128)S(1)} custom-call(bf16[2048,128]{1,0:T(8,128)(2,1)S(1)} %bitcast.27, bf16[256,1024]{1,0:T(8,128)(2,1)S(1)} %get-tuple-element.28.refs_1_, bf16[32,256,256]{2,1,0:T(8,128)(2,1)S(1)} %relayout.1.rows_ref.refs_2_), custom_call_target="tpu_custom_call" | custom-call | flops 1073741824 | bytes 2097152 | tf_op jit(solution)/shard_map/right/pallas_call | solution.py:239
  38.4 5.6 %collective-permute-done.8 = bf16[64,16,2,128]{3,2,1,0:T(2,128)(2,1)S(1)} collective-permute-done((bf16[64,16,2,128]{3,2,1,0:T(2,128)(2,1)S(1)}, bf16[64,16,2,128]{3,2,1,0:T(2,128)(2,1)S(1)}, u32[]{:S(2)}, u32[]{:S(2)}) %collective-permute-start.8) | collective-permute-done | bytes 524320 | tf_op jit(solution)/shard_map/ppermute | solution.py:30
  43.9 2.8 %right.3 = (bf16[64,256]{1,0:T(8,128)(2,1)S(1)}, bf16[64,256]{1,0:T(8,128)(2,1)S(1)}, bf16[64,256]{1,0:T(8,128)(2,1)S(1)}, bf16[64,256]{1,0:T(8,128)(2,1)S(1)}) custom-call(bf16[2048,128]{1,0:T(8,128)(2,1)S(1)} %bitcast.26, bf16[256,1024]{1,0:T(8,128)(2,1)S(1)} %get-tuple-element.28.refs_1_, bf16[32,256,256]{2,1,0:T(8,128)(2,1)S(1)} %relayout.1.rows_ref.refs_2_, ...), custom_call_target="tpu_custom_call" | custom-call | flops 1073741824 | bytes 2097152 | tf_op jit(solution)/shard_map/right/pallas_call | solution.py:239
  47.2 1.4 %collective-permute-start.12 = (bf16[64,256]{1,0:T(8,128)(2,1)S(1)}, bf16[64,256]{1,0:T(8,128)(2,1)S(1)}, u32[]{:S(2)}, u32[]{:S(2)}) collective-permute-start(bf16[64,256]{1,0:T(8,128)(2,1)S(1)} %get-tuple-element.32), channel_id=1, source_target_pairs={{0,3},{1,2},{2,1},{3,0},{4,7},{5,6},{6,5},{7,4},{8,11},{9,10},{10,... | collective-permute-start | bytes 98312 | tf_op jit(solution)/shard_map/ppermute | solution.py:34
  48.6 3.9 %center.1 = (f32[256,256]{1,0:T(8,128)S(1)}, bf16[256,256]{1,0:T(8,128)(2,1)S(1)}) custom-call(bf16[32,256,256]{2,1,0:T(8,128)(2,1)S(1)} %relayout.1.rows_ref.refs_2_, bf16[256,256]{1,0:T(8,128)(2,1)S(1)} %get-tuple-element.25.weight_ref), custom_call_target="tpu_custom_call" | custom-call | flops 2147483648 | bytes 4194304 | tf_op jit(solution)/shard_map/center/pallas_call | solution.py:151
  52.5 1.3 %collective-permute-start.7 = (bf16[256,256]{1,0:T(8,128)(2,1)S(1)}, bf16[256,256]{1,0:T(8,128)(2,1)S(1)}, u32[]{:S(2)}, u32[]{:S(2)}) collective-permute-start(bf16[256,256]{1,0:T(8,128)(2,1)S(1)} %get-tuple-element.27), channel_id=1, source_target_pairs={{4,0},{8,4},{12,8},{16,12},{20,16},{24,20},{28,24},{5,1},{9,5},{13... | collective-permute-start | bytes 393224 | tf_op jit(solution)/shard_map/ppermute | solution.py:30
  53.8 5.2 %collective-permute-start.6 = (bf16[256,256]{1,0:T(8,128)(2,1)S(1)}, bf16[256,256]{1,0:T(8,128)(2,1)S(1)}, u32[]{:S(2)}, u32[]{:S(2)}) collective-permute-start(bf16[256,256]{1,0:T(8,128)(2,1)S(1)} %get-tuple-element.27), channel_id=1, source_target_pairs={{0,4},{4,8},{8,12},{12,16},{16,20},{20,24},{24,28},{1,5},{5,9},{9,... | collective-permute-start | bytes 393224 | tf_op jit(solution)/shard_map/ppermute | solution.py:30
  59.0 4.8 %collective-permute-start.13 = (bf16[4,64,256]{2,1,0:T(8,128)(2,1)S(1)}, bf16[4,64,256]{2,1,0:T(8,128)(2,1)S(1)}, u32[]{:S(2)}, u32[]{:S(2)}) collective-permute-start(bf16[4,64,256]{2,1,0:T(8,128)(2,1)S(1)} %pad_maximum_fusion.1), channel_id=1, source_target_pairs={{0,4},{4,8},{8,12},{12,16},{16,20},{20,24},{24,28},{1,5},{5,9},{9,... | collective-permute-start | bytes 393224 | tf_op jit(solution)/shard_map/ppermute | solution.py:30
  64.1 2.8 %collective-permute-done.13.left_ref = bf16[4,64,256]{2,1,0:T(8,128)(2,1)S(1)} collective-permute-done((bf16[4,64,256]{2,1,0:T(8,128)(2,1)S(1)}, bf16[4,64,256]{2,1,0:T(8,128)(2,1)S(1)}, u32[]{:S(2)}, u32[]{:S(2)}) %collective-permute-start.13) | collective-permute-done | bytes 131104 | tf_op jit(solution)/shard_map/ppermute | solution.py:30
  66.8 2.0 %screen.1 = f32[1,256,768]{2,1,0:T(8,128)} custom-call(s32[4]{0:T(128)S(1)} %pad_add_fusion.where, f32[256,256]{1,0:T(8,128)S(1)} %get-tuple-element.26.center_ref, bf16[256,256]{1,0:T(8,128)(2,1)S(1)} %collective-permute-done.6.below_ref, bf16[256,256]{1,0:T(8,128)(2,1)S(1)} %collective-permute-done.7.above_ref, ...), custom_call_target="tpu_custom_call" | custom-call | flops 369098752 | bytes 1048576 | tf_op jit(solution)/shard_map/screen/pallas_call | solution.py:297
  (30 shorter events, 3.2 us)
Async XLA Ops:
  1.4 8.2 %collective-permute-start.2 = (bf16[272,128]{1,0:T(8,128)(2,1)S(1)}, bf16[272,128]{1,0:T(8,128)(2,1)S(1)}, u32[]{:S(2)}, u32[]{:S(2)}) collective-permute-start(bf16[272,128]{1,0:T(8,128)(2,1)S(1)} %fusion.1), channel_id=1, source_target_pairs={{8,0},{12,4},{16,8},{20,12},{24,16},{28,20},{9,1},{13,5},{17,9},{2... | collective-permute-start | bytes 208904 | tf_op jit(solution)/shard_map/ppermute | solution.py:30
  2.7 7.0 %collective-permute-start.1 = (bf16[272,128]{1,0:T(8,128)(2,1)S(1)}, bf16[272,128]{1,0:T(8,128)(2,1)S(1)}, u32[]{:S(2)}, u32[]{:S(2)}) collective-permute-start(bf16[272,128]{1,0:T(8,128)(2,1)S(1)} %fusion.1), channel_id=1, source_target_pairs={{0,4},{4,8},{8,12},{12,16},{16,20},{20,24},{24,28},{1,5},{5,9},{9,... | collective-permute-start | bytes 208904 | tf_op jit(solution)/shard_map/ppermute | solution.py:30
  7.6 6.4 %collective-permute-start = (bf16[272,128]{1,0:T(8,128)(2,1)S(1)}, bf16[272,128]{1,0:T(8,128)(2,1)S(1)}, u32[]{:S(2)}, u32[]{:S(2)}) collective-permute-start(bf16[272,128]{1,0:T(8,128)(2,1)S(1)} %fusion.1), channel_id=1, source_target_pairs={{4,0},{8,4},{12,8},{16,12},{20,16},{24,20},{28,24},{5,1},{9,5},{13... | collective-permute-start | bytes 208904 | tf_op jit(solution)/shard_map/ppermute | solution.py:30
  14.0 14.5 %collective-permute-start.4 = (bf16[4,256,128]{2,1,0:T(8,128)(2,1)S(1)}, bf16[4,256,128]{2,1,0:T(8,128)(2,1)S(1)}, u32[]{:S(2)}, u32[]{:S(2)}) collective-permute-start(bf16[4,256,128]{2,1,0:T(8,128)(2,1)S(1)} %pad_maximum_fusion.refs_0_), channel_id=1, source_target_pairs={{0,2},{1,3},{2,0},{3,1},{4,6},{5,7},{6,4},{7,5},{8,10},{9,11},{10,... | collective-permute-start | bytes 786440 | tf_op jit(solution)/shard_map/ppermute | solution.py:34
  18.0 17.7 %collective-permute-start.9 = (bf16[64,16,2,128]{3,2,1,0:T(2,128)(2,1)S(1)}, bf16[64,16,2,128]{3,2,1,0:T(2,128)(2,1)S(1)}, u32[]{:S(2)}, u32[]{:S(2)}) collective-permute-start(bf16[64,16,2,128]{3,2,1,0:T(2,128)(2,1)S(1)} %get-tuple-element.33), channel_id=1, source_target_pairs={{4,0},{8,4},{12,8},{16,12},{20,16},{24,20},{28,24},{5,1},{9,5},{13... | collective-permute-start | bytes 1572872 | tf_op jit(solution)/shard_map/ppermute | solution.py:30
  19.3 24.7 %collective-permute-start.8 = (bf16[64,16,2,128]{3,2,1,0:T(2,128)(2,1)S(1)}, bf16[64,16,2,128]{3,2,1,0:T(2,128)(2,1)S(1)}, u32[]{:S(2)}, u32[]{:S(2)}) collective-permute-start(bf16[64,16,2,128]{3,2,1,0:T(2,128)(2,1)S(1)} %get-tuple-element.34), channel_id=1, source_target_pairs={{4,0},{8,4},{12,8},{16,12},{20,16},{24,20},{28,24},{5,1},{9,5},{13... | collective-permute-start | bytes 1572872 | tf_op jit(solution)/shard_map/ppermute | solution.py:30
  20.6 2.2 %copy-start = (bf16[256,32,2,128]{3,2,1,0:T(2,128)(2,1)S(1)}, bf16[256,32,2,128]{3,2,1,0:T(2,128)(2,1)}, u32[]{:S(2)}) copy-start(bf16[256,32,2,128]{3,2,1,0:T(2,128)(2,1)} %param.8) | copy-start | bytes 12582916
  22.7 6.3 %copy-start.2 = (s32[1,2]{1,0:T(1,128)S(1)}, s32[1,2]{1,0:T(1,128)}, u32[]{:S(2)}) copy-start(s32[1,2]{1,0:T(1,128)} %param.11) | copy-start | bytes 28
  22.7 7.7 %copy-start.1 = (f32[4,4]{1,0:T(4,128)S(1)}, f32[4,4]{1,0:T(4,128)}, u32[]{:S(2)}) copy-start(f32[4,4]{1,0:T(4,128)} %constant.41.clone.table) | copy-start | bytes 196
  28.4 1.6 %collective-permute-start.3 = (bf16[4,256,128]{2,1,0:T(8,128)(2,1)S(1)}, bf16[4,256,128]{2,1,0:T(8,128)(2,1)S(1)}, u32[]{:S(2)}, u32[]{:S(2)}) collective-permute-start(bf16[4,256,128]{2,1,0:T(8,128)(2,1)S(1)} %pad_maximum_fusion.refs_0_), channel_id=1, source_target_pairs={{0,1},{1,0},{2,3},{3,2},{4,5},{5,4},{6,7},{7,6},{8,9},{9,8},{10,11... | collective-permute-start | bytes 786440 | tf_op jit(solution)/shard_map/ppermute | solution.py:34
  28.5 1.9 %collective-permute-start.5 = (bf16[4,256,128]{2,1,0:T(8,128)(2,1)S(1)}, bf16[4,256,128]{2,1,0:T(8,128)(2,1)S(1)}, u32[]{:S(2)}, u32[]{:S(2)}) collective-permute-start(bf16[4,256,128]{2,1,0:T(8,128)(2,1)S(1)} %collective-permute-done.4.refs_2_), channel_id=1, source_target_pairs={{0,1},{1,0},{2,3},{3,2},{4,5},{5,4},{6,7},{7,6},{8,9},{9,8},{10,11... | collective-permute-start | bytes 786440 | tf_op jit(solution)/shard_map/ppermute | solution.py:34
  46.7 17.2 %copy-start.3 = (s32[1,3]{1,0:T(1,128)S(1)}, s32[1,3]{1,0:T(1,128)}, u32[]{:S(2)}) copy-start(s32[1,3]{1,0:T(1,128)} %param.12) | copy-start | bytes 40
  46.7 12.3 %collective-permute-start.10 = (bf16[64,256]{1,0:T(8,128)(2,1)S(1)}, bf16[64,256]{1,0:T(8,128)(2,1)S(1)}, u32[]{:S(2)}, u32[]{:S(2)}) collective-permute-start(bf16[64,256]{1,0:T(8,128)(2,1)S(1)} %get-tuple-element.30), channel_id=1, source_target_pairs={{0,1},{1,0},{2,3},{3,2},{4,5},{5,4},{6,7},{7,6},{8,9},{9,8},{10,11... | collective-permute-start | bytes 98312 | tf_op jit(solution)/shard_map/ppermute | solution.py:34
  46.8 12.2 %collective-permute-start.11 = (bf16[64,256]{1,0:T(8,128)(2,1)S(1)}, bf16[64,256]{1,0:T(8,128)(2,1)S(1)}, u32[]{:S(2)}, u32[]{:S(2)}) collective-permute-start(bf16[64,256]{1,0:T(8,128)(2,1)S(1)} %get-tuple-element.31), channel_id=1, source_target_pairs={{0,2},{1,3},{2,0},{3,1},{4,6},{5,7},{6,4},{7,5},{8,10},{9,11},{10,... | collective-permute-start | bytes 98312 | tf_op jit(solution)/shard_map/ppermute | solution.py:34
  47.2 11.8 %collective-permute-start.12 = (bf16[64,256]{1,0:T(8,128)(2,1)S(1)}, bf16[64,256]{1,0:T(8,128)(2,1)S(1)}, u32[]{:S(2)}, u32[]{:S(2)}) collective-permute-start(bf16[64,256]{1,0:T(8,128)(2,1)S(1)} %get-tuple-element.32), channel_id=1, source_target_pairs={{0,3},{1,2},{2,1},{3,0},{4,7},{5,6},{6,5},{7,4},{8,11},{9,10},{10,... | collective-permute-start | bytes 98312 | tf_op jit(solution)/shard_map/ppermute | solution.py:34
  52.5 11.5 %collective-permute-start.7 = (bf16[256,256]{1,0:T(8,128)(2,1)S(1)}, bf16[256,256]{1,0:T(8,128)(2,1)S(1)}, u32[]{:S(2)}, u32[]{:S(2)}) collective-permute-start(bf16[256,256]{1,0:T(8,128)(2,1)S(1)} %get-tuple-element.27), channel_id=1, source_target_pairs={{4,0},{8,4},{12,8},{16,12},{20,16},{24,20},{28,24},{5,1},{9,5},{13... | collective-permute-start | bytes 393224 | tf_op jit(solution)/shard_map/ppermute | solution.py:30
  53.8 10.3 %collective-permute-start.6 = (bf16[256,256]{1,0:T(8,128)(2,1)S(1)}, bf16[256,256]{1,0:T(8,128)(2,1)S(1)}, u32[]{:S(2)}, u32[]{:S(2)}) collective-permute-start(bf16[256,256]{1,0:T(8,128)(2,1)S(1)} %get-tuple-element.27), channel_id=1, source_target_pairs={{0,4},{4,8},{8,12},{12,16},{16,20},{20,24},{24,28},{1,5},{5,9},{9,... | collective-permute-start | bytes 393224 | tf_op jit(solution)/shard_map/ppermute | solution.py:30
  59.0 7.8 %collective-permute-start.13 = (bf16[4,64,256]{2,1,0:T(8,128)(2,1)S(1)}, bf16[4,64,256]{2,1,0:T(8,128)(2,1)S(1)}, u32[]{:S(2)}, u32[]{:S(2)}) collective-permute-start(bf16[4,64,256]{2,1,0:T(8,128)(2,1)S(1)} %pad_maximum_fusion.1), channel_id=1, source_target_pairs={{0,4},{4,8},{8,12},{12,16},{16,20},{20,24},{24,28},{1,5},{5,9},{9,... | collective-permute-start | bytes 393224 | tf_op jit(solution)/shard_map/ppermute | solution.py:30

commit v2 on v1

v2 whole, which is shorter than its diff:
```python
import functools
import math

import jax
import jax.numpy as jnp
import numpy as np
from jax import lax
from jax.experimental import pallas as pl
from jax.experimental.pallas import tpu as pltpu
from jax.sharding import PartitionSpec as P

time_points = (0.1, 0.5, 1.5, 4.0)
time_weights = (0.2, 0.6, 1.2, 2.5)
omega_points = (0.2, 0.9, 2.5, 7.0)

f32, bf16 = jnp.float32, jnp.bfloat16
VMEM_BYTES = 24 * 2**20
PREPARE_BYTES = 60 * 2**20
RELAYOUT_BYTES = 56 * 2**20
TILE = 16


def cosine_table():
    points = np.array(time_points, np.float32)
    weights = np.array(time_weights, np.float32)
    omegas = np.array(omega_points, np.float32)
    return weights[None, :] * np.cos(omegas[:, None] * points[None, :])


def shift(block, distance):
    devices = range(lax.axis_size("region"))
    route = [(i - distance, i) for i in devices if i - distance in devices]
    return lax.ppermute(block, "region", route)


def partner(block, bit):
    return lax.ppermute(block, "tm", [(i, i ^ bit) for i in range(lax.axis_size("tm"))])


def mm(a, b):
    return jnp.dot(a, b, preferred_element_type=f32)


def mm_nt(a, b):
    return lax.dot_general(a, b, (((1,), (1,)), ((), ())), preferred_element_type=f32)


def spec_all(count):
    return [pl.BlockSpec(memory_space=pltpu.VMEM)] * count


SMEM = pl.BlockSpec(memory_space=pltpu.SMEM)
HBM = pl.BlockSpec(memory_space=pltpu.HBM)


def swap_matrix(tile):
    size = tile * tile
    to = lax.broadcasted_iota(jnp.int32, (size, size), 0)
    of = lax.broadcasted_iota(jnp.int32, (size, size), 1)
    return (of == (to % tile) * tile + to // tile).astype(f32).astype(bf16)


def turn(source, lead, rows, lines, put):
    swap = swap_matrix(TILE)
    places = [(r, c) for r in range(0, rows, TILE) for c in range(0, lines, TILE)]
    for at in range(0, len(places), 2):
        pair = places[at : at + 2]
        blocks = [
            jnp.concatenate([source(lead + r + i, c) for i in range(TILE)], 0) for r, c in pair
        ]
        width = blocks[0].shape[1]
        moved = mm(swap, jnp.concatenate(blocks, 1)).astype(bf16)
        for h, (r, c) in enumerate(pair):
            for i in range(TILE):
                put(c + i, r, moved[i * TILE : (i + 1) * TILE, h * width : (h + 1) * width])


def relayout_kernel(kb, chunks, x_ref, out_ref, buffer, sems):
    rows, lines, nu = x_ref.shape
    part = rows // chunks
    copies = [
        pltpu.make_async_copy(
            x_ref.at[pl.ds(c * part, part)], buffer.at[pl.ds(c * part, part)], sems.at[c]
        )
        for c in range(chunks)
    ]
    for copy in copies:
        copy.start()
    for c in range(chunks):
        copies[c].wait()

        def put(line, row, value):
            k = line % kb
            start = c * part + row
            out_ref[line // kb, start : start + TILE, k * nu : (k + 1) * nu] = value

        turn(lambda r, l: buffer[r, l : l + TILE, :], c * part, part, lines, put)


def relayout(lined, kb, chunks):
    rows, lines, nu = lined.shape
    return pl.pallas_call(
        functools.partial(relayout_kernel, kb, chunks),
        out_shape=jax.ShapeDtypeStruct((lines // kb, rows, kb * nu), bf16),
        in_specs=[HBM],
        out_specs=pl.BlockSpec(memory_space=pltpu.VMEM),
        scratch_shapes=[
            pltpu.VMEM((rows, lines, nu), bf16),
            pltpu.SemaphoreType.DMA((chunks,)),
        ],
        compiler_params=pltpu.CompilerParams(vmem_limit_bytes=RELAYOUT_BYTES),
        cost_estimate=pl.CostEstimate(flops=0, bytes_accessed=0, transcendentals=0),
        name="relayout",
    )(lined)


def prepare_kernel(first, where, offsets_ref, x_ref, occ_ref, virt_ref, head_ref, tail_ref, green_ref, offsets, sems):
    cols = tail_ref.shape[0]
    notes = head_ref.shape[0] - cols
    blocks = occ_ref.shape[0]
    lines = x_ref.shape[1]
    rows = pl.ds(where[0] * cols, cols)
    moves = [
        (offsets_ref, offsets),
        (x_ref.at[rows, pl.ds(0, first)], head_ref.at[pl.ds(notes, cols)]),
        (x_ref.at[rows, pl.ds(first, lines - first)], tail_ref),
    ]
    for ref in (head_ref, green_ref):
        moves.append((occ_ref, ref.at[pl.ds(0, blocks)]))
        moves.append((virt_ref, ref.at[pl.ds(blocks, blocks)]))
    copies = [pltpu.make_async_copy(*move, sems.at[i]) for i, move in enumerate(moves)]
    for copy in copies:
        copy.start()
    copies[0].wait()
    shape = head_ref.shape[1:]
    line = lax.broadcasted_iota(jnp.int32, shape, 0)
    values = jnp.where(line < shape[0] // 2, offsets[0, 0], offsets[0, 1])
    head_ref[2 * blocks] = values.astype(f32).astype(bf16)
    for copy in copies[1:]:
        copy.wait()


def prepare(where, offsets, lined, occ, virt, first, n):
    rows, lines, nu = lined.shape
    blocks = occ.shape[0]
    cols = rows // n
    return pl.pallas_call(
        functools.partial(prepare_kernel, first),
        out_shape=[
            jax.ShapeDtypeStruct((2 * blocks + 1 + cols, first, nu), bf16),
            jax.ShapeDtypeStruct((cols, lines - first, nu), bf16),
            jax.ShapeDtypeStruct((2 * blocks, TILE, nu), bf16),
        ],
        in_specs=[SMEM] + [HBM] * 4,
        out_specs=spec_all(3),
        scratch_shapes=[pltpu.SMEM(offsets.shape, jnp.int32), pltpu.SemaphoreType.DMA((7,))],
        compiler_params=pltpu.CompilerParams(vmem_limit_bytes=PREPARE_BYTES),
        cost_estimate=pl.CostEstimate(flops=0, bytes_accessed=0, transcendentals=0),
        name="prepare",
    )(where, offsets, lined, occ, virt)


def weights_kernel(n, place, where, offsets, table, head_ref, *refs):
    greens, (center_ref, right_ref, terms) = refs[:n], refs[n:]
    nu = greens[0].shape[1] // 2
    me = where[0]
    note = head_ref[place].astype(f32)
    half = note.shape[0] // 2
    told = [jnp.max(note[:half]), jnp.max(note[half:])]
    own = [offsets[0, s] + 1 for s in range(2)]
    following = [told[s].astype(jnp.int32) + 2 for s in range(2)]

    def pick(green, places):
        occ = jnp.concatenate([green[p, :nu, :] for p in places], 0)
        virt = jnp.concatenate([green[p, nu:, :] for p in places], 0)
        return jnp.concatenate([occ, virt], 1), jnp.concatenate([virt, occ], 1)

    center = None
    for i in range(n):
        first, first_swapped = pick(greens[i], own)
        _, second_swapped = pick(greens[i], following)
        term = table[me, me ^ i] * mm_nt(first, first_swapped)
        center = term if center is None else center + term
        terms[i] = mm_nt(second_swapped, first)
    center_ref[...] = center.astype(bf16)
    size = center_ref.shape[0]
    for q in range(n):
        total = table[me ^ q, me] * terms[0]
        for i in range(1, n):
            total = total + table[me ^ q, me ^ i] * terms[i]
        right_ref[:, q * size : (q + 1) * size] = total.astype(bf16)


def weights(where, offsets, head, place, greens):
    n = len(greens)
    size = 2 * greens[0].shape[1] // 2
    return pl.pallas_call(
        functools.partial(weights_kernel, n, place),
        out_shape=[
            jax.ShapeDtypeStruct((size, size), bf16),
            jax.ShapeDtypeStruct((size, n * size), bf16),
        ],
        in_specs=[SMEM, SMEM, SMEM] + spec_all(n + 1),
        out_specs=spec_all(2),
        scratch_shapes=[pltpu.VMEM((n, size, size), f32)],
        compiler_params=pltpu.CompilerParams(vmem_limit_bytes=VMEM_BYTES),
        cost_estimate=pl.CostEstimate(
            flops=0, bytes_accessed=0, transcendentals=0
        ),
        name="weights",
    )(where, offsets, jnp.asarray(cosine_table()), head, *greens)


def product(rows_ref, first, count, left):
    right = jnp.concatenate([rows_ref[first + i] for i in range(count)], 1)
    return mm_nt(jnp.concatenate(left, 1), right)


def center_kernel(scale, group, rows_ref, weight_ref, out_ref, low_ref):
    mus, rows, width = rows_ref.shape
    total = None
    for first in range(0, mus, group):
        lines = rows_ref[first : first + group].reshape(group * rows, width)
        turned = mm(lines, weight_ref[...]).astype(bf16)
        left = [turned[i * rows : (i + 1) * rows] for i in range(group)]
        part = product(rows_ref, first, group, left)
        total = part if total is None else total + part
    out_ref[...] = scale * total
    low_ref[...] = (scale * total).astype(bf16)


def center_block(scale, turned_rows, weight, group):
    mus, rows, width = turned_rows.shape
    return pl.pallas_call(
        functools.partial(center_kernel, scale, group),
        out_shape=[
            jax.ShapeDtypeStruct((rows, rows), f32),
            jax.ShapeDtypeStruct((rows, rows), bf16),
        ],
        in_specs=spec_all(2),
        out_specs=spec_all(2),
        compiler_params=pltpu.CompilerParams(vmem_limit_bytes=VMEM_BYTES),
        cost_estimate=pl.CostEstimate(
            flops=0,
            bytes_accessed=0,
            transcendentals=0,
        ),
        name="center",
    )(turned_rows, weight)


def right_kernel(n, kb, lead, first, last, group, scale, *refs):
    far_ref, weight_ref, rows_ref = refs[:3]
    refs = refs[3:]
    total = None
    if first > 0:
        total, refs = refs[0][...], refs[1:]
    outs, flat = refs[:-1], refs[-1]
    mus, cols, width = flat.shape
    nu = far_ref.shape[2]

    def put(line, row, value):
        k = line % kb
        flat[line // kb, row : row + TILE, k * nu : (k + 1) * nu] = value

    turn(lambda r, l: far_ref[r, l : l + TILE, :], lead, cols, mus * kb, put)
    for mu in range(0, mus, group):
        lines = flat[mu : mu + group].reshape(group * cols, width)
        turned = mm(lines, weight_ref[...]).astype(bf16)
        left = [
            jnp.concatenate(
                [
                    turned[i * cols : (i + 1) * cols, q * width : (q + 1) * width]
                    for q in range(n)
                ],
                0,
            )
            for i in range(group)
        ]
        part = product(rows_ref, first + mu, group, left)
        total = part if total is None else total + part
    if last:
        for q in range(n):
            outs[q][...] = (scale * total[q * cols : (q + 1) * cols]).astype(bf16)
    else:
        outs[0][...] = total


def right_part(scale, far, lead, kb, weight, turned_rows, before, first, last, group):
    cols, lines, nu = far.shape
    cols -= lead
    mus = lines // kb
    _, rows, width = turned_rows.shape
    n = weight.shape[1] // width
    operands = [far, weight, turned_rows]
    if first > 0:
        operands.append(before)
    if last:
        out_shape = [jax.ShapeDtypeStruct((cols, rows), bf16)] * n
    else:
        out_shape = [jax.ShapeDtypeStruct((n * cols, rows), f32)]
    return pl.pallas_call(
        functools.partial(right_kernel, n, kb, lead, first, last, group, scale),
        out_shape=out_shape,
        in_specs=spec_all(len(operands)),
        out_specs=spec_all(len(out_shape)),
        scratch_shapes=[pltpu.VMEM((mus, cols, width), bf16)],
        compiler_params=pltpu.CompilerParams(vmem_limit_bytes=VMEM_BYTES),
        cost_estimate=pl.CostEstimate(
            flops=0,
            bytes_accessed=0,
            transcendentals=0,
        ),
        name="right",
    )(*operands)


def split(value):
    high = value.astype(bf16)
    return high, (value - high.astype(f32)).astype(bf16)


def screen_kernel(n, where, pattern, center_ref, below_ref, above_ref, left_ref, *refs):
    pieces, (out_ref, left, right_t) = refs[:n], refs[n:]
    me = where[0]
    cols = pieces[0].shape[0]
    size = center_ref.shape[0]
    for i in range(n):
        start = pl.multiple_of((me ^ i) * cols, cols)
        left[pl.ds(start, cols), :] = left_ref[i]
        right_t[pl.ds(start, cols), :] = pieces[i][...]
    masks = [pattern[0, e].astype(f32) for e in range(3)]
    lower = left[...] * masks[0].astype(bf16)
    upper = right_t[...].T * masks[2].astype(bf16)
    center = center_ref[...]
    high, low = split(center)
    out_ref[0, :, :size] = masks[0] * (
        lower.astype(f32) + mm(lower, below_ref[...]) + mm(high, lower) + mm(low, lower)
    )
    out_ref[0, :, size : 2 * size] = masks[1] * (
        center
        + mm_nt(lower, lower)
        + mm_nt(upper, upper)
        + mm(high, high)
        + mm(high, low)
        + mm(low, high)
    )
    out_ref[0, :, 2 * size :] = masks[2] * (
        upper.astype(f32) + mm(upper, above_ref[...]) + mm(high, upper) + mm(low, upper)
    )


def screen(where, pattern, center, below, above, left, pieces):
    n = len(pieces)
    size = center.shape[0]
    return pl.pallas_call(
        functools.partial(screen_kernel, n),
        out_shape=jax.ShapeDtypeStruct((1, size, 3 * size), f32),
        in_specs=[SMEM, SMEM] + spec_all(4 + n),
        out_specs=pl.BlockSpec(memory_space=pltpu.VMEM),
        scratch_shapes=[pltpu.VMEM((size, size), bf16)] * 2,
        compiler_params=pltpu.CompilerParams(vmem_limit_bytes=VMEM_BYTES),
        cost_estimate=pl.CostEstimate(
            flops=0, bytes_accessed=0, transcendentals=0
        ),
        name="screen",
    )(where, pattern, center, below, above, left, *pieces)


def local(tensor, g_occ, g_virt, offsets, pattern):
    rows, mus, kb, nu = tensor.shape
    lam = g_occ.shape[2]
    n = lax.axis_size("tm")
    assert n & (n - 1) == 0 and rows % n == 0
    me = lax.axis_index("tm")
    scale = 1.0 / math.sqrt(2.0 * mus * lam) / (3.0 * rows) ** 0.25
    cols = rows // n
    blocks = nu // TILE
    lines = mus * kb
    first = TILE
    where = me[None].astype(jnp.int32)
    lined = tensor.reshape(rows, lines, nu)
    split_rows = lambda x: x.reshape(blocks, TILE, lam)
    head, tail, green = prepare(
        where, offsets, lined, split_rows(g_occ), split_rows(g_virt), first, n
    )
    far_head, far_tail = shift(head, -1), shift(tail, -1)

    size = 2 * nu
    below, second = shift(green, 1), shift(green, -2)
    above = far_head[: 2 * blocks]
    stack = jnp.stack([x.reshape(size, lam) for x in (below, green, above, second)], 0)
    greens = {0: stack}
    bit = n // 2
    while bit:
        for i in list(greens):
            greens[i ^ bit] = partner(greens[i], bit)
        bit //= 2
    center_weight, right_weight = weights(
        where, offsets, far_head, 2 * blocks, [greens[i] for i in range(n)]
    )

    turned_rows = relayout(lined, kb, 4)
    center, center_low = center_block(scale, turned_rows, center_weight, 4)
    center_below, center_above = shift(center_low, 1), shift(center_low, -1)

    right_weight, center = lax.optimization_barrier((right_weight, center))
    lead = 2 * blocks + 1
    begun = right_part(scale, far_head, lead, kb, right_weight, turned_rows, None, 0, False, 4)
    parts = right_part(
        scale, far_tail, 0, kb, right_weight, turned_rows, begun[0], first // kb, True, 4
    )
    pieces = [parts[0]] + [partner(parts[i], i) for i in range(1, n)]
    left = shift(jnp.stack(pieces, 0), 1)
    return screen(where, pattern, center, center_below, center_above, left, pieces)


def solution(mesh):
    return jax.shard_map(
        local,
        mesh=mesh,
        in_specs=(
            P("region", None, None, None),
            P("tm", "region", None),
            P("tm", "region", None),
            P("region", None),
            P("region", None),
        ),
        out_specs=P("tm", "region", None),
        check_vma=False,
    )
```

time: 69.3 us -> 76.4 us (1.10)
  waiting for transfers between devices: 18 us -> 31.1 us
  local copies, waits for them, and re-layouts: 4.15 us -> 2.21 us
  other arithmetic: 2.43 us -> 0.9 us
  Pallas kernels: 18.2 us -> 16.8 us
  starting transfers between devices: 25.8 us -> 24.8 us
    ppermute x8 -> x7, waiting for transfers between devices: 16.7 us -> 25.5 us  [shift(): return lax.ppermute(block, 'region', route)]
    ppermute x6, waiting for transfers between devices: 1.32 us -> 5.61 us  [partner(): lax.ppermute(block, 'tm', [(i, i ^ bit) for i in range(lax.axis_size('tm'...]
    dynamic_slice x1 -> x0, local copies, waits for them, and re-layouts: 1.93 us -> none  [local(): slab = lax.dynamic_slice(tensor, start, (cols, mus // chunks, kb, nu))]
    pallas_call x5 -> x6, Pallas kernels: 16.2 us -> 14.8 us  [the longest x1 4.97 us: relayout(): pl.pallas_call(functools.partial(relayout_kernel, kb, chunks), out_shape=...]
    concatenate x3 -> x0, other arithmetic: 0.93 us -> none  [the longest x1 0.78 us: local(): parcel = jnp.concatenate([g_occ[0], g_virt[0], note], 0)]
    ppermute x6, starting transfers between devices: 4.52 us -> 3.68 us  [partner(): lax.ppermute(block, 'tm', [(i, i ^ bit) for i in range(lax.axis_size('tm'...]
    ppermute x8 -> x7, starting transfers between devices: 21.3 us -> 21.1 us  [shift(): return lax.ppermute(block, 'region', route)]
  transfers between devices with their start and end apart: 14 -> 13, of which waited for: 7 -> 5; matrix products, arithmetic and copies ran while one was open for 4% -> 1% of each run, Pallas kernels for 20% -> 13%
where the time goes in v2:
time: 76.4 us; the launch traced here: 76 us
  waiting for transfers between devices  31.1 us (41%)
  starting transfers between devices  24.8 us (32%)
  Pallas kernels  16.8 us (22%)
  local copies, waits for them, and re-layouts  2.21 us (3%)
  other arithmetic  0.9 us (1%)
    ppermute x7, waiting for transfers between devices, shift(): return lax.ppermute(block, 'region', route)  25.5 us
    ppermute x7, starting transfers between devices, shift(): return lax.ppermute(block, 'region', route)  21.1 us
    ppermute x6, waiting for transfers between devices, partner(): lax.ppermute(block, 'tm', [(i, i ^ bit) for i in range(lax.axis_size('tm'...  5.61 us
    pallas_call x1, Pallas kernels, relayout(): pl.pallas_call(functools.partial(relayout_kernel, kb, chunks), out_shape=...  4.97 us
    ppermute x6, starting transfers between devices, partner(): lax.ppermute(block, 'tm', [(i, i ^ bit) for i in range(lax.axis_size('tm'...  3.68 us
    pallas_call x2, Pallas kernels, right_part(): pl.pallas_call(functools.partial(right_kernel, n, kb, lead, first, last,...  3.63 us
    pallas_call x1, Pallas kernels, center_block(): pl.pallas_call(functools.partial(center_kernel, scale, group), out_shape=...  2.69 us
    pallas_call x1, Pallas kernels, prepare(): pl.pallas_call(functools.partial(prepare_kernel, first), out_shape=[jax.S...  2.28 us
  transfers between devices with their start and end apart: 13, of which 5 were waited for; matrix products, arithmetic and copies ran while one was open for 1% of the time, Pallas kernels for 13%

profile of v2, /device:TPU:0, one launch (start us, length us, event | category | flops | bytes accessed | tf_op | source)
XLA Modules:
  0.0 76.0 jit_solution(6169902109417249350)
XLA Ops:
  0.0 2.3 %prepare.1 = (bf16[81,16,128]{2,1,0:T(8,128)(2,1)}, bf16[64,48,128]{2,1,0:T(8,128)(2,1)}, bf16[16,16,128]{2,1,0:T(8,128)(2,1)}) custom-call(s32[1]{0:T(128)} %bitcast.where, s32[1,2]{1,0:T(1,128)} %offsets.1, bf16[256,64,128]{2,1,0:T(8,128)(2,1)} %bitcast.16, bf16[8,16,128]{2,1,0:T(8,128)(2,1)} %bitcast.22, bf16[8,16,128]{2,1,0:T(8,128)(2,1)} %bitcast.23), custom_call_target="tpu_custom_call" | custom-call | tf_op jit(solution)/shard_map/prepare/pallas_call | solution.py:147
  2.3 1.3 %collective-permute-start = (bf16[81,16,128]{2,1,0:T(8,128)(2,1)}, bf16[81,16,128]{2,1,0:T(8,128)(2,1)S(1)}, u32[]{:S(2)}, u32[]{:S(2)}) collective-permute-start(bf16[81,16,128]{2,1,0:T(8,128)(2,1)} %get-tuple-element.18), channel_id=1, source_target_pairs={{4,0},{8,4},{12,8},{16,12},{20,16},{24,20},{28,24},{5,1},{9,5},{13... | collective-permute-start | bytes 995336 | tf_op jit(solution)/shard_map/ppermute | solution.py:33
  3.6 1.3 %collective-permute-start.8 = (bf16[64,48,128]{2,1,0:T(8,128)(2,1)}, bf16[64,48,128]{2,1,0:T(8,128)(2,1)S(1)}, u32[]{:S(2)}, u32[]{:S(2)}) collective-permute-start(bf16[64,48,128]{2,1,0:T(8,128)(2,1)} %get-tuple-element.25), channel_id=1, source_target_pairs={{4,0},{8,4},{12,8},{16,12},{20,16},{24,20},{28,24},{5,1},{9,5},{13... | collective-permute-start | bytes 2359304 | tf_op jit(solution)/shard_map/ppermute | solution.py:33
  4.9 1.3 %collective-permute-start.2 = (bf16[16,16,128]{2,1,0:T(8,128)(2,1)}, bf16[16,16,128]{2,1,0:T(8,128)(2,1)S(1)}, u32[]{:S(2)}, u32[]{:S(2)}) collective-permute-start(bf16[16,16,128]{2,1,0:T(8,128)(2,1)} %get-tuple-element.19), channel_id=1, source_target_pairs={{8,0},{12,4},{16,8},{20,12},{24,16},{28,20},{9,1},{13,5},{17,9},{2... | collective-permute-start | bytes 196616 | tf_op jit(solution)/shard_map/ppermute | solution.py:33
  6.2 6.1 %collective-permute-start.1 = (bf16[16,16,128]{2,1,0:T(8,128)(2,1)}, bf16[16,16,128]{2,1,0:T(8,128)(2,1)S(1)}, u32[]{:S(2)}, u32[]{:S(2)}) collective-permute-start(bf16[16,16,128]{2,1,0:T(8,128)(2,1)} %get-tuple-element.19), channel_id=1, source_target_pairs={{0,4},{4,8},{8,12},{12,16},{16,20},{20,24},{24,28},{1,5},{5,9},{9,... | collective-permute-start | bytes 196616 | tf_op jit(solution)/shard_map/ppermute | solution.py:33
  12.3 3.7 %collective-permute-done.head_ref.refs_0_ = bf16[81,16,128]{2,1,0:T(8,128)(2,1)S(1)} collective-permute-done((bf16[81,16,128]{2,1,0:T(8,128)(2,1)}, bf16[81,16,128]{2,1,0:T(8,128)(2,1)S(1)}, u32[]{:S(2)}, u32[]{:S(2)}) %collective-permute-start) | collective-permute-done | bytes 331808 | tf_op jit(solution)/shard_map/ppermute | solution.py:33
  16.0 18.6 %collective-permute-done.2 = bf16[16,16,128]{2,1,0:T(8,128)(2,1)S(1)} collective-permute-done((bf16[16,16,128]{2,1,0:T(8,128)(2,1)}, bf16[16,16,128]{2,1,0:T(8,128)(2,1)S(1)}, u32[]{:S(2)}, u32[]{:S(2)}) %collective-permute-start.2) | collective-permute-done | bytes 65568 | tf_op jit(solution)/shard_map/ppermute | solution.py:33
  34.6 0.9 %pad_maximum_fusion.refs_0_ = bf16[4,256,128]{2,1,0:T(8,128)(2,1)S(1)} fusion(bf16[1,256,128]{2,1,0:T(8,128)(2,1)S(1)} %bitcast.20, bf16[1,256,128]{2,1,0:T(8,128)(2,1)S(1)} %bitcast.18, bf16[1,256,128]{2,1,0:T(8,128)(2,1)} %bitcast.19, bf16[1,256,128]{2,1,0:T(8,128)(2,1)S(1)} %bitcast.21), kind=kLoop, calls=%fused_computation | loop fusion | flops 393216 | bytes 524288 | tf_op jit(solution)/shard_map/stack | solution.py:392
  35.5 1.6 %collective-permute-start.4 = (bf16[4,256,128]{2,1,0:T(8,128)(2,1)S(1)}, bf16[4,256,128]{2,1,0:T(8,128)(2,1)S(1)}, u32[]{:S(2)}, u32[]{:S(2)}) collective-permute-start(bf16[4,256,128]{2,1,0:T(8,128)(2,1)S(1)} %pad_maximum_fusion.refs_0_), channel_id=1, source_target_pairs={{0,2},{1,3},{2,0},{3,1},{4,6},{5,7},{6,4},{7,5},{8,10},{9,11},{10,... | collective-permute-start | bytes 786440 | tf_op jit(solution)/shard_map/ppermute | solution.py:37
  37.1 5.6 %collective-permute-done.4.refs_2_ = bf16[4,256,128]{2,1,0:T(8,128)(2,1)S(1)} collective-permute-done((bf16[4,256,128]{2,1,0:T(8,128)(2,1)S(1)}, bf16[4,256,128]{2,1,0:T(8,128)(2,1)S(1)}, u32[]{:S(2)}, u32[]{:S(2)}) %collective-permute-start.4) | collective-permute-done | bytes 262176 | tf_op jit(solution)/shard_map/ppermute | solution.py:37
  42.7 5.0 %relayout.1.rows_ref.refs_2_ = bf16[32,256,256]{2,1,0:T(8,128)(2,1)} custom-call(bf16[256,64,128]{2,1,0:T(8,128)(2,1)} %bitcast.17), custom_call_target="tpu_custom_call" | custom-call | tf_op jit(solution)/shard_map/relayout/pallas_call | solution.py:102
  47.7 1.2 %weights.1 = (bf16[256,256]{1,0:T(8,128)(2,1)S(1)}, bf16[256,1024]{1,0:T(8,128)(2,1)S(1)}) custom-call(s32[1]{0:T(128)} %bitcast.where, s32[1,2]{1,0:T(1,128)S(1)} %copy-done.2, f32[4,4]{1,0:T(4,128)S(1)} %copy-done.1, bf16[81,16,128]{2,1,0:T(8,128)(2,1)S(1)} %collective-permute-done.head_ref.refs_0_, bf16[4,256,128]{2,1,0:T(8,128)(2,1)S(1)} %pad_maximum_fusion.refs_0_, ...), custom_call_target="tpu_custom_call" | custom-call | tf_op jit(solution)/shard_map/weights/pallas_call | solution.py:197
  49.0 2.2 %copy-done = bf16[32,256,256]{2,1,0:T(8,128)(2,1)S(1)} copy-done((bf16[32,256,256]{2,1,0:T(8,128)(2,1)S(1)}, bf16[32,256,256]{2,1,0:T(8,128)(2,1)}, u32[]{:S(2)}) %copy-start) | copy-done | bytes 4194328
  51.2 2.7 %center.1 = (f32[256,256]{1,0:T(8,128)S(1)}, bf16[256,256]{1,0:T(8,128)(2,1)S(1)}) custom-call(bf16[32,256,256]{2,1,0:T(8,128)(2,1)S(1)} %copy-done, bf16[256,256]{1,0:T(8,128)(2,1)S(1)} %get-tuple-element.21.weight_ref), custom_call_target="tpu_custom_call" | custom-call | tf_op jit(solution)/shard_map/center/pallas_call | solution.py:234
  53.8 1.4 %right.2.refs_3_ = f32[256,256]{1,0:T(8,128)S(1)} custom-call(bf16[81,16,128]{2,1,0:T(8,128)(2,1)S(1)} %collective-permute-done.head_ref.refs_0_, bf16[256,1024]{1,0:T(8,128)(2,1)S(1)} %get-tuple-element.26.refs_1_, bf16[32,256,256]{2,1,0:T(8,128)(2,1)S(1)} %copy-done), custom_call_target="tpu_custom_call" | custom-call | tf_op jit(solution)/shard_map/right/pallas_call | solution.py:302
  55.2 2.3 %right.3 = (bf16[64,256]{1,0:T(8,128)(2,1)S(1)}, bf16[64,256]{1,0:T(8,128)(2,1)S(1)}, bf16[64,256]{1,0:T(8,128)(2,1)S(1)}, bf16[64,256]{1,0:T(8,128)(2,1)S(1)}) custom-call(bf16[64,48,128]{2,1,0:T(8,128)(2,1)S(1)} %collective-permute-done.8.refs_0_, bf16[256,1024]{1,0:T(8,128)(2,1)S(1)} %get-tuple-element.26.refs_1_, bf16[32,256,256]{2,1,0:T(8,128)(2,1)S(1)} %copy-done, ...), custom_call_target="tpu_custom_call" | custom-call | tf_op jit(solution)/shard_map/right/pallas_call | solution.py:302
  57.5 0.6 collective-permute-start.9
  58.1 1.5 %collective-permute-start.10 = (bf16[64,256]{1,0:T(8,128)(2,1)S(1)}, bf16[64,256]{1,0:T(8,128)(2,1)S(1)}, u32[]{:S(2)}, u32[]{:S(2)}) collective-permute-start(bf16[64,256]{1,0:T(8,128)(2,1)S(1)} %get-tuple-element.29), channel_id=1, source_target_pairs={{0,2},{1,3},{2,0},{3,1},{4,6},{5,7},{6,4},{7,5},{8,10},{9,11},{10,... | collective-permute-start | bytes 98312 | tf_op jit(solution)/shard_map/ppermute | solution.py:37
  59.6 1.3 %collective-permute-start.7 = (bf16[256,256]{1,0:T(8,128)(2,1)S(1)}, bf16[256,256]{1,0:T(8,128)(2,1)S(1)}, u32[]{:S(2)}, u32[]{:S(2)}) collective-permute-start(bf16[256,256]{1,0:T(8,128)(2,1)S(1)} %get-tuple-element.24), channel_id=1, source_target_pairs={{4,0},{8,4},{12,8},{16,12},{20,16},{24,20},{28,24},{5,1},{9,5},{13... | collective-permute-start | bytes 393224 | tf_op jit(solution)/shard_map/ppermute | solution.py:33
  60.9 5.1 %collective-permute-start.6 = (bf16[256,256]{1,0:T(8,128)(2,1)S(1)}, bf16[256,256]{1,0:T(8,128)(2,1)S(1)}, u32[]{:S(2)}, u32[]{:S(2)}) collective-permute-start(bf16[256,256]{1,0:T(8,128)(2,1)S(1)} %get-tuple-element.24), channel_id=1, source_target_pairs={{0,4},{4,8},{8,12},{12,16},{16,20},{20,24},{24,28},{1,5},{5,9},{9,... | collective-permute-start | bytes 393224 | tf_op jit(solution)/shard_map/ppermute | solution.py:33
  66.0 4.8 %collective-permute-start.12 = (bf16[4,64,256]{2,1,0:T(8,128)(2,1)S(1)}, bf16[4,64,256]{2,1,0:T(8,128)(2,1)S(1)}, u32[]{:S(2)}, u32[]{:S(2)}) collective-permute-start(bf16[4,64,256]{2,1,0:T(8,128)(2,1)S(1)} %pad_maximum_fusion.1), channel_id=1, source_target_pairs={{0,4},{4,8},{8,12},{12,16},{16,20},{20,24},{24,28},{1,5},{5,9},{9,... | collective-permute-start | bytes 393224 | tf_op jit(solution)/shard_map/ppermute | solution.py:33
  70.9 0.4 collective-permute-done.6.below_ref
  71.3 2.8 %collective-permute-done.12.left_ref = bf16[4,64,256]{2,1,0:T(8,128)(2,1)S(1)} collective-permute-done((bf16[4,64,256]{2,1,0:T(8,128)(2,1)S(1)}, bf16[4,64,256]{2,1,0:T(8,128)(2,1)S(1)}, u32[]{:S(2)}, u32[]{:S(2)}) %collective-permute-start.12) | collective-permute-done | bytes 131104 | tf_op jit(solution)/shard_map/ppermute | solution.py:33
  74.1 2.0 %screen.1 = f32[1,256,768]{2,1,0:T(8,128)} custom-call(s32[1]{0:T(128)} %bitcast.where, s32[1,3]{1,0:T(1,128)S(1)} %copy-done.3, f32[256,256]{1,0:T(8,128)S(1)} %get-tuple-element.23.center_ref, bf16[256,256]{1,0:T(8,128)(2,1)S(1)} %collective-permute-done.6.below_ref, bf16[256,256]{1,0:T(8,128)(2,1)S(1)} %collective-permute-done.7.above_ref, ...), custom_call_target="tpu_custom_call" | custom-call | tf_op jit(solution)/shard_map/screen/pallas_call | solution.py:356
  (20 shorter events, 0.1 us)
Async XLA Ops:
  2.3 13.7 %collective-permute-start = (bf16[81,16,128]{2,1,0:T(8,128)(2,1)}, bf16[81,16,128]{2,1,0:T(8,128)(2,1)S(1)}, u32[]{:S(2)}, u32[]{:S(2)}) collective-permute-start(bf16[81,16,128]{2,1,0:T(8,128)(2,1)} %get-tuple-element.18), channel_id=1, source_target_pairs={{4,0},{8,4},{12,8},{16,12},{20,16},{24,20},{28,24},{5,1},{9,5},{13... | collective-permute-start | bytes 995336 | tf_op jit(solution)/shard_map/ppermute | solution.py:33
  3.6 51.6 %collective-permute-start.8 = (bf16[64,48,128]{2,1,0:T(8,128)(2,1)}, bf16[64,48,128]{2,1,0:T(8,128)(2,1)S(1)}, u32[]{:S(2)}, u32[]{:S(2)}) collective-permute-start(bf16[64,48,128]{2,1,0:T(8,128)(2,1)} %get-tuple-element.25), channel_id=1, source_target_pairs={{4,0},{8,4},{12,8},{16,12},{20,16},{24,20},{28,24},{5,1},{9,5},{13... | collective-permute-start | bytes 2359304 | tf_op jit(solution)/shard_map/ppermute | solution.py:33
  4.9 29.7 %collective-permute-start.2 = (bf16[16,16,128]{2,1,0:T(8,128)(2,1)}, bf16[16,16,128]{2,1,0:T(8,128)(2,1)S(1)}, u32[]{:S(2)}, u32[]{:S(2)}) collective-permute-start(bf16[16,16,128]{2,1,0:T(8,128)(2,1)} %get-tuple-element.19), channel_id=1, source_target_pairs={{8,0},{12,4},{16,8},{20,12},{24,16},{28,20},{9,1},{13,5},{17,9},{2... | collective-permute-start | bytes 196616 | tf_op jit(solution)/shard_map/ppermute | solution.py:33
  6.2 28.4 %collective-permute-start.1 = (bf16[16,16,128]{2,1,0:T(8,128)(2,1)}, bf16[16,16,128]{2,1,0:T(8,128)(2,1)S(1)}, u32[]{:S(2)}, u32[]{:S(2)}) collective-permute-start(bf16[16,16,128]{2,1,0:T(8,128)(2,1)} %get-tuple-element.19), channel_id=1, source_target_pairs={{0,4},{4,8},{8,12},{12,16},{16,20},{20,24},{24,28},{1,5},{5,9},{9,... | collective-permute-start | bytes 196616 | tf_op jit(solution)/shard_map/ppermute | solution.py:33
  35.5 12.2 %copy-start.1 = (f32[4,4]{1,0:T(4,128)S(1)}, f32[4,4]{1,0:T(4,128)}, u32[]{:S(2)}) copy-start(f32[4,4]{1,0:T(4,128)} %constant.6.clone.table) | copy-start | bytes 196
  35.5 12.2 %copy-start.2 = (s32[1,2]{1,0:T(1,128)S(1)}, s32[1,2]{1,0:T(1,128)}, u32[]{:S(2)}) copy-start(s32[1,2]{1,0:T(1,128)} %offsets.1) | copy-start | bytes 28
  35.5 7.2 %collective-permute-start.4 = (bf16[4,256,128]{2,1,0:T(8,128)(2,1)S(1)}, bf16[4,256,128]{2,1,0:T(8,128)(2,1)S(1)}, u32[]{:S(2)}, u32[]{:S(2)}) collective-permute-start(bf16[4,256,128]{2,1,0:T(8,128)(2,1)S(1)} %pad_maximum_fusion.refs_0_), channel_id=1, source_target_pairs={{0,2},{1,3},{2,0},{3,1},{4,6},{5,7},{6,4},{7,5},{8,10},{9,11},{10,... | collective-permute-start | bytes 786440 | tf_op jit(solution)/shard_map/ppermute | solution.py:37
  37.1 10.6 %collective-permute-start.3 = (bf16[4,256,128]{2,1,0:T(8,128)(2,1)S(1)}, bf16[4,256,128]{2,1,0:T(8,128)(2,1)S(1)}, u32[]{:S(2)}, u32[]{:S(2)}) collective-permute-start(bf16[4,256,128]{2,1,0:T(8,128)(2,1)S(1)} %pad_maximum_fusion.refs_0_), channel_id=1, source_target_pairs={{0,1},{1,0},{2,3},{3,2},{4,5},{5,4},{6,7},{7,6},{8,9},{9,8},{10,11... | collective-permute-start | bytes 786440 | tf_op jit(solution)/shard_map/ppermute | solution.py:37
  42.7 5.0 %collective-permute-start.5 = (bf16[4,256,128]{2,1,0:T(8,128)(2,1)S(1)}, bf16[4,256,128]{2,1,0:T(8,128)(2,1)S(1)}, u32[]{:S(2)}, u32[]{:S(2)}) collective-permute-start(bf16[4,256,128]{2,1,0:T(8,128)(2,1)S(1)} %collective-permute-done.4.refs_2_), channel_id=1, source_target_pairs={{0,1},{1,0},{2,3},{3,2},{4,5},{5,4},{6,7},{7,6},{8,9},{9,8},{10,11... | collective-permute-start | bytes 786440 | tf_op jit(solution)/shard_map/ppermute | solution.py:37
  49.0 2.2 %copy-start = (bf16[32,256,256]{2,1,0:T(8,128)(2,1)S(1)}, bf16[32,256,256]{2,1,0:T(8,128)(2,1)}, u32[]{:S(2)}) copy-start(bf16[32,256,256]{2,1,0:T(8,128)(2,1)} %relayout.1.rows_ref.refs_2_) | copy-start | bytes 12582916
  55.2 18.8 %copy-start.3 = (s32[1,3]{1,0:T(1,128)S(1)}, s32[1,3]{1,0:T(1,128)}, u32[]{:S(2)}) copy-start(s32[1,3]{1,0:T(1,128)} %pattern.1) | copy-start | bytes 40
  57.5 8.4 %collective-permute-start.9 = (bf16[64,256]{1,0:T(8,128)(2,1)S(1)}, bf16[64,256]{1,0:T(8,128)(2,1)S(1)}, u32[]{:S(2)}, u32[]{:S(2)}) collective-permute-start(bf16[64,256]{1,0:T(8,128)(2,1)S(1)} %get-tuple-element.28), channel_id=1, source_target_pairs={{0,1},{1,0},{2,3},{3,2},{4,5},{5,4},{6,7},{7,6},{8,9},{9,8},{10,11... | collective-permute-start | bytes 98312 | tf_op jit(solution)/shard_map/ppermute | solution.py:37
  58.1 7.9 %collective-permute-start.10 = (bf16[64,256]{1,0:T(8,128)(2,1)S(1)}, bf16[64,256]{1,0:T(8,128)(2,1)S(1)}, u32[]{:S(2)}, u32[]{:S(2)}) collective-permute-start(bf16[64,256]{1,0:T(8,128)(2,1)S(1)} %get-tuple-element.29), channel_id=1, source_target_pairs={{0,2},{1,3},{2,0},{3,1},{4,6},{5,7},{6,4},{7,5},{8,10},{9,11},{10,... | collective-permute-start | bytes 98312 | tf_op jit(solution)/shard_map/ppermute | solution.py:37
  59.6 6.4 %collective-permute-start.11 = (bf16[64,256]{1,0:T(8,128)(2,1)S(1)}, bf16[64,256]{1,0:T(8,128)(2,1)S(1)}, u32[]{:S(2)}, u32[]{:S(2)}) collective-permute-start(bf16[64,256]{1,0:T(8,128)(2,1)S(1)} %get-tuple-element.30), channel_id=1, source_target_pairs={{0,3},{1,2},{2,1},{3,0},{4,7},{5,6},{6,5},{7,4},{8,11},{9,10},{10,... | collective-permute-start | bytes 98312 | tf_op jit(solution)/shard_map/ppermute | solution.py:37
  59.6 11.2 %collective-permute-start.7 = (bf16[256,256]{1,0:T(8,128)(2,1)S(1)}, bf16[256,256]{1,0:T(8,128)(2,1)S(1)}, u32[]{:S(2)}, u32[]{:S(2)}) collective-permute-start(bf16[256,256]{1,0:T(8,128)(2,1)S(1)} %get-tuple-element.24), channel_id=1, source_target_pairs={{4,0},{8,4},{12,8},{16,12},{20,16},{24,20},{28,24},{5,1},{9,5},{13... | collective-permute-start | bytes 393224 | tf_op jit(solution)/shard_map/ppermute | solution.py:33
  60.9 10.4 %collective-permute-start.6 = (bf16[256,256]{1,0:T(8,128)(2,1)S(1)}, bf16[256,256]{1,0:T(8,128)(2,1)S(1)}, u32[]{:S(2)}, u32[]{:S(2)}) collective-permute-start(bf16[256,256]{1,0:T(8,128)(2,1)S(1)} %get-tuple-element.24), channel_id=1, source_target_pairs={{0,4},{4,8},{8,12},{12,16},{16,20},{20,24},{24,28},{1,5},{5,9},{9,... | collective-permute-start | bytes 393224 | tf_op jit(solution)/shard_map/ppermute | solution.py:33
  66.0 8.0 %collective-permute-start.12 = (bf16[4,64,256]{2,1,0:T(8,128)(2,1)S(1)}, bf16[4,64,256]{2,1,0:T(8,128)(2,1)S(1)}, u32[]{:S(2)}, u32[]{:S(2)}) collective-permute-start(bf16[4,64,256]{2,1,0:T(8,128)(2,1)S(1)} %pad_maximum_fusion.1), channel_id=1, source_target_pairs={{0,4},{4,8},{8,12},{12,16},{16,20},{20,24},{24,28},{1,5},{5,9},{9,... | collective-permute-start | bytes 393224 | tf_op jit(solution)/shard_map/ppermute | solution.py:33

commit v3 on v2

--- a/solution.py
+++ b/solution.py
@@ -16,8 +16,9 @@
 f32, bf16 = jnp.float32, jnp.bfloat16
 VMEM_BYTES = 24 * 2**20
 PREPARE_BYTES = 60 * 2**20
-RELAYOUT_BYTES = 56 * 2**20
+RELAYOUT_BYTES = 46 * 2**20
 TILE = 16
+COST = 3
 
 
 def cosine_table():
@@ -109,7 +110,7 @@
             pltpu.SemaphoreType.DMA((chunks,)),
         ],
         compiler_params=pltpu.CompilerParams(vmem_limit_bytes=RELAYOUT_BYTES),
-        cost_estimate=pl.CostEstimate(flops=0, bytes_accessed=0, transcendentals=0),
+        cost_estimate=pl.CostEstimate(flops=0, bytes_accessed=4 * lined.size // COST, transcendentals=0),
         name="relayout",
     )(lined)
 
@@ -155,7 +156,7 @@
         out_specs=spec_all(3),
         scratch_shapes=[pltpu.SMEM(offsets.shape, jnp.int32), pltpu.SemaphoreType.DMA((7,))],
         compiler_params=pltpu.CompilerParams(vmem_limit_bytes=PREPARE_BYTES),
-        cost_estimate=pl.CostEstimate(flops=0, bytes_accessed=0, transcendentals=0),
+        cost_estimate=pl.CostEstimate(flops=0, bytes_accessed=4 * lined.size // n // COST, transcendentals=0),
         name="prepare",
     )(where, offsets, lined, occ, virt)
 
@@ -205,7 +206,7 @@
         scratch_shapes=[pltpu.VMEM((n, size, size), f32)],
         compiler_params=pltpu.CompilerParams(vmem_limit_bytes=VMEM_BYTES),
         cost_estimate=pl.CostEstimate(
-            flops=0, bytes_accessed=0, transcendentals=0
+            flops=4 * n * size**3 // COST, bytes_accessed=n * size**2 * 4 // COST, transcendentals=0
         ),
         name="weights",
     )(where, offsets, jnp.asarray(cosine_table()), head, *greens)
@@ -241,8 +242,8 @@
         out_specs=spec_all(2),
         compiler_params=pltpu.CompilerParams(vmem_limit_bytes=VMEM_BYTES),
         cost_estimate=pl.CostEstimate(
-            flops=0,
-            bytes_accessed=0,
+            flops=2 * mus * rows * width * (width + rows) // COST,
+            bytes_accessed=2 * mus * rows * width // COST,
             transcendentals=0,
         ),
         name="center",
@@ -307,8 +308,8 @@
         scratch_shapes=[pltpu.VMEM((mus, cols, width), bf16)],
         compiler_params=pltpu.CompilerParams(vmem_limit_bytes=VMEM_BYTES),
         cost_estimate=pl.CostEstimate(
-            flops=0,
-            bytes_accessed=0,
+            flops=2 * mus * cols * n * width * (width + rows) // COST,
+            bytes_accessed=2 * mus * rows * width // COST,
             transcendentals=0,
         ),
         name="right",
@@ -320,51 +321,99 @@
     return high, (value - high.astype(f32)).astype(bf16)
 
 
-def screen_kernel(n, where, pattern, center_ref, below_ref, above_ref, left_ref, *refs):
-    pieces, (out_ref, left, right_t) = refs[:n], refs[n:]
+def upper_kernel(n, where, pattern, center_ref, above_ref, *refs):
+    pieces, (out_ref, middle_ref, right_t, block, sem) = refs[:n], refs[n:]
     me = where[0]
     cols = pieces[0].shape[0]
     size = center_ref.shape[0]
     for i in range(n):
         start = pl.multiple_of((me ^ i) * cols, cols)
-        left[pl.ds(start, cols), :] = left_ref[i]
         right_t[pl.ds(start, cols), :] = pieces[i][...]
-    masks = [pattern[0, e].astype(f32) for e in range(3)]
-    lower = left[...] * masks[0].astype(bf16)
-    upper = right_t[...].T * masks[2].astype(bf16)
+    mask = pattern[0, 2].astype(f32)
+    upper = right_t[...].T * mask.astype(bf16)
     center = center_ref[...]
     high, low = split(center)
-    out_ref[0, :, :size] = masks[0] * (
-        lower.astype(f32) + mm(lower, below_ref[...]) + mm(high, lower) + mm(low, lower)
-    )
-    out_ref[0, :, size : 2 * size] = masks[1] * (
-        center
-        + mm_nt(lower, lower)
-        + mm_nt(upper, upper)
-        + mm(high, high)
-        + mm(high, low)
-        + mm(low, high)
-    )
-    out_ref[0, :, 2 * size :] = masks[2] * (
+    block[...] = mask * (
         upper.astype(f32) + mm(upper, above_ref[...]) + mm(high, upper) + mm(low, upper)
     )
-
-
-def screen(where, pattern, center, below, above, left, pieces):
+    copy = pltpu.make_async_copy(block, out_ref.at[0, :, pl.ds(2 * size, size)], sem)
+    copy.start()
+    middle_ref[...] = (
+        center + mm_nt(upper, upper) + mm(high, high) + mm(high, low) + mm(low, high)
+    )
+    copy.wait()
+
+
+def upper_blocks(where, pattern, center, above, pieces):
     n = len(pieces)
     size = center.shape[0]
     return pl.pallas_call(
-        functools.partial(screen_kernel, n),
-        out_shape=jax.ShapeDtypeStruct((1, size, 3 * size), f32),
-        in_specs=[SMEM, SMEM] + spec_all(4 + n),
-        out_specs=pl.BlockSpec(memory_space=pltpu.VMEM),
-        scratch_shapes=[pltpu.VMEM((size, size), bf16)] * 2,
+        functools.partial(upper_kernel, n),
+        out_shape=[
+            jax.ShapeDtypeStruct((1, size, 3 * size), f32),
+            jax.ShapeDtypeStruct((size, size), f32),
+        ],
+        in_specs=[SMEM, SMEM] + spec_all(2 + n),
+        out_specs=[HBM] + spec_all(1),
+        scratch_shapes=[
+            pltpu.VMEM((size, size), bf16),
+            pltpu.VMEM((size, size), f32),
+            pltpu.SemaphoreType.DMA,
+        ],
         compiler_params=pltpu.CompilerParams(vmem_limit_bytes=VMEM_BYTES),
         cost_estimate=pl.CostEstimate(
-            flops=0, bytes_accessed=0, transcendentals=0
-        ),
-        name="screen",
-    )(where, pattern, center, below, above, left, *pieces)
+            flops=16 * size**3 // COST, bytes_accessed=12 * size**2 // COST, transcendentals=0
+        ),
+        name="upper",
+    )(where, pattern, center, above, *pieces)
+
+
+def lower_kernel(n, where, pattern, center_ref, middle_ref, below_ref, left_ref, _, out_ref, left, blocks, sems):
+    me = where[0]
+    cols = left_ref.shape[1]
+    size = center_ref.shape[0]
+    for i in range(n):
+        start = pl.multiple_of((me ^ i) * cols, cols)
+        left[pl.ds(start, cols), :] = left_ref[i]
+    masks = [pattern[0, e].astype(f32) for e in range(2)]
+    lower = left[...] * masks[0].astype(bf16)
+    high, low = split(center_ref[...])
+    copies = [
+        pltpu.make_async_copy(
+            blocks.at[e], out_ref.at[0, :, pl.ds(e * size, size)], sems.at[e]
+        )
+        for e in range(2)
+    ]
+    blocks[0] = masks[0] * (
+        lower.astype(f32) + mm(lower, below_ref[...]) + mm(high, lower) + mm(low, lower)
+    )
+    copies[0].start()
+    blocks[1] = masks[1] * (middle_ref[...] + mm_nt(lower, lower))
+    copies[1].start()
+    for copy in copies:
+        copy.wait()
+
+
+def lower_blocks(where, pattern, center, middle, below, left, out):
+    n = left.shape[0]
+    size = center.shape[0]
+    return pl.pallas_call(
+        functools.partial(lower_kernel, n),
+        out_shape=jax.ShapeDtypeStruct((1, size, 3 * size), f32),
+        in_specs=[SMEM, SMEM] + spec_all(4) + [HBM],
+        out_specs=HBM,
+        input_output_aliases={6: 0},
+        scratch_shapes=[
+            pltpu.VMEM((size, size), bf16),
+            pltpu.VMEM((2, size, size), f32),
+            pltpu.SemaphoreType.DMA((2,)),
+        ],
+        compiler_params=pltpu.CompilerParams(vmem_limit_bytes=VMEM_BYTES),
+        cost_estimate=pl.CostEstimate(
+            flops=10 * size**3 // COST, bytes_accessed=12 * size**2 // COST, transcendentals=0
+        ),
+        name="lower",
+    )(where, pattern, center, middle, below, left, out)
 
 
 def local(tensor, g_occ, g_virt, offsets, pattern):
@@ -390,6 +439,8 @@
     below, second = shift(green, 1), shift(green, -2)
     above = far_head[: 2 * blocks]
     stack = jnp.stack([x.reshape(size, lam) for x in (below, green, above, second)], 0)
+    turned_rows = relayout(lined, kb, 4)
+    stack, turned_rows = lax.optimization_barrier((stack, turned_rows))
     greens = {0: stack}
     bit = n // 2
     while bit:
@@ -400,9 +451,7 @@
         where, offsets, far_head, 2 * blocks, [greens[i] for i in range(n)]
     )
 
-    turned_rows = relayout(lined, kb, 4)
     center, center_low = center_block(scale, turned_rows, center_weight, 4)
-    center_below, center_above = shift(center_low, 1), shift(center_low, -1)
 
     right_weight, center = lax.optimization_barrier((right_weight, center))
     lead = 2 * blocks + 1
@@ -411,8 +460,13 @@
         scale, far_tail, 0, kb, right_weight, turned_rows, begun[0], first // kb, True, 4
     )
     pieces = [parts[0]] + [partner(parts[i], i) for i in range(1, n)]
+    center_below, center_above = shift(center_low, 1), shift(center_low, -1)
+    *pieces, center_below, center_above = lax.optimization_barrier(
+        (*pieces, center_below, center_above)
+    )
     left = shift(jnp.stack(pieces, 0), 1)
-    return screen(where, pattern, center, center_below, center_above, left, pieces)
+    out, middle = upper_blocks(where, pattern, center, center_above, pieces)
+    return lower_blocks(where, pattern, center, middle, center_below, left, out)
 
 
 def solution(mesh):

time: 76.4 us -> 55.5 us (0.73)
  waiting for transfers between devices: 31.1 us -> 14.5 us
  local copies, waits for them, and re-layouts: 2.21 us -> 0.03 us
  other arithmetic: 0.9 us -> 0.05 us
    ppermute x7, waiting for transfers between devices: 25.5 us -> 4.49 us  [shift(): return lax.ppermute(block, 'region', route)]
    ppermute x6, waiting for transfers between devices: 5.61 us -> 10 us  [partner(): lax.ppermute(block, 'tm', [(i, i ^ bit) for i in range(lax.axis_size('tm'...]
    unnamed x8, local copies, waits for them, and re-layouts: 2.2 us -> 0.02 us
    pallas_call x1, Pallas kernels: 4.97 us -> 3.02 us  [relayout(): pl.pallas_call(functools.partial(relayout_kernel, kb, chunks), out_shape=...]
    pallas_call x1 -> x2, Pallas kernels: 1.99 us -> 3.32 us  [the longest x1 1.67 us: lower_blocks(): pl.pallas_call(functools.partial(lower_kernel, n), out_shape=jax.ShapeDty...]
    another operation x1, other arithmetic: 0.87 us -> 0.04 us  [local(): jnp.stack([x.reshape(size, lam) for x in (below, green, above, second)], 0)]
  transfers between devices with their start and end apart: 13 -> 13, of which waited for: 5 -> 7; matrix products, arithmetic and copies ran while one was open for 1% -> 0% of each run, Pallas kernels for 13% -> 22%
where the time goes in v3:
time: 55.5 us; the launch traced here: 55.2 us
  starting transfers between devices  24.2 us (44%)
  Pallas kernels  16.2 us (29%)
  waiting for transfers between devices  14.5 us (26%)
    ppermute x7, starting transfers between devices, shift(): return lax.ppermute(block, 'region', route)  20.7 us
    ppermute x6, waiting for transfers between devices, partner(): lax.ppermute(block, 'tm', [(i, i ^ bit) for i in range(lax.axis_size('tm'...  10 us
    ppermute x7, waiting for transfers between devices, shift(): return lax.ppermute(block, 'region', route)  4.49 us
    pallas_call x2, Pallas kernels, right_part(): pl.pallas_call(functools.partial(right_kernel, n, kb, lead, first, last,...  3.63 us
    ppermute x6, starting transfers between devices, partner(): lax.ppermute(block, 'tm', [(i, i ^ bit) for i in range(lax.axis_size('tm'...  3.52 us
    pallas_call x1, Pallas kernels, relayout(): pl.pallas_call(functools.partial(relayout_kernel, kb, chunks), out_shape=...  3.02 us
    pallas_call x1, Pallas kernels, center_block(): pl.pallas_call(functools.partial(center_kernel, scale, group), out_shape=...  2.69 us
    pallas_call x1, Pallas kernels, prepare(): pl.pallas_call(functools.partial(prepare_kernel, first), out_shape=[jax.S...  2.28 us
  transfers between devices with their start and end apart: 13, of which 7 were waited for; matrix products, arithmetic and copies ran while one was open for 0% of the time, Pallas kernels for 22%

profile of v3, /device:TPU:0, one launch (start us, length us, event | category | flops | bytes accessed | tf_op | source)
XLA Modules:
  0.0 55.2 jit_solution(6383756535865366885)
XLA Ops:
  0.0 2.3 %prepare.1 = (bf16[81,16,128]{2,1,0:T(8,128)(2,1)}, bf16[64,48,128]{2,1,0:T(8,128)(2,1)}, bf16[16,16,128]{2,1,0:T(8,128)(2,1)}) custom-call(s32[1]{0:T(128)} %bitcast.where, s32[1,2]{1,0:T(1,128)} %offsets.1, bf16[256,64,128]{2,1,0:T(8,128)(2,1)} %bitcast.16, bf16[8,16,128]{2,1,0:T(8,128)(2,1)} %bitcast.22, bf16[8,16,128]{2,1,0:T(8,128)(2,1)} %bitcast.23), custom_call_target="tpu_custom_call" | custom-call | bytes 699050 | tf_op jit(solution)/shard_map/prepare/pallas_call | solution.py:148
  2.3 1.3 %collective-permute-start = (bf16[81,16,128]{2,1,0:T(8,128)(2,1)}, bf16[81,16,128]{2,1,0:T(8,128)(2,1)S(1)}, u32[]{:S(2)}, u32[]{:S(2)}) collective-permute-start(bf16[81,16,128]{2,1,0:T(8,128)(2,1)} %get-tuple-element.28), channel_id=1, source_target_pairs={{4,0},{8,4},{12,8},{16,12},{20,16},{24,20},{28,24},{5,1},{9,5},{13... | collective-permute-start | bytes 995336 | tf_op jit(solution)/shard_map/ppermute | solution.py:34
  3.6 1.3 %collective-permute-start.2 = (bf16[16,16,128]{2,1,0:T(8,128)(2,1)}, bf16[16,16,128]{2,1,0:T(8,128)(2,1)S(1)}, u32[]{:S(2)}, u32[]{:S(2)}) collective-permute-start(bf16[16,16,128]{2,1,0:T(8,128)(2,1)} %get-tuple-element.29), channel_id=1, source_target_pairs={{8,0},{12,4},{16,8},{20,12},{24,16},{28,20},{9,1},{13,5},{17,9},{2... | collective-permute-start | bytes 196616 | tf_op jit(solution)/shard_map/ppermute | solution.py:34
  4.9 5.5 %collective-permute-start.1 = (bf16[16,16,128]{2,1,0:T(8,128)(2,1)}, bf16[16,16,128]{2,1,0:T(8,128)(2,1)S(1)}, u32[]{:S(2)}, u32[]{:S(2)}) collective-permute-start(bf16[16,16,128]{2,1,0:T(8,128)(2,1)} %get-tuple-element.29), channel_id=1, source_target_pairs={{0,4},{4,8},{8,12},{12,16},{16,20},{20,24},{24,28},{1,5},{5,9},{9,... | collective-permute-start | bytes 196616 | tf_op jit(solution)/shard_map/ppermute | solution.py:34
  10.4 1.4 %collective-permute-start.6 = (bf16[64,48,128]{2,1,0:T(8,128)(2,1)}, bf16[64,48,128]{2,1,0:T(8,128)(2,1)S(1)}, u32[]{:S(2)}, u32[]{:S(2)}) collective-permute-start(bf16[64,48,128]{2,1,0:T(8,128)(2,1)} %get-tuple-element.36), channel_id=1, source_target_pairs={{4,0},{8,4},{12,8},{16,12},{20,16},{24,20},{28,24},{5,1},{9,5},{13... | collective-permute-start | bytes 2359304 | tf_op jit(solution)/shard_map/ppermute | solution.py:34
  11.8 3.0 %relayout.1.rows_ref.refs_2_ = bf16[32,256,256]{2,1,0:T(8,128)(2,1)S(1)} custom-call(bf16[256,64,128]{2,1,0:T(8,128)(2,1)} %bitcast.17), custom_call_target="tpu_custom_call" | custom-call | bytes 2796202 | tf_op jit(solution)/shard_map/relayout/pallas_call | solution.py:103
  15.1 2.8 %collective-permute-done.2 = bf16[16,16,128]{2,1,0:T(8,128)(2,1)S(1)} collective-permute-done((bf16[16,16,128]{2,1,0:T(8,128)(2,1)}, bf16[16,16,128]{2,1,0:T(8,128)(2,1)S(1)}, u32[]{:S(2)}, u32[]{:S(2)}) %collective-permute-start.2) | collective-permute-done | bytes 65568 | tf_op jit(solution)/shard_map/ppermute | solution.py:34
  18.0 1.6 %collective-permute-start.4 = (bf16[4,256,128]{2,1,0:T(8,128)(2,1)S(1)}, bf16[4,256,128]{2,1,0:T(8,128)(2,1)S(1)}, u32[]{:S(2)}, u32[]{:S(2)}) collective-permute-start(bf16[4,256,128]{2,1,0:T(8,128)(2,1)S(1)} %pad_maximum_fusion.refs_0_), channel_id=1, source_target_pairs={{0,2},{1,3},{2,0},{3,1},{4,6},{5,7},{6,4},{7,5},{8,10},{9,11},{10,... | collective-permute-start | bytes 786440 | tf_op jit(solution)/shard_map/ppermute | solution.py:38
  19.6 5.4 %collective-permute-done.4.refs_2_ = bf16[4,256,128]{2,1,0:T(8,128)(2,1)S(1)} collective-permute-done((bf16[4,256,128]{2,1,0:T(8,128)(2,1)S(1)}, bf16[4,256,128]{2,1,0:T(8,128)(2,1)S(1)}, u32[]{:S(2)}, u32[]{:S(2)}) %collective-permute-start.4) | collective-permute-done | bytes 262176 | tf_op jit(solution)/shard_map/ppermute | solution.py:38
  25.0 1.5 %collective-permute-done.5.refs_3_ = bf16[4,256,128]{2,1,0:T(8,128)(2,1)S(1)} collective-permute-done((bf16[4,256,128]{2,1,0:T(8,128)(2,1)S(1)}, bf16[4,256,128]{2,1,0:T(8,128)(2,1)S(1)}, u32[]{:S(2)}, u32[]{:S(2)}) %collective-permute-start.5) | collective-permute-done | bytes 262176 | tf_op jit(solution)/shard_map/ppermute | solution.py:38
  26.5 1.2 %weights.1 = (bf16[256,256]{1,0:T(8,128)(2,1)S(1)}, bf16[256,1024]{1,0:T(8,128)(2,1)S(1)}) custom-call(s32[1]{0:T(128)} %bitcast.where, s32[1,2]{1,0:T(1,128)S(1)} %copy-done.1, f32[4,4]{1,0:T(4,128)S(1)} %copy-done, bf16[81,16,128]{2,1,0:T(8,128)(2,1)S(1)} %collective-permute-done.head_ref.refs_0_, bf16[4,256,128]{2,1,0:T(8,128)(2,1)S(1)} %pad_maximum_fusion.refs_0_, ...), custom_call_target="tpu_custom_call" | custom-call | flops 89478488 | bytes 349525 | tf_op jit(solution)/shard_map/weights/pallas_call | solution.py:198
  27.8 2.7 %center.1 = (f32[256,256]{1,0:T(8,128)S(1)}, bf16[256,256]{1,0:T(8,128)(2,1)S(1)}) custom-call(bf16[32,256,256]{2,1,0:T(8,128)(2,1)S(1)} %relayout.1.rows_ref.refs_2_, bf16[256,256]{1,0:T(8,128)(2,1)S(1)} %get-tuple-element.33.weight_ref), custom_call_target="tpu_custom_call" | custom-call | flops 715827904 | bytes 1398101 | tf_op jit(solution)/shard_map/center/pallas_call | solution.py:235
  30.5 1.3 %collective-permute-start.11 = (bf16[256,256]{1,0:T(8,128)(2,1)S(1)}, bf16[256,256]{1,0:T(8,128)(2,1)S(1)}, u32[]{:S(2)}, u32[]{:S(2)}) collective-permute-start(bf16[256,256]{1,0:T(8,128)(2,1)S(1)} %get-tuple-element.42), channel_id=1, source_target_pairs={{4,0},{8,4},{12,8},{16,12},{20,16},{24,20},{28,24},{5,1},{9,5},{13... | collective-permute-start | bytes 393224 | tf_op jit(solution)/shard_map/ppermute | solution.py:34
  31.8 5.1 %collective-permute-start.10 = (bf16[256,256]{1,0:T(8,128)(2,1)S(1)}, bf16[256,256]{1,0:T(8,128)(2,1)S(1)}, u32[]{:S(2)}, u32[]{:S(2)}) collective-permute-start(bf16[256,256]{1,0:T(8,128)(2,1)S(1)} %get-tuple-element.42), channel_id=1, source_target_pairs={{0,4},{4,8},{8,12},{12,16},{16,20},{20,24},{24,28},{1,5},{5,9},{9,... | collective-permute-start | bytes 393224 | tf_op jit(solution)/shard_map/ppermute | solution.py:34
  36.9 1.4 %right.2.refs_3_ = f32[256,256]{1,0:T(8,128)S(1)} custom-call(bf16[81,16,128]{2,1,0:T(8,128)(2,1)S(1)} %collective-permute-done.head_ref.refs_0_, bf16[256,1024]{1,0:T(8,128)(2,1)S(1)} %get-tuple-element.37.refs_1_, bf16[32,256,256]{2,1,0:T(8,128)(2,1)S(1)} %relayout.1.rows_ref.refs_2_), custom_call_target="tpu_custom_call" | custom-call | flops 178956976 | bytes 349525 | tf_op jit(solution)/shard_map/right/pallas_call | solution.py:303
  38.3 2.3 %right.3 = (bf16[64,256]{1,0:T(8,128)(2,1)S(1)}, bf16[64,256]{1,0:T(8,128)(2,1)S(1)}, bf16[64,256]{1,0:T(8,128)(2,1)S(1)}, bf16[64,256]{1,0:T(8,128)(2,1)S(1)}) custom-call(bf16[64,48,128]{2,1,0:T(8,128)(2,1)S(1)} %collective-permute-done.6.refs_0_, bf16[256,1024]{1,0:T(8,128)(2,1)S(1)} %get-tuple-element.37.refs_1_, ...), custom_call_target="tpu_custom_call" | custom-call | flops 536870912 | bytes 1048576 | tf_op jit(solution)/shard_map/right/pallas_call | solution.py:303
  40.6 1.6 %collective-permute-start.8 = (bf16[64,256]{1,0:T(8,128)(2,1)S(1)}, bf16[64,256]{1,0:T(8,128)(2,1)S(1)}, u32[]{:S(2)}, u32[]{:S(2)}) collective-permute-start(bf16[64,256]{1,0:T(8,128)(2,1)S(1)} %get-tuple-element.40), channel_id=1, source_target_pairs={{0,2},{1,3},{2,0},{3,1},{4,6},{5,7},{6,4},{7,5},{8,10},{9,11},{10,... | collective-permute-start | bytes 98312 | tf_op jit(solution)/shard_map/ppermute | solution.py:38
  42.2 0.3 collective-permute-start.9
  42.5 2.1 %collective-permute-done.8.refs_2_ = bf16[64,256]{1,0:T(8,128)(2,1)S(1)} collective-permute-done((bf16[64,256]{1,0:T(8,128)(2,1)S(1)}, bf16[64,256]{1,0:T(8,128)(2,1)S(1)}, u32[]{:S(2)}, u32[]{:S(2)}) %collective-permute-start.8) | collective-permute-done | bytes 32800 | tf_op jit(solution)/shard_map/ppermute | solution.py:38
  44.6 0.9 %collective-permute-done.9.refs_3_ = bf16[64,256]{1,0:T(8,128)(2,1)S(1)} collective-permute-done((bf16[64,256]{1,0:T(8,128)(2,1)S(1)}, bf16[64,256]{1,0:T(8,128)(2,1)S(1)}, u32[]{:S(2)}, u32[]{:S(2)}) %collective-permute-start.9) | collective-permute-done | bytes 32800 | tf_op jit(solution)/shard_map/ppermute | solution.py:38
  45.6 4.8 %collective-permute-start.12 = (bf16[4,64,256]{2,1,0:T(8,128)(2,1)S(1)}, bf16[4,64,256]{2,1,0:T(8,128)(2,1)S(1)}, u32[]{:S(2)}, u32[]{:S(2)}) collective-permute-start(bf16[4,64,256]{2,1,0:T(8,128)(2,1)S(1)} %pad_maximum_fusion.1), channel_id=1, source_target_pairs={{0,4},{4,8},{8,12},{12,16},{16,20},{20,24},{24,28},{1,5},{5,9},{9,... | collective-permute-start | bytes 393224 | tf_op jit(solution)/shard_map/ppermute | solution.py:34
  50.4 1.6 %upper.1 = (f32[1,256,768]{2,1,0:T(8,128)}, f32[256,256]{1,0:T(8,128)S(1)}) custom-call(s32[1]{0:T(128)} %bitcast.where, s32[1,3]{1,0:T(1,128)S(1)} %copy-done.2, f32[256,256]{1,0:T(8,128)S(1)} %get-tuple-element.35.center_ref, bf16[256,256]{1,0:T(8,128)(2,1)S(1)} %collective-permute-done.11.above_ref, bf16[64,256]{1,0:T(8,128)(2,1)S(1)} %get-tuple-element.44.refs_0_, ...), custom_call_target="tpu_custom_call" | custom-call | flops 89478488 | bytes 262144 | tf_op jit(solution)/shard_map/upper/pallas_call | solution.py:350
  52.1 1.4 %collective-permute-done.12.left_ref = bf16[4,64,256]{2,1,0:T(8,128)(2,1)S(1)} collective-permute-done((bf16[4,64,256]{2,1,0:T(8,128)(2,1)S(1)}, bf16[4,64,256]{2,1,0:T(8,128)(2,1)S(1)}, u32[]{:S(2)}, u32[]{:S(2)}) %collective-permute-start.12) | collective-permute-done | bytes 131104 | tf_op jit(solution)/shard_map/ppermute | solution.py:34
  53.5 1.7 %lower.1 = f32[1,256,768]{2,1,0:T(8,128)} custom-call(s32[1]{0:T(128)} %bitcast.where, s32[1,3]{1,0:T(1,128)S(1)} %copy-done.2, f32[256,256]{1,0:T(8,128)S(1)} %get-tuple-element.35.center_ref, f32[256,256]{1,0:T(8,128)S(1)} %get-tuple-element.48.middle_ref, bf16[256,256]{1,0:T(8,128)(2,1)S(1)} %collective-permute-done.10.below_ref, ...), custom_call_target="tpu_custom_call", output_to_operand_aliasing={{}: (6, {})} | custom-call | flops 55924052 | bytes 262144 | tf_op jit(solution)/shard_map/lower/pallas_call | solution.py:400
  (21 shorter events, 0.4 us)
Async XLA Ops:
  2.3 12.8 %collective-permute-start = (bf16[81,16,128]{2,1,0:T(8,128)(2,1)}, bf16[81,16,128]{2,1,0:T(8,128)(2,1)S(1)}, u32[]{:S(2)}, u32[]{:S(2)}) collective-permute-start(bf16[81,16,128]{2,1,0:T(8,128)(2,1)} %get-tuple-element.28), channel_id=1, source_target_pairs={{4,0},{8,4},{12,8},{16,12},{20,16},{24,20},{28,24},{5,1},{9,5},{13... | collective-permute-start | bytes 995336 | tf_op jit(solution)/shard_map/ppermute | solution.py:34
  3.6 14.4 %collective-permute-start.2 = (bf16[16,16,128]{2,1,0:T(8,128)(2,1)}, bf16[16,16,128]{2,1,0:T(8,128)(2,1)S(1)}, u32[]{:S(2)}, u32[]{:S(2)}) collective-permute-start(bf16[16,16,128]{2,1,0:T(8,128)(2,1)} %get-tuple-element.29), channel_id=1, source_target_pairs={{8,0},{12,4},{16,8},{20,12},{24,16},{28,20},{9,1},{13,5},{17,9},{2... | collective-permute-start | bytes 196616 | tf_op jit(solution)/shard_map/ppermute | solution.py:34
  4.9 13.1 %collective-permute-start.1 = (bf16[16,16,128]{2,1,0:T(8,128)(2,1)}, bf16[16,16,128]{2,1,0:T(8,128)(2,1)S(1)}, u32[]{:S(2)}, u32[]{:S(2)}) collective-permute-start(bf16[16,16,128]{2,1,0:T(8,128)(2,1)} %get-tuple-element.29), channel_id=1, source_target_pairs={{0,4},{4,8},{8,12},{12,16},{16,20},{20,24},{24,28},{1,5},{5,9},{9,... | collective-permute-start | bytes 196616 | tf_op jit(solution)/shard_map/ppermute | solution.py:34
  10.4 7.6 %copy-start.3 = (bf16[16,16,128]{2,1,0:T(8,128)(2,1)S(1)}, bf16[16,16,128]{2,1,0:T(8,128)(2,1)}, u32[]{:S(2)}) copy-start(bf16[16,16,128]{2,1,0:T(8,128)(2,1)} %get-tuple-element.29) | copy-start | bytes 196612
  10.4 16.1 %copy-start = (f32[4,4]{1,0:T(4,128)S(1)}, f32[4,4]{1,0:T(4,128)}, u32[]{:S(2)}) copy-start(f32[4,4]{1,0:T(4,128)} %constant.6.clone.table) | copy-start | bytes 196
  10.4 16.1 %copy-start.1 = (s32[1,2]{1,0:T(1,128)S(1)}, s32[1,2]{1,0:T(1,128)}, u32[]{:S(2)}) copy-start(s32[1,2]{1,0:T(1,128)} %offsets.1) | copy-start | bytes 28
  10.4 27.9 %collective-permute-start.6 = (bf16[64,48,128]{2,1,0:T(8,128)(2,1)}, bf16[64,48,128]{2,1,0:T(8,128)(2,1)S(1)}, u32[]{:S(2)}, u32[]{:S(2)}) collective-permute-start(bf16[64,48,128]{2,1,0:T(8,128)(2,1)} %get-tuple-element.36), channel_id=1, source_target_pairs={{4,0},{8,4},{12,8},{16,12},{20,16},{24,20},{28,24},{5,1},{9,5},{13... | collective-permute-start | bytes 2359304 | tf_op jit(solution)/shard_map/ppermute | solution.py:34
  18.0 7.0 %collective-permute-start.4 = (bf16[4,256,128]{2,1,0:T(8,128)(2,1)S(1)}, bf16[4,256,128]{2,1,0:T(8,128)(2,1)S(1)}, u32[]{:S(2)}, u32[]{:S(2)}) collective-permute-start(bf16[4,256,128]{2,1,0:T(8,128)(2,1)S(1)} %pad_maximum_fusion.refs_0_), channel_id=1, source_target_pairs={{0,2},{1,3},{2,0},{3,1},{4,6},{5,7},{6,4},{7,5},{8,10},{9,11},{10,... | collective-permute-start | bytes 786440 | tf_op jit(solution)/shard_map/ppermute | solution.py:38
  19.6 5.4 %collective-permute-start.3 = (bf16[4,256,128]{2,1,0:T(8,128)(2,1)S(1)}, bf16[4,256,128]{2,1,0:T(8,128)(2,1)S(1)}, u32[]{:S(2)}, u32[]{:S(2)}) collective-permute-start(bf16[4,256,128]{2,1,0:T(8,128)(2,1)S(1)} %pad_maximum_fusion.refs_0_), channel_id=1, source_target_pairs={{0,1},{1,0},{2,3},{3,2},{4,5},{5,4},{6,7},{7,6},{8,9},{9,8},{10,11... | collective-permute-start | bytes 786440 | tf_op jit(solution)/shard_map/ppermute | solution.py:38
  25.0 1.5 %collective-permute-start.5 = (bf16[4,256,128]{2,1,0:T(8,128)(2,1)S(1)}, bf16[4,256,128]{2,1,0:T(8,128)(2,1)S(1)}, u32[]{:S(2)}, u32[]{:S(2)}) collective-permute-start(bf16[4,256,128]{2,1,0:T(8,128)(2,1)S(1)} %collective-permute-done.4.refs_2_), channel_id=1, source_target_pairs={{0,1},{1,0},{2,3},{3,2},{4,5},{5,4},{6,7},{7,6},{8,9},{9,8},{10,11... | collective-permute-start | bytes 786440 | tf_op jit(solution)/shard_map/ppermute | solution.py:38
  30.5 15.1 %collective-permute-start.11 = (bf16[256,256]{1,0:T(8,128)(2,1)S(1)}, bf16[256,256]{1,0:T(8,128)(2,1)S(1)}, u32[]{:S(2)}, u32[]{:S(2)}) collective-permute-start(bf16[256,256]{1,0:T(8,128)(2,1)S(1)} %get-tuple-element.42), channel_id=1, source_target_pairs={{4,0},{8,4},{12,8},{16,12},{20,16},{24,20},{28,24},{5,1},{9,5},{13... | collective-permute-start | bytes 393224 | tf_op jit(solution)/shard_map/ppermute | solution.py:34
  31.8 13.8 %collective-permute-start.10 = (bf16[256,256]{1,0:T(8,128)(2,1)S(1)}, bf16[256,256]{1,0:T(8,128)(2,1)S(1)}, u32[]{:S(2)}, u32[]{:S(2)}) collective-permute-start(bf16[256,256]{1,0:T(8,128)(2,1)S(1)} %get-tuple-element.42), channel_id=1, source_target_pairs={{0,4},{4,8},{8,12},{12,16},{16,20},{20,24},{24,28},{1,5},{5,9},{9,... | collective-permute-start | bytes 393224 | tf_op jit(solution)/shard_map/ppermute | solution.py:34
  38.3 12.2 %copy-start.2 = (s32[1,3]{1,0:T(1,128)S(1)}, s32[1,3]{1,0:T(1,128)}, u32[]{:S(2)}) copy-start(s32[1,3]{1,0:T(1,128)} %pattern.3) | copy-start | bytes 40
  40.6 1.9 %collective-permute-start.7 = (bf16[64,256]{1,0:T(8,128)(2,1)S(1)}, bf16[64,256]{1,0:T(8,128)(2,1)S(1)}, u32[]{:S(2)}, u32[]{:S(2)}) collective-permute-start(bf16[64,256]{1,0:T(8,128)(2,1)S(1)} %get-tuple-element.39), channel_id=1, source_target_pairs={{0,1},{1,0},{2,3},{3,2},{4,5},{5,4},{6,7},{7,6},{8,9},{9,8},{10,11... | collective-permute-start | bytes 98312 | tf_op jit(solution)/shard_map/ppermute | solution.py:38
  40.6 4.0 %collective-permute-start.8 = (bf16[64,256]{1,0:T(8,128)(2,1)S(1)}, bf16[64,256]{1,0:T(8,128)(2,1)S(1)}, u32[]{:S(2)}, u32[]{:S(2)}) collective-permute-start(bf16[64,256]{1,0:T(8,128)(2,1)S(1)} %get-tuple-element.40), channel_id=1, source_target_pairs={{0,2},{1,3},{2,0},{3,1},{4,6},{5,7},{6,4},{7,5},{8,10},{9,11},{10,... | collective-permute-start | bytes 98312 | tf_op jit(solution)/shard_map/ppermute | solution.py:38
  42.2 3.3 %collective-permute-start.9 = (bf16[64,256]{1,0:T(8,128)(2,1)S(1)}, bf16[64,256]{1,0:T(8,128)(2,1)S(1)}, u32[]{:S(2)}, u32[]{:S(2)}) collective-permute-start(bf16[64,256]{1,0:T(8,128)(2,1)S(1)} %get-tuple-element.41), channel_id=1, source_target_pairs={{0,3},{1,2},{2,1},{3,0},{4,7},{5,6},{6,5},{7,4},{8,11},{9,10},{10,... | collective-permute-start | bytes 98312 | tf_op jit(solution)/shard_map/ppermute | solution.py:38
  45.6 7.9 %collective-permute-start.12 = (bf16[4,64,256]{2,1,0:T(8,128)(2,1)S(1)}, bf16[4,64,256]{2,1,0:T(8,128)(2,1)S(1)}, u32[]{:S(2)}, u32[]{:S(2)}) collective-permute-start(bf16[4,64,256]{2,1,0:T(8,128)(2,1)S(1)} %pad_maximum_fusion.1), channel_id=1, source_target_pairs={{0,4},{4,8},{8,12},{12,16},{16,20},{20,24},{24,28},{1,5},{5,9},{9,... | collective-permute-start | bytes 393224 | tf_op jit(solution)/shard_map/ppermute | solution.py:34

commit v4 on v3

--- a/solution.py
+++ b/solution.py
@@ -15,7 +15,7 @@
 
 f32, bf16 = jnp.float32, jnp.bfloat16
 VMEM_BYTES = 24 * 2**20
-PREPARE_BYTES = 60 * 2**20
+PREPARE_BYTES = 59 * 2**20
 RELAYOUT_BYTES = 46 * 2**20
 TILE = 16
 COST = 3
@@ -115,20 +115,31 @@
     )(lined)
 
 
-def prepare_kernel(first, where, offsets_ref, x_ref, occ_ref, virt_ref, head_ref, tail_ref, green_ref, offsets, sems):
-    cols = tail_ref.shape[0]
-    notes = head_ref.shape[0] - cols
-    blocks = occ_ref.shape[0]
-    lines = x_ref.shape[1]
-    rows = pl.ds(where[0] * cols, cols)
+def pieces_of(span, cols):
+    runs, at = [], span[0]
+    while at < span[1]:
+        group, row = divmod(at, cols)
+        count = min(cols - row, span[1] - at)
+        runs.append((group, row, count, at - span[0]))
+        at += count
+    return runs
+
+
+def prepare_kernel(spans, cols, offsets_ref, x_ref, occ_ref, virt_ref, *refs):
+    parts, (offsets, sems) = refs[: len(spans)], refs[len(spans) :]
+    blocks, tile, _ = occ_ref.shape
+    mine = lax.axis_index("tm") * cols
+    head_ref = parts[0]
     moves = [
         (offsets_ref, offsets),
-        (x_ref.at[rows, pl.ds(0, first)], head_ref.at[pl.ds(notes, cols)]),
-        (x_ref.at[rows, pl.ds(first, lines - first)], tail_ref),
+        (occ_ref, head_ref.at[pl.ds(0, blocks)]),
+        (virt_ref, head_ref.at[pl.ds(blocks, blocks)]),
     ]
-    for ref in (head_ref, green_ref):
-        moves.append((occ_ref, ref.at[pl.ds(0, blocks)]))
-        moves.append((virt_ref, ref.at[pl.ds(blocks, blocks)]))
+    for ref, span in zip(parts, spans):
+        lead = 2 * blocks + 1 if ref is head_ref else 0
+        for group, row, count, place in pieces_of(span, cols):
+            source = x_ref.at[pl.ds(mine + row, count), pl.ds(group * tile, tile)]
+            moves.append((source, ref.at[pl.ds(lead + place, count)]))
     copies = [pltpu.make_async_copy(*move, sems.at[i]) for i, move in enumerate(moves)]
     for copy in copies:
         copy.start()
@@ -141,30 +152,32 @@
         copy.wait()
 
 
-def prepare(where, offsets, lined, occ, virt, first, n):
-    rows, lines, nu = lined.shape
-    blocks = occ.shape[0]
+def prepare(offsets, lined, occ, virt, spans, n):
+    rows, _, nu = lined.shape
+    blocks, tile, _ = occ.shape
     cols = rows // n
-    return pl.pallas_call(
-        functools.partial(prepare_kernel, first),
-        out_shape=[
-            jax.ShapeDtypeStruct((2 * blocks + 1 + cols, first, nu), bf16),
-            jax.ShapeDtypeStruct((cols, lines - first, nu), bf16),
-            jax.ShapeDtypeStruct((2 * blocks, TILE, nu), bf16),
-        ],
-        in_specs=[SMEM] + [HBM] * 4,
-        out_specs=spec_all(3),
-        scratch_shapes=[pltpu.SMEM(offsets.shape, jnp.int32), pltpu.SemaphoreType.DMA((7,))],
+    tiles = [last - first for first, last in spans]
+    tiles[0] += 2 * blocks + 1
+    moves = 3 + sum(len(pieces_of(span, cols)) for span in spans)
+    return pl.pallas_call(
+        functools.partial(prepare_kernel, spans, cols),
+        out_shape=[jax.ShapeDtypeStruct((t, tile, nu), bf16) for t in tiles],
+        in_specs=[HBM] * 4,
+        out_specs=spec_all(len(spans)),
+        scratch_shapes=[
+            pltpu.SMEM(offsets.shape, jnp.int32),
+            pltpu.SemaphoreType.DMA((moves,)),
+        ],
         compiler_params=pltpu.CompilerParams(vmem_limit_bytes=PREPARE_BYTES),
-        cost_estimate=pl.CostEstimate(flops=0, bytes_accessed=4 * lined.size // n // COST, transcendentals=0),
+        cost_estimate=pl.CostEstimate(flops=0, bytes_accessed=2**20 // COST, transcendentals=0),
         name="prepare",
-    )(where, offsets, lined, occ, virt)
-
-
-def weights_kernel(n, place, where, offsets, table, head_ref, *refs):
+    )(offsets, lined, occ, virt)
+
+
+def weights_kernel(n, place, offsets, table, head_ref, *refs):
     greens, (center_ref, right_ref, terms) = refs[:n], refs[n:]
     nu = greens[0].shape[1] // 2
-    me = where[0]
+    me = lax.axis_index("tm")
     note = head_ref[place].astype(f32)
     half = note.shape[0] // 2
     told = [jnp.max(note[:half]), jnp.max(note[half:])]
@@ -192,7 +205,7 @@
         right_ref[:, q * size : (q + 1) * size] = total.astype(bf16)
 
 
-def weights(where, offsets, head, place, greens):
+def weights(offsets, head, place, greens):
     n = len(greens)
     size = 2 * greens[0].shape[1] // 2
     return pl.pallas_call(
@@ -201,7 +214,7 @@
             jax.ShapeDtypeStruct((size, size), bf16),
             jax.ShapeDtypeStruct((size, n * size), bf16),
         ],
-        in_specs=[SMEM, SMEM, SMEM] + spec_all(n + 1),
+        in_specs=[SMEM, SMEM] + spec_all(n + 1),
         out_specs=spec_all(2),
         scratch_shapes=[pltpu.VMEM((n, size, size), f32)],
         compiler_params=pltpu.CompilerParams(vmem_limit_bytes=VMEM_BYTES),
@@ -209,7 +222,7 @@
             flops=4 * n * size**3 // COST, bytes_accessed=n * size**2 * 4 // COST, transcendentals=0
         ),
         name="weights",
-    )(where, offsets, jnp.asarray(cosine_table()), head, *greens)
+    )(offsets, jnp.asarray(cosine_table()), head, *greens)
 
 
 def product(rows_ref, first, count, left):
@@ -250,21 +263,29 @@
     )(turned_rows, weight)
 
 
-def right_kernel(n, kb, lead, first, last, group, scale, *refs):
-    far_ref, weight_ref, rows_ref = refs[:3]
-    refs = refs[3:]
+def right_kernel(n, kb, spans, leads, groups, first, last, group, scale, *refs):
+    fars, refs = refs[: len(spans)], refs[len(spans) :]
+    weight_ref, rows_ref = refs[:2]
+    refs = refs[2:]
     total = None
-    if first > 0:
+    if not first:
         total, refs = refs[0][...], refs[1:]
     outs, flat = refs[:-1], refs[-1]
     mus, cols, width = flat.shape
-    nu = far_ref.shape[2]
+    nu = width // kb
+    start = groups[0] * TILE
+
+    def source(row, line):
+        at = (start + line) // TILE * cols + row
+        for far, span, lead in zip(fars, spans, leads):
+            if span[0] <= at < span[1]:
+                return far[lead + at - span[0]]
 
     def put(line, row, value):
         k = line % kb
         flat[line // kb, row : row + TILE, k * nu : (k + 1) * nu] = value
 
-    turn(lambda r, l: far_ref[r, l : l + TILE, :], lead, cols, mus * kb, put)
+    turn(source, 0, cols, mus * kb, put)
     for mu in range(0, mus, group):
         lines = flat[mu : mu + group].reshape(group * cols, width)
         turned = mm(lines, weight_ref[...]).astype(bf16)
@@ -278,7 +299,7 @@
             )
             for i in range(group)
         ]
-        part = product(rows_ref, first + mu, group, left)
+        part = product(rows_ref, start // kb + mu, group, left)
         total = part if total is None else total + part
     if last:
         for q in range(n):
@@ -287,21 +308,22 @@
         outs[0][...] = total
 
 
-def right_part(scale, far, lead, kb, weight, turned_rows, before, first, last, group):
-    cols, lines, nu = far.shape
-    cols -= lead
-    mus = lines // kb
+def right_part(scale, fars, spans, leads, kb, weight, turned_rows, before, groups, last, group):
     _, rows, width = turned_rows.shape
     n = weight.shape[1] // width
-    operands = [far, weight, turned_rows]
-    if first > 0:
+    cols = rows // n
+    mus = (groups[1] - groups[0]) * TILE // kb
+    operands = [*fars, weight, turned_rows]
+    if before is not None:
         operands.append(before)
     if last:
         out_shape = [jax.ShapeDtypeStruct((cols, rows), bf16)] * n
     else:
         out_shape = [jax.ShapeDtypeStruct((n * cols, rows), f32)]
     return pl.pallas_call(
-        functools.partial(right_kernel, n, kb, lead, first, last, group, scale),
+        functools.partial(
+            right_kernel, n, kb, spans, leads, groups, before is None, last, group, scale
+        ),
         out_shape=out_shape,
         in_specs=spec_all(len(operands)),
         out_specs=spec_all(len(out_shape)),
@@ -321,9 +343,9 @@
     return high, (value - high.astype(f32)).astype(bf16)
 
 
-def upper_kernel(n, where, pattern, center_ref, above_ref, *refs):
+def upper_kernel(n, pattern, center_ref, above_ref, *refs):
     pieces, (out_ref, middle_ref, right_t, block, sem) = refs[:n], refs[n:]
-    me = where[0]
+    me = lax.axis_index("tm")
     cols = pieces[0].shape[0]
     size = center_ref.shape[0]
     for i in range(n):
@@ -344,7 +366,7 @@
     copy.wait()
 
 
-def upper_blocks(where, pattern, center, above, pieces):
+def upper_blocks(pattern, center, above, pieces):
     n = len(pieces)
     size = center.shape[0]
     return pl.pallas_call(
@@ -353,7 +375,7 @@
             jax.ShapeDtypeStruct((1, size, 3 * size), f32),
             jax.ShapeDtypeStruct((size, size), f32),
         ],
-        in_specs=[SMEM, SMEM] + spec_all(2 + n),
+        in_specs=[SMEM] + spec_all(2 + n),
         out_specs=[HBM] + spec_all(1),
         scratch_shapes=[
             pltpu.VMEM((size, size), bf16),
@@ -365,11 +387,11 @@
             flops=16 * size**3 // COST, bytes_accessed=12 * size**2 // COST, transcendentals=0
         ),
         name="upper",
-    )(where, pattern, center, above, *pieces)
-
-
-def lower_kernel(n, where, pattern, center_ref, middle_ref, below_ref, left_ref, _, out_ref, left, blocks, sems):
-    me = where[0]
+    )(pattern, center, above, *pieces)
+
+
+def lower_kernel(n, pattern, center_ref, middle_ref, below_ref, left_ref, _, out_ref, left, blocks, sems):
+    me = lax.axis_index("tm")
     cols = left_ref.shape[1]
     size = center_ref.shape[0]
     for i in range(n):
@@ -394,15 +416,15 @@
         copy.wait()
 
 
-def lower_blocks(where, pattern, center, middle, below, left, out):
+def lower_blocks(pattern, center, middle, below, left, out):
     n = left.shape[0]
     size = center.shape[0]
     return pl.pallas_call(
         functools.partial(lower_kernel, n),
         out_shape=jax.ShapeDtypeStruct((1, size, 3 * size), f32),
-        in_specs=[SMEM, SMEM] + spec_all(4) + [HBM],
+        in_specs=[SMEM] + spec_all(4) + [HBM],
         out_specs=HBM,
-        input_output_aliases={6: 0},
+        input_output_aliases={5: 0},
         scratch_shapes=[
             pltpu.VMEM((size, size), bf16),
             pltpu.VMEM((2, size, size), f32),
@@ -413,7 +435,7 @@
             flops=10 * size**3 // COST, bytes_accessed=12 * size**2 // COST, transcendentals=0
         ),
         name="lower",
-    )(where, pattern, center, middle, below, left, out)
+    )(pattern, center, middle, below, left, out)
 
 
 def local(tensor, g_occ, g_virt, offsets, pattern):
@@ -421,52 +443,49 @@
     lam = g_occ.shape[2]
     n = lax.axis_size("tm")
     assert n & (n - 1) == 0 and rows % n == 0
-    me = lax.axis_index("tm")
     scale = 1.0 / math.sqrt(2.0 * mus * lam) / (3.0 * rows) ** 0.25
-    cols = rows // n
     blocks = nu // TILE
     lines = mus * kb
-    first = TILE
-    where = me[None].astype(jnp.int32)
+    groups, cols = lines // TILE, rows // n
+    cuts = (0, 64, groups * cols)
+    spans = tuple(zip(cuts, cuts[1:]))
     lined = tensor.reshape(rows, lines, nu)
     split_rows = lambda x: x.reshape(blocks, TILE, lam)
-    head, tail, green = prepare(
-        where, offsets, lined, split_rows(g_occ), split_rows(g_virt), first, n
-    )
+    own = jnp.concatenate([g_occ[0], g_virt[0]], 0)
+    below, second = shift(own, 1), shift(own, -2)
+    head, tail = prepare(offsets, lined, split_rows(g_occ), split_rows(g_virt), spans, n)
     far_head, far_tail = shift(head, -1), shift(tail, -1)
 
     size = 2 * nu
-    below, second = shift(green, 1), shift(green, -2)
     above = far_head[: 2 * blocks]
-    stack = jnp.stack([x.reshape(size, lam) for x in (below, green, above, second)], 0)
+    stack = jnp.stack([x.reshape(size, lam) for x in (below, own, above, second)], 0)
     turned_rows = relayout(lined, kb, 4)
-    stack, turned_rows = lax.optimization_barrier((stack, turned_rows))
     greens = {0: stack}
     bit = n // 2
     while bit:
         for i in list(greens):
+            if i:
+                greens[i], turned_rows = lax.optimization_barrier((greens[i], turned_rows))
             greens[i ^ bit] = partner(greens[i], bit)
         bit //= 2
     center_weight, right_weight = weights(
-        where, offsets, far_head, 2 * blocks, [greens[i] for i in range(n)]
+        offsets, far_head, 2 * blocks, [greens[i] for i in range(n)]
     )
 
     center, center_low = center_block(scale, turned_rows, center_weight, 4)
 
     right_weight, center = lax.optimization_barrier((right_weight, center))
     lead = 2 * blocks + 1
-    begun = right_part(scale, far_head, lead, kb, right_weight, turned_rows, None, 0, False, 4)
     parts = right_part(
-        scale, far_tail, 0, kb, right_weight, turned_rows, begun[0], first // kb, True, 4
+        scale, (far_head, far_tail), spans, (lead, 0), kb, right_weight, turned_rows,
+        None, (0, groups), True, 4,
     )
     pieces = [parts[0]] + [partner(parts[i], i) for i in range(1, n)]
     center_below, center_above = shift(center_low, 1), shift(center_low, -1)
-    *pieces, center_below, center_above = lax.optimization_barrier(
-        (*pieces, center_below, center_above)
-    )
+    *pieces, center_above = lax.optimization_barrier((*pieces, center_above))
     left = shift(jnp.stack(pieces, 0), 1)
-    out, middle = upper_blocks(where, pattern, center, center_above, pieces)
-    return lower_blocks(where, pattern, center, middle, center_below, left, out)
+    out, middle = upper_blocks(pattern, center, center_above, pieces)
+    return lower_blocks(pattern, center, middle, center_below, left, out)
 
 
 def solution(mesh):

time: 55.5 us -> 52.1 us (0.939)
  waiting for transfers between devices: 14.5 us -> 12.6 us
  starting transfers between devices: 24.2 us -> 23.1 us
    ppermute x6, waiting for transfers between devices: 10 us -> 3.61 us  [partner(): lax.ppermute(block, 'tm', [(i, i ^ bit) for i in range(lax.axis_size('tm'...]
    ppermute x7, waiting for transfers between devices: 4.49 us -> 8.99 us  [shift(): return lax.ppermute(block, 'region', route)]
    ppermute x7, starting transfers between devices: 20.7 us -> 19.5 us  [shift(): return lax.ppermute(block, 'region', route)]
    pallas_call x3 -> x2, Pallas kernels: 5.91 us -> 5.44 us  [the longest x1 3.15 us: right_part(): pl.pallas_call(functools.partial(right_kernel, n, kb, spans, leads, group...]
  transfers between devices with their start and end apart: 13 -> 13, of which waited for: 7 -> 6; matrix products, arithmetic and copies ran while one was open for 0% -> 0% of each run, Pallas kernels for 22% -> 23%
where the time goes in v4:
time: 52.1 us; the launch traced here: 51.7 us
  starting transfers between devices  23.1 us (44%)
  Pallas kernels  15.7 us (30%)
  waiting for transfers between devices  12.6 us (24%)
    ppermute x7, starting transfers between devices, shift(): return lax.ppermute(block, 'region', route)  19.5 us
    ppermute x7, waiting for transfers between devices, shift(): return lax.ppermute(block, 'region', route)  8.99 us
    ppermute x6, waiting for transfers between devices, partner(): lax.ppermute(block, 'tm', [(i, i ^ bit) for i in range(lax.axis_size('tm'...  3.61 us
    ppermute x6, starting transfers between devices, partner(): lax.ppermute(block, 'tm', [(i, i ^ bit) for i in range(lax.axis_size('tm'...  3.59 us
    pallas_call x1, Pallas kernels, right_part(): pl.pallas_call(functools.partial(right_kernel, n, kb, spans, leads, group...  3.15 us
    pallas_call x1, Pallas kernels, relayout(): pl.pallas_call(functools.partial(relayout_kernel, kb, chunks), out_shape=...  3.02 us
    pallas_call x1, Pallas kernels, center_block(): pl.pallas_call(functools.partial(center_kernel, scale, group), out_shape=...  2.7 us
    pallas_call x1, Pallas kernels, prepare(): pl.pallas_call(functools.partial(prepare_kernel, spans, cols), out_shape=...  2.29 us
  transfers between devices with their start and end apart: 13, of which 6 were waited for; matrix products, arithmetic and copies ran while one was open for 0% of the time, Pallas kernels for 23%

profile of v4, /device:TPU:0, one launch (start us, length us, event | category | flops | bytes accessed | tf_op | source)
XLA Modules:
  0.0 51.7 jit_solution(9037280539867571039)
XLA Ops:
  0.0 2.3 %prepare.1 = (bf16[81,16,128]{2,1,0:T(8,128)(2,1)}, bf16[192,16,128]{2,1,0:T(8,128)(2,1)}) custom-call(s32[1,2]{1,0:T(1,128)} %offsets.1, bf16[256,64,128]{2,1,0:T(8,128)(2,1)} %bitcast.18, bf16[8,16,128]{2,1,0:T(8,128)(2,1)} %bitcast.21, bf16[8,16,128]{2,1,0:T(8,128)(2,1)} %bitcast.23), custom_call_target="tpu_custom_call" | custom-call | bytes 349525 | tf_op jit(solution)/shard_map/prepare/pallas_call | solution.py:162
  2.3 1.3 %collective-permute-start = (bf16[81,16,128]{2,1,0:T(8,128)(2,1)}, bf16[81,16,128]{2,1,0:T(8,128)(2,1)S(1)}, u32[]{:S(2)}, u32[]{:S(2)}) collective-permute-start(bf16[81,16,128]{2,1,0:T(8,128)(2,1)} %get-tuple-element.26), channel_id=1, source_target_pairs={{4,0},{8,4},{12,8},{16,12},{20,16},{24,20},{28,24},{5,1},{9,5},{13... | collective-permute-start | bytes 995336 | tf_op jit(solution)/shard_map/ppermute | solution.py:34
  3.6 1.3 %collective-permute-start.2 = (bf16[256,128]{1,0:T(8,128)(2,1)S(1)}, bf16[256,128]{1,0:T(8,128)(2,1)S(1)}, u32[]{:S(2)}, u32[]{:S(2)}) collective-permute-start(bf16[256,128]{1,0:T(8,128)(2,1)S(1)} %get-tuple-element.48), channel_id=1, source_target_pairs={{8,0},{12,4},{16,8},{20,12},{24,16},{28,20},{9,1},{13,5},{17,9},{2... | collective-permute-start | bytes 196616 | tf_op jit(solution)/shard_map/ppermute | solution.py:34
  4.9 5.5 %collective-permute-start.1 = (bf16[256,128]{1,0:T(8,128)(2,1)S(1)}, bf16[256,128]{1,0:T(8,128)(2,1)S(1)}, u32[]{:S(2)}, u32[]{:S(2)}) collective-permute-start(bf16[256,128]{1,0:T(8,128)(2,1)S(1)} %get-tuple-element.48), channel_id=1, source_target_pairs={{0,4},{4,8},{8,12},{12,16},{16,20},{20,24},{24,28},{1,5},{5,9},{9,... | collective-permute-start | bytes 196616 | tf_op jit(solution)/shard_map/ppermute | solution.py:34
  10.4 1.3 %collective-permute-start.6 = (bf16[192,16,128]{2,1,0:T(8,128)(2,1)}, bf16[192,16,128]{2,1,0:T(8,128)(2,1)S(1)}, u32[]{:S(2)}, u32[]{:S(2)}) collective-permute-start(bf16[192,16,128]{2,1,0:T(8,128)(2,1)} %get-tuple-element.33), channel_id=1, source_target_pairs={{4,0},{8,4},{12,8},{16,12},{20,16},{24,20},{28,24},{5,1},{9,5},{13... | collective-permute-start | bytes 2359304 | tf_op jit(solution)/shard_map/ppermute | solution.py:34
  11.7 3.4 %collective-permute-done.head_ref.refs_0_ = bf16[81,16,128]{2,1,0:T(8,128)(2,1)S(1)} collective-permute-done((bf16[81,16,128]{2,1,0:T(8,128)(2,1)}, bf16[81,16,128]{2,1,0:T(8,128)(2,1)S(1)}, u32[]{:S(2)}, u32[]{:S(2)}) %collective-permute-start) | collective-permute-done | bytes 331808 | tf_op jit(solution)/shard_map/ppermute | solution.py:34
  15.2 2.9 %collective-permute-done.2 = bf16[256,128]{1,0:T(8,128)(2,1)S(1)} collective-permute-done((bf16[256,128]{1,0:T(8,128)(2,1)S(1)}, bf16[256,128]{1,0:T(8,128)(2,1)S(1)}, u32[]{:S(2)}, u32[]{:S(2)}) %collective-permute-start.2) | collective-permute-done | bytes 65568 | tf_op jit(solution)/shard_map/ppermute | solution.py:34
  18.2 1.6 %collective-permute-start.4 = (bf16[4,256,128]{2,1,0:T(8,128)(2,1)S(1)}, bf16[4,256,128]{2,1,0:T(8,128)(2,1)S(1)}, u32[]{:S(2)}, u32[]{:S(2)}) collective-permute-start(bf16[4,256,128]{2,1,0:T(8,128)(2,1)S(1)} %pad_maximum_fusion.refs_0_), channel_id=1, source_target_pairs={{0,2},{1,3},{2,0},{3,1},{4,6},{5,7},{6,4},{7,5},{8,10},{9,11},{10,... | collective-permute-start | bytes 786440 | tf_op jit(solution)/shard_map/ppermute | solution.py:38
  19.7 3.0 %relayout.1.rows_ref.refs_3_ = bf16[32,256,256]{2,1,0:T(8,128)(2,1)S(1)} custom-call(bf16[256,64,128]{2,1,0:T(8,128)(2,1)} %bitcast.19), custom_call_target="tpu_custom_call" | custom-call | bytes 2796202 | tf_op jit(solution)/shard_map/relayout/pallas_call | solution.py:103
  22.8 0.1 collective-permute-start.3
  22.9 2.1 %collective-permute-done.4.refs_2_ = bf16[4,256,128]{2,1,0:T(8,128)(2,1)S(1)} collective-permute-done((bf16[4,256,128]{2,1,0:T(8,128)(2,1)S(1)}, bf16[4,256,128]{2,1,0:T(8,128)(2,1)S(1)}, u32[]{:S(2)}, u32[]{:S(2)}) %collective-permute-start.4) | collective-permute-done | bytes 262176 | tf_op jit(solution)/shard_map/ppermute | solution.py:38
  24.9 1.5 %collective-permute-done.5.refs_3_ = bf16[4,256,128]{2,1,0:T(8,128)(2,1)S(1)} collective-permute-done((bf16[4,256,128]{2,1,0:T(8,128)(2,1)S(1)}, bf16[4,256,128]{2,1,0:T(8,128)(2,1)S(1)}, u32[]{:S(2)}, u32[]{:S(2)}) %collective-permute-start.5) | collective-permute-done | bytes 262176 | tf_op jit(solution)/shard_map/ppermute | solution.py:38
  26.5 1.2 %weights.1 = (bf16[256,256]{1,0:T(8,128)(2,1)S(1)}, bf16[256,1024]{1,0:T(8,128)(2,1)S(1)}) custom-call(s32[1,2]{1,0:T(1,128)S(1)} %copy-done, f32[4,4]{1,0:T(4,128)S(1)} %copy-done.1, bf16[81,16,128]{2,1,0:T(8,128)(2,1)S(1)} %collective-permute-done.head_ref.refs_0_, bf16[4,256,128]{2,1,0:T(8,128)(2,1)S(1)} %pad_maximum_fusion.refs_0_, ...), custom_call_target="tpu_custom_call" | custom-call | flops 89478488 | bytes 349525 | tf_op jit(solution)/shard_map/weights/pallas_call | solution.py:211
  27.7 2.7 %center.1 = (f32[256,256]{1,0:T(8,128)S(1)}, bf16[256,256]{1,0:T(8,128)(2,1)S(1)}) custom-call(bf16[32,256,256]{2,1,0:T(8,128)(2,1)S(1)} %relayout.1.rows_ref.refs_3_, bf16[256,256]{1,0:T(8,128)(2,1)S(1)} %get-tuple-element.30.weight_ref), custom_call_target="tpu_custom_call" | custom-call | flops 715827904 | bytes 1398101 | tf_op jit(solution)/shard_map/center/pallas_call | solution.py:248
  30.4 1.3 %collective-permute-start.10 = (bf16[256,256]{1,0:T(8,128)(2,1)S(1)}, bf16[256,256]{1,0:T(8,128)(2,1)S(1)}, u32[]{:S(2)}, u32[]{:S(2)}) collective-permute-start(bf16[256,256]{1,0:T(8,128)(2,1)S(1)} %get-tuple-element.39), channel_id=1, source_target_pairs={{4,0},{8,4},{12,8},{16,12},{20,16},{24,20},{28,24},{5,1},{9,5},{13... | collective-permute-start | bytes 393224 | tf_op jit(solution)/shard_map/ppermute | solution.py:34
  31.7 1.3 %collective-permute-done.6.refs_1_ = bf16[192,16,128]{2,1,0:T(8,128)(2,1)S(1)} collective-permute-done((bf16[192,16,128]{2,1,0:T(8,128)(2,1)}, bf16[192,16,128]{2,1,0:T(8,128)(2,1)S(1)}, u32[]{:S(2)}, u32[]{:S(2)}) %collective-permute-start.6) | collective-permute-done | bytes 786464 | tf_op jit(solution)/shard_map/ppermute | solution.py:34
  33.1 3.1 %right.1 = (bf16[64,256]{1,0:T(8,128)(2,1)S(1)}, bf16[64,256]{1,0:T(8,128)(2,1)S(1)}, bf16[64,256]{1,0:T(8,128)(2,1)S(1)}, bf16[64,256]{1,0:T(8,128)(2,1)S(1)}) custom-call(bf16[81,16,128]{2,1,0:T(8,128)(2,1)S(1)} %collective-permute-done.head_ref.refs_0_, bf16[192,16,128]{2,1,0:T(8,128)(2,1)S(1)} %collective-permute-done.6.refs_1_, ...), custom_call_target="tpu_custom_call" | custom-call | flops 715827904 | bytes 1398101 | tf_op jit(solution)/shard_map/right/pallas_call | solution.py:323
  36.3 1.6 %collective-permute-start.8 = (bf16[64,256]{1,0:T(8,128)(2,1)S(1)}, bf16[64,256]{1,0:T(8,128)(2,1)S(1)}, u32[]{:S(2)}, u32[]{:S(2)}) collective-permute-start(bf16[64,256]{1,0:T(8,128)(2,1)S(1)} %get-tuple-element.37), channel_id=1, source_target_pairs={{0,2},{1,3},{2,0},{3,1},{4,6},{5,7},{6,4},{7,5},{8,10},{9,11},{10,... | collective-permute-start | bytes 98312 | tf_op jit(solution)/shard_map/ppermute | solution.py:38
  37.9 0.3 collective-permute-start.9
  38.2 4.9 %collective-permute-start.11 = (bf16[256,256]{1,0:T(8,128)(2,1)S(1)}, bf16[256,256]{1,0:T(8,128)(2,1)S(1)}, u32[]{:S(2)}, u32[]{:S(2)}) collective-permute-start(bf16[256,256]{1,0:T(8,128)(2,1)S(1)} %get-tuple-element.39), channel_id=1, source_target_pairs={{0,4},{4,8},{8,12},{12,16},{16,20},{20,24},{24,28},{1,5},{5,9},{9,... | collective-permute-start | bytes 393224 | tf_op jit(solution)/shard_map/ppermute | solution.py:34
  43.2 3.9 %collective-permute-start.12 = (bf16[4,64,256]{2,1,0:T(8,128)(2,1)S(1)}, bf16[4,64,256]{2,1,0:T(8,128)(2,1)S(1)}, u32[]{:S(2)}, u32[]{:S(2)}) collective-permute-start(bf16[4,64,256]{2,1,0:T(8,128)(2,1)S(1)} %pad_maximum_fusion.1), channel_id=1, source_target_pairs={{0,4},{4,8},{8,12},{12,16},{16,20},{20,24},{24,28},{1,5},{5,9},{9,... | collective-permute-start | bytes 393224 | tf_op jit(solution)/shard_map/ppermute | solution.py:34
  47.1 1.7 %upper.1 = (f32[1,256,768]{2,1,0:T(8,128)}, f32[256,256]{1,0:T(8,128)S(1)}) custom-call(s32[1,3]{1,0:T(1,128)S(1)} %copy-done.2, f32[256,256]{1,0:T(8,128)S(1)} %get-tuple-element.32.center_ref, bf16[256,256]{1,0:T(8,128)(2,1)S(1)} %collective-permute-done.10.above_ref, bf16[64,256]{1,0:T(8,128)(2,1)S(1)} %get-tuple-element.41.refs_0_, ...), custom_call_target="tpu_custom_call" | custom-call | flops 89478488 | bytes 262144 | tf_op jit(solution)/shard_map/upper/pallas_call | solution.py:372
  48.8 1.3 %collective-permute-done.12.left_ref = bf16[4,64,256]{2,1,0:T(8,128)(2,1)S(1)} collective-permute-done((bf16[4,64,256]{2,1,0:T(8,128)(2,1)S(1)}, bf16[4,64,256]{2,1,0:T(8,128)(2,1)S(1)}, u32[]{:S(2)}, u32[]{:S(2)}) %collective-permute-start.12) | collective-permute-done | bytes 131104 | tf_op jit(solution)/shard_map/ppermute | solution.py:34
  50.0 1.7 %lower.1 = f32[1,256,768]{2,1,0:T(8,128)} custom-call(s32[1,3]{1,0:T(1,128)S(1)} %copy-done.2, f32[256,256]{1,0:T(8,128)S(1)} %get-tuple-element.32.center_ref, f32[256,256]{1,0:T(8,128)S(1)} %get-tuple-element.45.middle_ref, bf16[256,256]{1,0:T(8,128)(2,1)S(1)} %collective-permute-done.11.below_ref, ...), custom_call_target="tpu_custom_call", output_to_operand_aliasing={{}: (5, {})} | custom-call | flops 55924052 | bytes 262144 | tf_op jit(solution)/shard_map/lower/pallas_call | solution.py:422
  (23 shorter events, 0.2 us)
Async XLA Ops:
  0.0 3.6 %copy-start.3 = (bf16[1,128,128]{2,1,0:T(8,128)(2,1)S(1)}, bf16[1,128,128]{2,1,0:T(8,128)(2,1)}, u32[]{:S(2)}) copy-start(bf16[1,128,128]{2,1,0:T(8,128)(2,1)} %param.7) | copy-start | bytes 98308
  0.0 3.6 %copy-start.4 = (bf16[1,128,128]{2,1,0:T(8,128)(2,1)S(1)}, bf16[1,128,128]{2,1,0:T(8,128)(2,1)}, u32[]{:S(2)}) copy-start(bf16[1,128,128]{2,1,0:T(8,128)(2,1)} %param.8) | copy-start | bytes 98308
  2.3 12.8 %collective-permute-start = (bf16[81,16,128]{2,1,0:T(8,128)(2,1)}, bf16[81,16,128]{2,1,0:T(8,128)(2,1)S(1)}, u32[]{:S(2)}, u32[]{:S(2)}) collective-permute-start(bf16[81,16,128]{2,1,0:T(8,128)(2,1)} %get-tuple-element.26), channel_id=1, source_target_pairs={{4,0},{8,4},{12,8},{16,12},{20,16},{24,20},{28,24},{5,1},{9,5},{13... | collective-permute-start | bytes 995336 | tf_op jit(solution)/shard_map/ppermute | solution.py:34
  3.6 14.4 %collective-permute-start.2 = (bf16[256,128]{1,0:T(8,128)(2,1)S(1)}, bf16[256,128]{1,0:T(8,128)(2,1)S(1)}, u32[]{:S(2)}, u32[]{:S(2)}) collective-permute-start(bf16[256,128]{1,0:T(8,128)(2,1)S(1)} %get-tuple-element.48), channel_id=1, source_target_pairs={{8,0},{12,4},{16,8},{20,12},{24,16},{28,20},{9,1},{13,5},{17,9},{2... | collective-permute-start | bytes 196616 | tf_op jit(solution)/shard_map/ppermute | solution.py:34
  4.9 13.2 %collective-permute-start.1 = (bf16[256,128]{1,0:T(8,128)(2,1)S(1)}, bf16[256,128]{1,0:T(8,128)(2,1)S(1)}, u32[]{:S(2)}, u32[]{:S(2)}) collective-permute-start(bf16[256,128]{1,0:T(8,128)(2,1)S(1)} %get-tuple-element.48), channel_id=1, source_target_pairs={{0,4},{4,8},{8,12},{12,16},{16,20},{20,24},{24,28},{1,5},{5,9},{9,... | collective-permute-start | bytes 196616 | tf_op jit(solution)/shard_map/ppermute | solution.py:34
  10.4 22.6 %collective-permute-start.6 = (bf16[192,16,128]{2,1,0:T(8,128)(2,1)}, bf16[192,16,128]{2,1,0:T(8,128)(2,1)S(1)}, u32[]{:S(2)}, u32[]{:S(2)}) collective-permute-start(bf16[192,16,128]{2,1,0:T(8,128)(2,1)} %get-tuple-element.33), channel_id=1, source_target_pairs={{4,0},{8,4},{12,8},{16,12},{20,16},{24,20},{28,24},{5,1},{9,5},{13... | collective-permute-start | bytes 2359304 | tf_op jit(solution)/shard_map/ppermute | solution.py:34
  18.1 8.3 %copy-start = (s32[1,2]{1,0:T(1,128)S(1)}, s32[1,2]{1,0:T(1,128)}, u32[]{:S(2)}) copy-start(s32[1,2]{1,0:T(1,128)} %offsets.1) | copy-start | bytes 28
  18.2 8.3 %copy-start.1 = (f32[4,4]{1,0:T(4,128)S(1)}, f32[4,4]{1,0:T(4,128)}, u32[]{:S(2)}) copy-start(f32[4,4]{1,0:T(4,128)} %constant.2.clone.table) | copy-start | bytes 196
  18.2 6.8 %collective-permute-start.4 = (bf16[4,256,128]{2,1,0:T(8,128)(2,1)S(1)}, bf16[4,256,128]{2,1,0:T(8,128)(2,1)S(1)}, u32[]{:S(2)}, u32[]{:S(2)}) collective-permute-start(bf16[4,256,128]{2,1,0:T(8,128)(2,1)S(1)} %pad_maximum_fusion.refs_0_), channel_id=1, source_target_pairs={{0,2},{1,3},{2,0},{3,1},{4,6},{5,7},{6,4},{7,5},{8,10},{9,11},{10,... | collective-permute-start | bytes 786440 | tf_op jit(solution)/shard_map/ppermute | solution.py:38
  22.8 2.2 %collective-permute-start.3 = (bf16[4,256,128]{2,1,0:T(8,128)(2,1)S(1)}, bf16[4,256,128]{2,1,0:T(8,128)(2,1)S(1)}, u32[]{:S(2)}, u32[]{:S(2)}) collective-permute-start(bf16[4,256,128]{2,1,0:T(8,128)(2,1)S(1)} %pad_maximum_fusion.refs_0_), channel_id=1, source_target_pairs={{0,1},{1,0},{2,3},{3,2},{4,5},{5,4},{6,7},{7,6},{8,9},{9,8},{10,11... | collective-permute-start | bytes 786440 | tf_op jit(solution)/shard_map/ppermute | solution.py:38
  24.9 1.5 %collective-permute-start.5 = (bf16[4,256,128]{2,1,0:T(8,128)(2,1)S(1)}, bf16[4,256,128]{2,1,0:T(8,128)(2,1)S(1)}, u32[]{:S(2)}, u32[]{:S(2)}) collective-permute-start(bf16[4,256,128]{2,1,0:T(8,128)(2,1)S(1)} %collective-permute-done.4.refs_2_), channel_id=1, source_target_pairs={{0,1},{1,0},{2,3},{3,2},{4,5},{5,4},{6,7},{7,6},{8,9},{9,8},{10,11... | collective-permute-start | bytes 786440 | tf_op jit(solution)/shard_map/ppermute | solution.py:38
  27.7 19.4 %copy-start.2 = (s32[1,3]{1,0:T(1,128)S(1)}, s32[1,3]{1,0:T(1,128)}, u32[]{:S(2)}) copy-start(s32[1,3]{1,0:T(1,128)} %pattern.3) | copy-start | bytes 40
  30.4 12.7 %collective-permute-start.10 = (bf16[256,256]{1,0:T(8,128)(2,1)S(1)}, bf16[256,256]{1,0:T(8,128)(2,1)S(1)}, u32[]{:S(2)}, u32[]{:S(2)}) collective-permute-start(bf16[256,256]{1,0:T(8,128)(2,1)S(1)} %get-tuple-element.39), channel_id=1, source_target_pairs={{4,0},{8,4},{12,8},{16,12},{20,16},{24,20},{28,24},{5,1},{9,5},{13... | collective-permute-start | bytes 393224 | tf_op jit(solution)/shard_map/ppermute | solution.py:34
  36.2 6.9 %collective-permute-start.7 = (bf16[64,256]{1,0:T(8,128)(2,1)S(1)}, bf16[64,256]{1,0:T(8,128)(2,1)S(1)}, u32[]{:S(2)}, u32[]{:S(2)}) collective-permute-start(bf16[64,256]{1,0:T(8,128)(2,1)S(1)} %get-tuple-element.36), channel_id=1, source_target_pairs={{0,1},{1,0},{2,3},{3,2},{4,5},{5,4},{6,7},{7,6},{8,9},{9,8},{10,11... | collective-permute-start | bytes 98312 | tf_op jit(solution)/shard_map/ppermute | solution.py:38
  36.3 6.8 %collective-permute-start.8 = (bf16[64,256]{1,0:T(8,128)(2,1)S(1)}, bf16[64,256]{1,0:T(8,128)(2,1)S(1)}, u32[]{:S(2)}, u32[]{:S(2)}) collective-permute-start(bf16[64,256]{1,0:T(8,128)(2,1)S(1)} %get-tuple-element.37), channel_id=1, source_target_pairs={{0,2},{1,3},{2,0},{3,1},{4,6},{5,7},{6,4},{7,5},{8,10},{9,11},{10,... | collective-permute-start | bytes 98312 | tf_op jit(solution)/shard_map/ppermute | solution.py:38
  37.9 5.2 %collective-permute-start.9 = (bf16[64,256]{1,0:T(8,128)(2,1)S(1)}, bf16[64,256]{1,0:T(8,128)(2,1)S(1)}, u32[]{:S(2)}, u32[]{:S(2)}) collective-permute-start(bf16[64,256]{1,0:T(8,128)(2,1)S(1)} %get-tuple-element.38), channel_id=1, source_target_pairs={{0,3},{1,2},{2,1},{3,0},{4,7},{5,6},{6,5},{7,4},{8,11},{9,10},{10,... | collective-permute-start | bytes 98312 | tf_op jit(solution)/shard_map/ppermute | solution.py:38
  38.2 10.6 %collective-permute-start.11 = (bf16[256,256]{1,0:T(8,128)(2,1)S(1)}, bf16[256,256]{1,0:T(8,128)(2,1)S(1)}, u32[]{:S(2)}, u32[]{:S(2)}) collective-permute-start(bf16[256,256]{1,0:T(8,128)(2,1)S(1)} %get-tuple-element.39), channel_id=1, source_target_pairs={{0,4},{4,8},{8,12},{12,16},{16,20},{20,24},{24,28},{1,5},{5,9},{9,... | collective-permute-start | bytes 393224 | tf_op jit(solution)/shard_map/ppermute | solution.py:34
  43.2 6.9 %collective-permute-start.12 = (bf16[4,64,256]{2,1,0:T(8,128)(2,1)S(1)}, bf16[4,64,256]{2,1,0:T(8,128)(2,1)S(1)}, u32[]{:S(2)}, u32[]{:S(2)}) collective-permute-start(bf16[4,64,256]{2,1,0:T(8,128)(2,1)S(1)} %pad_maximum_fusion.1), channel_id=1, source_target_pairs={{0,4},{4,8},{8,12},{12,16},{16,20},{20,24},{24,28},{1,5},{5,9},{9,... | collective-permute-start | bytes 393224 | tf_op jit(solution)/shard_map/ppermute | solution.py:34

commit v5 on v4

--- a/solution.py
+++ b/solution.py
@@ -31,6 +31,14 @@
 def shift(block, distance):
     devices = range(lax.axis_size("region"))
     route = [(i - distance, i) for i in devices if i - distance in devices]
+    return lax.ppermute(block, "region", route)
+
+
+def swap_pairs(block, first):
+    count = lax.axis_size("region")
+    route = []
+    for i in range(first, count - 1, 2):
+        route += [(i, i + 1), (i + 1, i)]
     return lax.ppermute(block, "region", route)
 
 
@@ -126,7 +134,7 @@
 
 
 def prepare_kernel(spans, cols, offsets_ref, x_ref, occ_ref, virt_ref, *refs):
-    parts, (offsets, sems) = refs[: len(spans)], refs[len(spans) :]
+    parts, (note_ref, offsets, sems) = refs[: len(spans)], refs[len(spans) :]
     blocks, tile, _ = occ_ref.shape
     mine = lax.axis_index("tm") * cols
     head_ref = parts[0]
@@ -147,7 +155,8 @@
     shape = head_ref.shape[1:]
     line = lax.broadcasted_iota(jnp.int32, shape, 0)
     values = jnp.where(line < shape[0] // 2, offsets[0, 0], offsets[0, 1])
-    head_ref[2 * blocks] = values.astype(f32).astype(bf16)
+    note_ref[...] = values.astype(f32).astype(bf16)
+    head_ref[2 * blocks] = note_ref[...]
     for copy in copies[1:]:
         copy.wait()
 
@@ -161,9 +170,10 @@
     moves = 3 + sum(len(pieces_of(span, cols)) for span in spans)
     return pl.pallas_call(
         functools.partial(prepare_kernel, spans, cols),
-        out_shape=[jax.ShapeDtypeStruct((t, tile, nu), bf16) for t in tiles],
+        out_shape=[jax.ShapeDtypeStruct((t, tile, nu), bf16) for t in tiles]
+        + [jax.ShapeDtypeStruct((tile, nu), bf16)],
         in_specs=[HBM] * 4,
-        out_specs=spec_all(len(spans)),
+        out_specs=spec_all(len(spans) + 1),
         scratch_shapes=[
             pltpu.SMEM(offsets.shape, jnp.int32),
             pltpu.SemaphoreType.DMA((moves,)),
@@ -174,15 +184,25 @@
     )(offsets, lined, occ, virt)
 
 
-def weights_kernel(n, place, offsets, table, head_ref, *refs):
+def weights_kernel(n, place, note_ref, head_ref, *refs):
     greens, (center_ref, right_ref, terms) = refs[:n], refs[n:]
     nu = greens[0].shape[1] // 2
     me = lax.axis_index("tm")
-    note = head_ref[place].astype(f32)
-    half = note.shape[0] // 2
-    told = [jnp.max(note[:half]), jnp.max(note[half:])]
-    own = [offsets[0, s] + 1 for s in range(2)]
-    following = [told[s].astype(jnp.int32) + 2 for s in range(2)]
+    table = cosine_table()
+
+    def weight(frequency, time):
+        value = jnp.float32(table[frequency, time])
+        for m in range(1, n):
+            value = jnp.where(me == m, jnp.float32(table[m ^ frequency, m ^ time]), value)
+        return value
+
+    def told(note):
+        note = note.astype(f32)
+        half = note.shape[0] // 2
+        return [jnp.max(note[:half]).astype(jnp.int32), jnp.max(note[half:]).astype(jnp.int32)]
+
+    own = [offset + 1 for offset in told(note_ref[...])]
+    following = [offset + 2 for offset in told(head_ref[place])]
 
     def pick(green, places):
         occ = jnp.concatenate([green[p, :nu, :] for p in places], 0)
@@ -193,19 +213,19 @@
     for i in range(n):
         first, first_swapped = pick(greens[i], own)
         _, second_swapped = pick(greens[i], following)
-        term = table[me, me ^ i] * mm_nt(first, first_swapped)
+        term = weight(0, i) * mm_nt(first, first_swapped)
         center = term if center is None else center + term
         terms[i] = mm_nt(second_swapped, first)
     center_ref[...] = center.astype(bf16)
     size = center_ref.shape[0]
     for q in range(n):
-        total = table[me ^ q, me] * terms[0]
+        total = weight(q, 0) * terms[0]
         for i in range(1, n):
-            total = total + table[me ^ q, me ^ i] * terms[i]
+            total = total + weight(q, i) * terms[i]
         right_ref[:, q * size : (q + 1) * size] = total.astype(bf16)
 
 
-def weights(offsets, head, place, greens):
+def weights(note, head, place, greens):
     n = len(greens)
     size = 2 * greens[0].shape[1] // 2
     return pl.pallas_call(
@@ -214,7 +234,7 @@
             jax.ShapeDtypeStruct((size, size), bf16),
             jax.ShapeDtypeStruct((size, n * size), bf16),
         ],
-        in_specs=[SMEM, SMEM] + spec_all(n + 1),
+        in_specs=spec_all(n + 2),
         out_specs=spec_all(2),
         scratch_shapes=[pltpu.VMEM((n, size, size), f32)],
         compiler_params=pltpu.CompilerParams(vmem_limit_bytes=VMEM_BYTES),
@@ -222,7 +242,7 @@
             flops=4 * n * size**3 // COST, bytes_accessed=n * size**2 * 4 // COST, transcendentals=0
         ),
         name="weights",
-    )(offsets, jnp.asarray(cosine_table()), head, *greens)
+    )(note, head, *greens)
 
 
 def product(rows_ref, first, count, left):
@@ -343,30 +363,34 @@
     return high, (value - high.astype(f32)).astype(bf16)
 
 
-def upper_kernel(n, pattern, center_ref, above_ref, *refs):
-    pieces, (out_ref, middle_ref, right_t, block, sem) = refs[:n], refs[n:]
+def upper_kernel(n, pattern, center_ref, even_ref, odd_ref, *refs):
+    pieces, (out_ref, middle_ref, masks_ref, right_t, block, sem) = refs[:n], refs[n:]
     me = lax.axis_index("tm")
     cols = pieces[0].shape[0]
     size = center_ref.shape[0]
     for i in range(n):
         start = pl.multiple_of((me ^ i) * cols, cols)
         right_t[pl.ds(start, cols), :] = pieces[i][...]
+    parity = lax.axis_index("region") % 2
+    above = jnp.where(parity == 0, even_ref[...], odd_ref[...])
     mask = pattern[0, 2].astype(f32)
     upper = right_t[...].T * mask.astype(bf16)
     center = center_ref[...]
     high, low = split(center)
     block[...] = mask * (
-        upper.astype(f32) + mm(upper, above_ref[...]) + mm(high, upper) + mm(low, upper)
+        upper.astype(f32) + mm(upper, above) + mm(high, upper) + mm(low, upper)
     )
     copy = pltpu.make_async_copy(block, out_ref.at[0, :, pl.ds(2 * size, size)], sem)
     copy.start()
     middle_ref[...] = (
         center + mm_nt(upper, upper) + mm(high, high) + mm(high, low) + mm(low, high)
     )
+    for e in range(2):
+        masks_ref[e] = jnp.full(masks_ref.shape[1:], pattern[0, e].astype(f32))
     copy.wait()
 
 
-def upper_blocks(pattern, center, above, pieces):
+def upper_blocks(pattern, center, even, odd, pieces):
     n = len(pieces)
     size = center.shape[0]
     return pl.pallas_call(
@@ -374,9 +398,10 @@
         out_shape=[
             jax.ShapeDtypeStruct((1, size, 3 * size), f32),
             jax.ShapeDtypeStruct((size, size), f32),
-        ],
-        in_specs=[SMEM] + spec_all(2 + n),
-        out_specs=[HBM] + spec_all(1),
+            jax.ShapeDtypeStruct((2, 8, size), f32),
+        ],
+        in_specs=[SMEM] + spec_all(3 + n),
+        out_specs=[HBM] + spec_all(2),
         scratch_shapes=[
             pltpu.VMEM((size, size), bf16),
             pltpu.VMEM((size, size), f32),
@@ -387,17 +412,19 @@
             flops=16 * size**3 // COST, bytes_accessed=12 * size**2 // COST, transcendentals=0
         ),
         name="upper",
-    )(pattern, center, above, *pieces)
-
-
-def lower_kernel(n, pattern, center_ref, middle_ref, below_ref, left_ref, _, out_ref, left, blocks, sems):
+    )(pattern, center, even, odd, *pieces)
+
+
+def lower_kernel(n, masks_ref, center_ref, middle_ref, even_ref, odd_ref, left_ref, _, out_ref, left, blocks, sems):
     me = lax.axis_index("tm")
     cols = left_ref.shape[1]
     size = center_ref.shape[0]
     for i in range(n):
         start = pl.multiple_of((me ^ i) * cols, cols)
         left[pl.ds(start, cols), :] = left_ref[i]
-    masks = [pattern[0, e].astype(f32) for e in range(2)]
+    parity = lax.axis_index("region") % 2
+    below = jnp.where(parity == 0, odd_ref[...], even_ref[...])
+    masks = [masks_ref[e, :1, :] for e in range(2)]
     lower = left[...] * masks[0].astype(bf16)
     high, low = split(center_ref[...])
     copies = [
@@ -407,7 +434,7 @@
         for e in range(2)
     ]
     blocks[0] = masks[0] * (
-        lower.astype(f32) + mm(lower, below_ref[...]) + mm(high, lower) + mm(low, lower)
+        lower.astype(f32) + mm(lower, below) + mm(high, lower) + mm(low, lower)
     )
     copies[0].start()
     blocks[1] = masks[1] * (middle_ref[...] + mm_nt(lower, lower))
@@ -416,15 +443,15 @@
         copy.wait()
 
 
-def lower_blocks(pattern, center, middle, below, left, out):
+def lower_blocks(masks, center, middle, even, odd, left, out):
     n = left.shape[0]
     size = center.shape[0]
     return pl.pallas_call(
         functools.partial(lower_kernel, n),
         out_shape=jax.ShapeDtypeStruct((1, size, 3 * size), f32),
-        in_specs=[SMEM] + spec_all(4) + [HBM],
+        in_specs=spec_all(6) + [HBM],
         out_specs=HBM,
-        input_output_aliases={5: 0},
+        input_output_aliases={6: 0},
         scratch_shapes=[
             pltpu.VMEM((size, size), bf16),
             pltpu.VMEM((2, size, size), f32),
@@ -435,7 +462,7 @@
             flops=10 * size**3 // COST, bytes_accessed=12 * size**2 // COST, transcendentals=0
         ),
         name="lower",
-    )(pattern, center, middle, below, left, out)
+    )(masks, center, middle, even, odd, left, out)
 
 
 def local(tensor, g_occ, g_virt, offsets, pattern):
@@ -447,13 +474,13 @@
     blocks = nu // TILE
     lines = mus * kb
     groups, cols = lines // TILE, rows // n
-    cuts = (0, 64, groups * cols)
+    cuts = (0, cols, groups * cols)
     spans = tuple(zip(cuts, cuts[1:]))
     lined = tensor.reshape(rows, lines, nu)
     split_rows = lambda x: x.reshape(blocks, TILE, lam)
     own = jnp.concatenate([g_occ[0], g_virt[0]], 0)
-    below, second = shift(own, 1), shift(own, -2)
-    head, tail = prepare(offsets, lined, split_rows(g_occ), split_rows(g_virt), spans, n)
+    second, below = shift(own, -2), shift(own, 1)
+    head, tail, note = prepare(offsets, lined, split_rows(g_occ), split_rows(g_virt), spans, n)
     far_head, far_tail = shift(head, -1), shift(tail, -1)
 
     size = 2 * nu
@@ -469,23 +496,30 @@
             greens[i ^ bit] = partner(greens[i], bit)
         bit //= 2
     center_weight, right_weight = weights(
-        offsets, far_head, 2 * blocks, [greens[i] for i in range(n)]
+        note, far_head, 2 * blocks, [greens[i] for i in range(n)]
     )
 
     center, center_low = center_block(scale, turned_rows, center_weight, 4)
 
     right_weight, center = lax.optimization_barrier((right_weight, center))
     lead = 2 * blocks + 1
+    begun = right_part(
+        scale, (far_head,), spans[:1], (lead,), kb, right_weight, turned_rows,
+        None, (0, 1), False, 4,
+    )
     parts = right_part(
-        scale, (far_head, far_tail), spans, (lead, 0), kb, right_weight, turned_rows,
-        None, (0, groups), True, 4,
-    )
-    pieces = [parts[0]] + [partner(parts[i], i) for i in range(1, n)]
-    center_below, center_above = shift(center_low, 1), shift(center_low, -1)
-    *pieces, center_above = lax.optimization_barrier((*pieces, center_above))
+        scale, (far_tail,), spans[1:], (0,), kb, right_weight, turned_rows,
+        begun[0], (1, groups), True, 4,
+    )
+    pieces = dict(enumerate(parts))
+    for i in range(n - 1, 0, -1):
+        pieces[i] = partner(parts[i], i)
+    pieces = [pieces[i] for i in range(n)]
+    even, odd = swap_pairs(center_low, 0), swap_pairs(center_low, 1)
+    *pieces, even = lax.optimization_barrier((*pieces, even))
     left = shift(jnp.stack(pieces, 0), 1)
-    out, middle = upper_blocks(pattern, center, center_above, pieces)
-    return lower_blocks(pattern, center, middle, center_below, left, out)
+    out, middle, masks = upper_blocks(pattern, center, even, odd, pieces)
+    return lower_blocks(masks, center, middle, even, odd, left, out)
 
 
 def solution(mesh):

time: 52.1 us -> 50.6 us (0.971)
  starting transfers between devices: 23.1 us -> 20.4 us
  waiting for transfers between devices: 12.6 us -> 14.5 us
    ppermute x7 -> x5, starting transfers between devices: 19.5 us -> 13.2 us  [shift(): return lax.ppermute(block, 'region', route)]
    ppermute x0 -> x2, starting transfers between devices: none -> 3.52 us  [swap_pairs(): return lax.ppermute(block, 'region', route)]
    ppermute x6, waiting for transfers between devices: 3.61 us -> 5.99 us  [partner(): lax.ppermute(block, 'tm', [(i, i ^ bit) for i in range(lax.axis_size('tm'...]
    pallas_call x1, Pallas kernels: 1.66 us -> 1.14 us  [lower_blocks(): pl.pallas_call(functools.partial(lower_kernel, n), out_shape=jax.ShapeDty...]
    pallas_call x1 -> x2, Pallas kernels: 3.15 us -> 3.63 us  [right_part(): pl.pallas_call(functools.partial(right_kernel, n, kb, spans, leads, group...]
    ppermute x7 -> x5, waiting for transfers between devices: 8.99 us -> 8.54 us  [shift(): return lax.ppermute(block, 'region', route)]
  transfers between devices with their start and end apart: 13 -> 13, of which waited for: 6 -> 7; matrix products, arithmetic and copies ran while one was open for 0% -> 0% of each run, Pallas kernels for 23% -> 23%
where the time goes in v5:
time: 50.6 us; the launch traced here: 50.4 us
  starting transfers between devices  20.4 us (40%)
  Pallas kernels  15.2 us (30%)
  waiting for transfers between devices  14.5 us (29%)
    ppermute x5, starting transfers between devices, shift(): return lax.ppermute(block, 'region', route)  13.2 us
    ppermute x5, waiting for transfers between devices, shift(): return lax.ppermute(block, 'region', route)  8.54 us
    ppermute x6, waiting for transfers between devices, partner(): lax.ppermute(block, 'tm', [(i, i ^ bit) for i in range(lax.axis_size('tm'...  5.99 us
    pallas_call x2, Pallas kernels, right_part(): pl.pallas_call(functools.partial(right_kernel, n, kb, spans, leads, group...  3.63 us
    ppermute x6, starting transfers between devices, partner(): lax.ppermute(block, 'tm', [(i, i ^ bit) for i in range(lax.axis_size('tm'...  3.59 us
    ppermute x2, starting transfers between devices, swap_pairs(): return lax.ppermute(block, 'region', route)  3.52 us
    pallas_call x1, Pallas kernels, relayout(): pl.pallas_call(functools.partial(relayout_kernel, kb, chunks), out_shape=...  3.02 us
    pallas_call x1, Pallas kernels, center_block(): pl.pallas_call(functools.partial(center_kernel, scale, group), out_shape=...  2.7 us
  transfers between devices with their start and end apart: 13, of which 7 were waited for; matrix products, arithmetic and copies ran while one was open for 0% of the time, Pallas kernels for 23%

profile of v5, /device:TPU:0, one launch (start us, length us, event | category | flops | bytes accessed | tf_op | source)
XLA Modules:
  0.0 50.4 jit_solution(13242384607165894527)
XLA Ops:
  0.0 2.3 %prepare.1 = (bf16[81,16,128]{2,1,0:T(8,128)(2,1)}, bf16[192,16,128]{2,1,0:T(8,128)(2,1)}, bf16[16,128]{1,0:T(8,128)(2,1)}) custom-call(s32[1,2]{1,0:T(1,128)} %offsets_ref.1, bf16[256,64,128]{2,1,0:T(8,128)(2,1)} %bitcast.18, bf16[8,16,128]{2,1,0:T(8,128)(2,1)} %bitcast.21, bf16[8,16,128]{2,1,0:T(8,128)(2,1)} %bitcast.23), custom_call_target="tpu_custom_call" | custom-call | bytes 349525 | tf_op jit(solution)/shard_map/prepare/pallas_call | solution.py:171
  2.3 1.3 %collective-permute-start = (bf16[81,16,128]{2,1,0:T(8,128)(2,1)}, bf16[81,16,128]{2,1,0:T(8,128)(2,1)S(1)}, u32[]{:S(2)}, u32[]{:S(2)}) collective-permute-start(bf16[81,16,128]{2,1,0:T(8,128)(2,1)} %get-tuple-element.29), channel_id=1, source_target_pairs={{4,0},{8,4},{12,8},{16,12},{20,16},{24,20},{28,24},{5,1},{9,5},{13... | collective-permute-start | bytes 995336 | tf_op jit(solution)/shard_map/ppermute | solution.py:34
  3.6 1.3 %collective-permute-start.2 = (bf16[256,128]{1,0:T(8,128)(2,1)S(1)}, bf16[256,128]{1,0:T(8,128)(2,1)S(1)}, u32[]{:S(2)}, u32[]{:S(2)}) collective-permute-start(bf16[256,128]{1,0:T(8,128)(2,1)S(1)} %get-tuple-element.52), channel_id=1, source_target_pairs={{8,0},{12,4},{16,8},{20,12},{24,16},{28,20},{9,1},{13,5},{17,9},{2... | collective-permute-start | bytes 196616 | tf_op jit(solution)/shard_map/ppermute | solution.py:34
  4.9 5.5 %collective-permute-start.1 = (bf16[256,128]{1,0:T(8,128)(2,1)S(1)}, bf16[256,128]{1,0:T(8,128)(2,1)S(1)}, u32[]{:S(2)}, u32[]{:S(2)}) collective-permute-start(bf16[256,128]{1,0:T(8,128)(2,1)S(1)} %get-tuple-element.52), channel_id=1, source_target_pairs={{0,4},{4,8},{8,12},{12,16},{16,20},{20,24},{24,28},{1,5},{5,9},{9,... | collective-permute-start | bytes 196616 | tf_op jit(solution)/shard_map/ppermute | solution.py:34
  10.4 1.3 %collective-permute-start.6 = (bf16[192,16,128]{2,1,0:T(8,128)(2,1)}, bf16[192,16,128]{2,1,0:T(8,128)(2,1)S(1)}, u32[]{:S(2)}, u32[]{:S(2)}) collective-permute-start(bf16[192,16,128]{2,1,0:T(8,128)(2,1)} %get-tuple-element.36), channel_id=1, source_target_pairs={{4,0},{8,4},{12,8},{16,12},{20,16},{24,20},{28,24},{5,1},{9,5},{13... | collective-permute-start | bytes 2359304 | tf_op jit(solution)/shard_map/ppermute | solution.py:34
  11.7 3.4 %collective-permute-done.head_ref.refs_0_ = bf16[81,16,128]{2,1,0:T(8,128)(2,1)S(1)} collective-permute-done((bf16[81,16,128]{2,1,0:T(8,128)(2,1)}, bf16[81,16,128]{2,1,0:T(8,128)(2,1)S(1)}, u32[]{:S(2)}, u32[]{:S(2)}) %collective-permute-start) | collective-permute-done | bytes 331808 | tf_op jit(solution)/shard_map/ppermute | solution.py:34
  15.2 2.9 %collective-permute-done.2 = bf16[256,128]{1,0:T(8,128)(2,1)S(1)} collective-permute-done((bf16[256,128]{1,0:T(8,128)(2,1)S(1)}, bf16[256,128]{1,0:T(8,128)(2,1)S(1)}, u32[]{:S(2)}, u32[]{:S(2)}) %collective-permute-start.2) | collective-permute-done | bytes 65568 | tf_op jit(solution)/shard_map/ppermute | solution.py:34
  18.1 1.6 %collective-permute-start.4 = (bf16[4,256,128]{2,1,0:T(8,128)(2,1)S(1)}, bf16[4,256,128]{2,1,0:T(8,128)(2,1)S(1)}, u32[]{:S(2)}, u32[]{:S(2)}) collective-permute-start(bf16[4,256,128]{2,1,0:T(8,128)(2,1)S(1)} %pad_maximum_fusion.refs_0_), channel_id=1, source_target_pairs={{0,2},{1,3},{2,0},{3,1},{4,6},{5,7},{6,4},{7,5},{8,10},{9,11},{10,... | collective-permute-start | bytes 786440 | tf_op jit(solution)/shard_map/ppermute | solution.py:46
  19.7 3.0 %relayout.1.rows_ref.refs_2_ = bf16[32,256,256]{2,1,0:T(8,128)(2,1)S(1)} custom-call(bf16[256,64,128]{2,1,0:T(8,128)(2,1)} %bitcast.19), custom_call_target="tpu_custom_call" | custom-call | bytes 2796202 | tf_op jit(solution)/shard_map/relayout/pallas_call | solution.py:111
  22.8 2.1 %collective-permute-done.4.refs_2_ = bf16[4,256,128]{2,1,0:T(8,128)(2,1)S(1)} collective-permute-done((bf16[4,256,128]{2,1,0:T(8,128)(2,1)S(1)}, bf16[4,256,128]{2,1,0:T(8,128)(2,1)S(1)}, u32[]{:S(2)}, u32[]{:S(2)}) %collective-permute-start.4) | collective-permute-done | bytes 262176 | tf_op jit(solution)/shard_map/ppermute | solution.py:46
  24.9 1.5 %collective-permute-done.5.refs_3_ = bf16[4,256,128]{2,1,0:T(8,128)(2,1)S(1)} collective-permute-done((bf16[4,256,128]{2,1,0:T(8,128)(2,1)S(1)}, bf16[4,256,128]{2,1,0:T(8,128)(2,1)S(1)}, u32[]{:S(2)}, u32[]{:S(2)}) %collective-permute-start.5) | collective-permute-done | bytes 262176 | tf_op jit(solution)/shard_map/ppermute | solution.py:46
  26.4 0.8 %weights.1 = (bf16[256,256]{1,0:T(8,128)(2,1)S(1)}, bf16[256,1024]{1,0:T(8,128)(2,1)S(1)}) custom-call(bf16[16,128]{1,0:T(8,128)(2,1)S(1)} %copy-done, bf16[81,16,128]{2,1,0:T(8,128)(2,1)S(1)} %collective-permute-done.head_ref.refs_0_, bf16[4,256,128]{2,1,0:T(8,128)(2,1)S(1)} %pad_maximum_fusion.refs_0_, ...), custom_call_target="tpu_custom_call" | custom-call | flops 89478488 | bytes 349525 | tf_op jit(solution)/shard_map/weights/pallas_call | solution.py:231
  27.2 2.7 %center.1 = (f32[256,256]{1,0:T(8,128)S(1)}, bf16[256,256]{1,0:T(8,128)(2,1)S(1)}) custom-call(bf16[32,256,256]{2,1,0:T(8,128)(2,1)S(1)} %relayout.1.rows_ref.refs_2_, bf16[256,256]{1,0:T(8,128)(2,1)S(1)} %get-tuple-element.33.weight_ref), custom_call_target="tpu_custom_call" | custom-call | flops 715827904 | bytes 1398101 | tf_op jit(solution)/shard_map/center/pallas_call | solution.py:268
  29.9 2.9 %collective-permute-start.10 = (bf16[256,256]{1,0:T(8,128)(2,1)S(1)}, bf16[256,256]{1,0:T(8,128)(2,1)S(1)}, u32[]{:S(2)}, u32[]{:S(2)}) collective-permute-start(bf16[256,256]{1,0:T(8,128)(2,1)S(1)} %get-tuple-element.42), channel_id=1, source_target_pairs={{0,4},{4,0},{8,12},{12,8},{16,20},{20,16},{24,28},{28,24},{1,5},{5... | collective-permute-start | bytes 393224 | tf_op jit(solution)/shard_map/ppermute | solution.py:42
  32.8 1.4 %right.2.refs_3_ = f32[256,256]{1,0:T(8,128)S(1)} custom-call(bf16[81,16,128]{2,1,0:T(8,128)(2,1)S(1)} %collective-permute-done.head_ref.refs_0_, bf16[256,1024]{1,0:T(8,128)(2,1)S(1)} %get-tuple-element.37.refs_1_, bf16[32,256,256]{2,1,0:T(8,128)(2,1)S(1)} %relayout.1.rows_ref.refs_2_), custom_call_target="tpu_custom_call" | custom-call | flops 178956976 | bytes 349525 | tf_op jit(solution)/shard_map/right/pallas_call | solution.py:343
  34.2 2.3 %right.3 = (bf16[64,256]{1,0:T(8,128)(2,1)S(1)}, bf16[64,256]{1,0:T(8,128)(2,1)S(1)}, bf16[64,256]{1,0:T(8,128)(2,1)S(1)}, bf16[64,256]{1,0:T(8,128)(2,1)S(1)}) custom-call(bf16[192,16,128]{2,1,0:T(8,128)(2,1)S(1)} %collective-permute-done.6.refs_0_, bf16[256,1024]{1,0:T(8,128)(2,1)S(1)} %get-tuple-element.37.refs_1_, ...), custom_call_target="tpu_custom_call" | custom-call | flops 536870912 | bytes 1048576 | tf_op jit(solution)/shard_map/right/pallas_call | solution.py:343
  36.5 1.6 %collective-permute-start.8 = (bf16[64,256]{1,0:T(8,128)(2,1)S(1)}, bf16[64,256]{1,0:T(8,128)(2,1)S(1)}, u32[]{:S(2)}, u32[]{:S(2)}) collective-permute-start(bf16[64,256]{1,0:T(8,128)(2,1)S(1)} %get-tuple-element.40), channel_id=1, source_target_pairs={{0,2},{1,3},{2,0},{3,1},{4,6},{5,7},{6,4},{7,5},{8,10},{9,11},{10,... | collective-permute-start | bytes 98312 | tf_op jit(solution)/shard_map/ppermute | solution.py:46
  38.4 0.7 %collective-permute-start.11 = (bf16[256,256]{1,0:T(8,128)(2,1)S(1)}, bf16[256,256]{1,0:T(8,128)(2,1)S(1)}, u32[]{:S(2)}, u32[]{:S(2)}) collective-permute-start(bf16[256,256]{1,0:T(8,128)(2,1)S(1)} %get-tuple-element.42), channel_id=1, source_target_pairs={{4,8},{8,4},{12,16},{16,12},{20,24},{24,20},{5,9},{9,5},{13,17},{1... | collective-permute-start | bytes 393224 | tf_op jit(solution)/shard_map/ppermute | solution.py:42
  39.1 1.4 %collective-permute-done.8.refs_2_ = bf16[64,256]{1,0:T(8,128)(2,1)S(1)} collective-permute-done((bf16[64,256]{1,0:T(8,128)(2,1)S(1)}, bf16[64,256]{1,0:T(8,128)(2,1)S(1)}, u32[]{:S(2)}, u32[]{:S(2)}) %collective-permute-start.8) | collective-permute-done | bytes 32800 | tf_op jit(solution)/shard_map/ppermute | solution.py:46
  40.5 0.9 %collective-permute-done.9.refs_3_ = bf16[64,256]{1,0:T(8,128)(2,1)S(1)} collective-permute-done((bf16[64,256]{1,0:T(8,128)(2,1)S(1)}, bf16[64,256]{1,0:T(8,128)(2,1)S(1)}, u32[]{:S(2)}, u32[]{:S(2)}) %collective-permute-start.9) | collective-permute-done | bytes 32800 | tf_op jit(solution)/shard_map/ppermute | solution.py:46
  41.5 3.9 %collective-permute-start.12 = (bf16[4,64,256]{2,1,0:T(8,128)(2,1)S(1)}, bf16[4,64,256]{2,1,0:T(8,128)(2,1)S(1)}, u32[]{:S(2)}, u32[]{:S(2)}) collective-permute-start(bf16[4,64,256]{2,1,0:T(8,128)(2,1)S(1)} %pad_maximum_fusion.1), channel_id=1, source_target_pairs={{0,4},{4,8},{8,12},{12,16},{16,20},{20,24},{24,28},{1,5},{5,9},{9,... | collective-permute-start | bytes 393224 | tf_op jit(solution)/shard_map/ppermute | solution.py:34
  45.4 1.7 %upper.1 = (f32[1,256,768]{2,1,0:T(8,128)}, f32[256,256]{1,0:T(8,128)S(1)}, f32[2,8,256]{2,1,0:T(8,128)S(1)}) custom-call(s32[1,3]{1,0:T(1,128)S(1)} %copy-done.1, f32[256,256]{1,0:T(8,128)S(1)} %get-tuple-element.35.center_ref, bf16[256,256]{1,0:T(8,128)(2,1)S(1)} %collective-permute-done.10.even_ref, bf16[256,256]{1,0:T(8,128)(2,1)S(1)} %collective-permute-done.11.odd_ref, ...), custom_call_target="tpu_custom_call" | custom-call | flops 89478488 | bytes 262144 | tf_op jit(solution)/shard_map/upper/pallas_call | solution.py:396
  47.1 2.2 %collective-permute-done.12.left_ref = bf16[4,64,256]{2,1,0:T(8,128)(2,1)S(1)} collective-permute-done((bf16[4,64,256]{2,1,0:T(8,128)(2,1)S(1)}, bf16[4,64,256]{2,1,0:T(8,128)(2,1)S(1)}, u32[]{:S(2)}, u32[]{:S(2)}) %collective-permute-start.12) | collective-permute-done | bytes 131104 | tf_op jit(solution)/shard_map/ppermute | solution.py:34
  49.2 1.1 %lower.1 = f32[1,256,768]{2,1,0:T(8,128)} custom-call(f32[2,8,256]{2,1,0:T(8,128)S(1)} %get-tuple-element.48.masks_ref, f32[256,256]{1,0:T(8,128)S(1)} %get-tuple-element.35.center_ref, f32[256,256]{1,0:T(8,128)S(1)} %get-tuple-element.49.middle_ref, bf16[256,256]{1,0:T(8,128)(2,1)S(1)} %collective-permute-done.10.even_ref, ...), custom_call_target="tpu_custom_call", output_to_operand_aliasing={{}: (6, {})} | custom-call | flops 55924052 | bytes 262144 | tf_op jit(solution)/shard_map/lower/pallas_call | solution.py:449
  (22 shorter events, 0.5 us)
Async XLA Ops:
  0.0 3.6 %copy-start.2 = (bf16[1,128,128]{2,1,0:T(8,128)(2,1)S(1)}, bf16[1,128,128]{2,1,0:T(8,128)(2,1)}, u32[]{:S(2)}) copy-start(bf16[1,128,128]{2,1,0:T(8,128)(2,1)} %param.6) | copy-start | bytes 98308
  0.0 3.6 %copy-start.3 = (bf16[1,128,128]{2,1,0:T(8,128)(2,1)S(1)}, bf16[1,128,128]{2,1,0:T(8,128)(2,1)}, u32[]{:S(2)}) copy-start(bf16[1,128,128]{2,1,0:T(8,128)(2,1)} %param.7) | copy-start | bytes 98308
  2.3 12.8 %collective-permute-start = (bf16[81,16,128]{2,1,0:T(8,128)(2,1)}, bf16[81,16,128]{2,1,0:T(8,128)(2,1)S(1)}, u32[]{:S(2)}, u32[]{:S(2)}) collective-permute-start(bf16[81,16,128]{2,1,0:T(8,128)(2,1)} %get-tuple-element.29), channel_id=1, source_target_pairs={{4,0},{8,4},{12,8},{16,12},{20,16},{24,20},{28,24},{5,1},{9,5},{13... | collective-permute-start | bytes 995336 | tf_op jit(solution)/shard_map/ppermute | solution.py:34
  3.6 14.4 %collective-permute-start.2 = (bf16[256,128]{1,0:T(8,128)(2,1)S(1)}, bf16[256,128]{1,0:T(8,128)(2,1)S(1)}, u32[]{:S(2)}, u32[]{:S(2)}) collective-permute-start(bf16[256,128]{1,0:T(8,128)(2,1)S(1)} %get-tuple-element.52), channel_id=1, source_target_pairs={{8,0},{12,4},{16,8},{20,12},{24,16},{28,20},{9,1},{13,5},{17,9},{2... | collective-permute-start | bytes 196616 | tf_op jit(solution)/shard_map/ppermute | solution.py:34
  4.9 13.2 %collective-permute-start.1 = (bf16[256,128]{1,0:T(8,128)(2,1)S(1)}, bf16[256,128]{1,0:T(8,128)(2,1)S(1)}, u32[]{:S(2)}, u32[]{:S(2)}) collective-permute-start(bf16[256,128]{1,0:T(8,128)(2,1)S(1)} %get-tuple-element.52), channel_id=1, source_target_pairs={{0,4},{4,8},{8,12},{12,16},{16,20},{20,24},{24,28},{1,5},{5,9},{9,... | collective-permute-start | bytes 196616 | tf_op jit(solution)/shard_map/ppermute | solution.py:34
  10.4 23.7 %collective-permute-start.6 = (bf16[192,16,128]{2,1,0:T(8,128)(2,1)}, bf16[192,16,128]{2,1,0:T(8,128)(2,1)S(1)}, u32[]{:S(2)}, u32[]{:S(2)}) collective-permute-start(bf16[192,16,128]{2,1,0:T(8,128)(2,1)} %get-tuple-element.36), channel_id=1, source_target_pairs={{4,0},{8,4},{12,8},{16,12},{20,16},{24,20},{28,24},{5,1},{9,5},{13... | collective-permute-start | bytes 2359304 | tf_op jit(solution)/shard_map/ppermute | solution.py:34
  18.1 8.3 %copy-start = (bf16[16,128]{1,0:T(8,128)(2,1)S(1)}, bf16[16,128]{1,0:T(8,128)(2,1)}, u32[]{:S(2)}) copy-start(bf16[16,128]{1,0:T(8,128)(2,1)} %get-tuple-element.28.note_ref) | copy-start | bytes 12292
  18.1 6.8 %collective-permute-start.4 = (bf16[4,256,128]{2,1,0:T(8,128)(2,1)S(1)}, bf16[4,256,128]{2,1,0:T(8,128)(2,1)S(1)}, u32[]{:S(2)}, u32[]{:S(2)}) collective-permute-start(bf16[4,256,128]{2,1,0:T(8,128)(2,1)S(1)} %pad_maximum_fusion.refs_0_), channel_id=1, source_target_pairs={{0,2},{1,3},{2,0},{3,1},{4,6},{5,7},{6,4},{7,5},{8,10},{9,11},{10,... | collective-permute-start | bytes 786440 | tf_op jit(solution)/shard_map/ppermute | solution.py:46
  22.8 2.2 %collective-permute-start.3 = (bf16[4,256,128]{2,1,0:T(8,128)(2,1)S(1)}, bf16[4,256,128]{2,1,0:T(8,128)(2,1)S(1)}, u32[]{:S(2)}, u32[]{:S(2)}) collective-permute-start(bf16[4,256,128]{2,1,0:T(8,128)(2,1)S(1)} %pad_maximum_fusion.refs_0_), channel_id=1, source_target_pairs={{0,1},{1,0},{2,3},{3,2},{4,5},{5,4},{6,7},{7,6},{8,9},{9,8},{10,11... | collective-permute-start | bytes 786440 | tf_op jit(solution)/shard_map/ppermute | solution.py:46
  24.9 1.5 %collective-permute-start.5 = (bf16[4,256,128]{2,1,0:T(8,128)(2,1)S(1)}, bf16[4,256,128]{2,1,0:T(8,128)(2,1)S(1)}, u32[]{:S(2)}, u32[]{:S(2)}) collective-permute-start(bf16[4,256,128]{2,1,0:T(8,128)(2,1)S(1)} %collective-permute-done.4.refs_2_), channel_id=1, source_target_pairs={{0,1},{1,0},{2,3},{3,2},{4,5},{5,4},{6,7},{7,6},{8,9},{9,8},{10,11... | collective-permute-start | bytes 786440 | tf_op jit(solution)/shard_map/ppermute | solution.py:46
  29.9 11.5 %collective-permute-start.10 = (bf16[256,256]{1,0:T(8,128)(2,1)S(1)}, bf16[256,256]{1,0:T(8,128)(2,1)S(1)}, u32[]{:S(2)}, u32[]{:S(2)}) collective-permute-start(bf16[256,256]{1,0:T(8,128)(2,1)S(1)} %get-tuple-element.42), channel_id=1, source_target_pairs={{0,4},{4,0},{8,12},{12,8},{16,20},{20,16},{24,28},{28,24},{1,5},{5... | collective-permute-start | bytes 393224 | tf_op jit(solution)/shard_map/ppermute | solution.py:42
  34.1 11.2 %copy-start.1 = (s32[1,3]{1,0:T(1,128)S(1)}, s32[1,3]{1,0:T(1,128)}, u32[]{:S(2)}) copy-start(s32[1,3]{1,0:T(1,128)} %pattern.1) | copy-start | bytes 40
  36.4 2.6 %collective-permute-start.7 = (bf16[64,256]{1,0:T(8,128)(2,1)S(1)}, bf16[64,256]{1,0:T(8,128)(2,1)S(1)}, u32[]{:S(2)}, u32[]{:S(2)}) collective-permute-start(bf16[64,256]{1,0:T(8,128)(2,1)S(1)} %get-tuple-element.39), channel_id=1, source_target_pairs={{0,1},{1,0},{2,3},{3,2},{4,5},{5,4},{6,7},{7,6},{8,9},{9,8},{10,11... | collective-permute-start | bytes 98312 | tf_op jit(solution)/shard_map/ppermute | solution.py:46
  36.5 4.0 %collective-permute-start.8 = (bf16[64,256]{1,0:T(8,128)(2,1)S(1)}, bf16[64,256]{1,0:T(8,128)(2,1)S(1)}, u32[]{:S(2)}, u32[]{:S(2)}) collective-permute-start(bf16[64,256]{1,0:T(8,128)(2,1)S(1)} %get-tuple-element.40), channel_id=1, source_target_pairs={{0,2},{1,3},{2,0},{3,1},{4,6},{5,7},{6,4},{7,5},{8,10},{9,11},{10,... | collective-permute-start | bytes 98312 | tf_op jit(solution)/shard_map/ppermute | solution.py:46
  38.1 3.3 %collective-permute-start.9 = (bf16[64,256]{1,0:T(8,128)(2,1)S(1)}, bf16[64,256]{1,0:T(8,128)(2,1)S(1)}, u32[]{:S(2)}, u32[]{:S(2)}) collective-permute-start(bf16[64,256]{1,0:T(8,128)(2,1)S(1)} %get-tuple-element.41), channel_id=1, source_target_pairs={{0,3},{1,2},{2,1},{3,0},{4,7},{5,6},{6,5},{7,4},{8,11},{9,10},{10,... | collective-permute-start | bytes 98312 | tf_op jit(solution)/shard_map/ppermute | solution.py:46
  38.4 7.0 %collective-permute-start.11 = (bf16[256,256]{1,0:T(8,128)(2,1)S(1)}, bf16[256,256]{1,0:T(8,128)(2,1)S(1)}, u32[]{:S(2)}, u32[]{:S(2)}) collective-permute-start(bf16[256,256]{1,0:T(8,128)(2,1)S(1)} %get-tuple-element.42), channel_id=1, source_target_pairs={{4,8},{8,4},{12,16},{16,12},{20,24},{24,20},{5,9},{9,5},{13,17},{1... | collective-permute-start | bytes 393224 | tf_op jit(solution)/shard_map/ppermute | solution.py:42
  41.5 7.8 %collective-permute-start.12 = (bf16[4,64,256]{2,1,0:T(8,128)(2,1)S(1)}, bf16[4,64,256]{2,1,0:T(8,128)(2,1)S(1)}, u32[]{:S(2)}, u32[]{:S(2)}) collective-permute-start(bf16[4,64,256]{2,1,0:T(8,128)(2,1)S(1)} %pad_maximum_fusion.1), channel_id=1, source_target_pairs={{0,4},{4,8},{8,12},{12,16},{16,20},{20,24},{24,28},{1,5},{5,9},{9,... | collective-permute-start | bytes 393224 | tf_op jit(solution)/shard_map/ppermute | solution.py:34

commit v6 on v5

--- a/solution.py
+++ b/solution.py
@@ -499,17 +499,17 @@
         note, far_head, 2 * blocks, [greens[i] for i in range(n)]
     )
 
-    center, center_low = center_block(scale, turned_rows, center_weight, 4)
+    center, center_low = center_block(scale, turned_rows, center_weight, 2)
 
     right_weight, center = lax.optimization_barrier((right_weight, center))
     lead = 2 * blocks + 1
     begun = right_part(
         scale, (far_head,), spans[:1], (lead,), kb, right_weight, turned_rows,
-        None, (0, 1), False, 4,
+        None, (0, 1), False, 2,
     )
     parts = right_part(
         scale, (far_tail,), spans[1:], (0,), kb, right_weight, turned_rows,
-        begun[0], (1, groups), True, 4,
+        begun[0], (1, groups), True, 2,
     )
     pieces = dict(enumerate(parts))
     for i in range(n - 1, 0, -1):

time: 50.6 us -> 50.5 us (level)
  transfers between devices with their start and end apart: 13 -> 13, of which waited for: 7 -> 7; matrix products, arithmetic and copies ran while one was open for 0% -> 0% of each run, Pallas kernels for 23% -> 22%
where the time goes in v6:
time: 50.5 us; the launch traced here: 50.3 us
  starting transfers between devices  20.7 us (41%)
  Pallas kernels  14.7 us (29%)
  waiting for transfers between devices  14.6 us (29%)
    ppermute x5, starting transfers between devices, shift(): return lax.ppermute(block, 'region', route)  13.6 us
    ppermute x5, waiting for transfers between devices, shift(): return lax.ppermute(block, 'region', route)  8.54 us
    ppermute x6, waiting for transfers between devices, partner(): lax.ppermute(block, 'tm', [(i, i ^ bit) for i in range(lax.axis_size('tm'...  6.01 us
    ppermute x6, starting transfers between devices, partner(): lax.ppermute(block, 'tm', [(i, i ^ bit) for i in range(lax.axis_size('tm'...  3.59 us
    ppermute x2, starting transfers between devices, swap_pairs(): return lax.ppermute(block, 'region', route)  3.52 us
    pallas_call x2, Pallas kernels, right_part(): pl.pallas_call(functools.partial(right_kernel, n, kb, spans, leads, group...  3.25 us
    pallas_call x1, Pallas kernels, relayout(): pl.pallas_call(functools.partial(relayout_kernel, kb, chunks), out_shape=...  3.02 us
    pallas_call x1, Pallas kernels, center_block(): pl.pallas_call(functools.partial(center_kernel, scale, group), out_shape=...  2.59 us
  transfers between devices with their start and end apart: 13, of which 7 were waited for; matrix products, arithmetic and copies ran while one was open for 0% of the time, Pallas kernels for 22%

profile of v6, /device:TPU:0, one launch (start us, length us, event | category | flops | bytes accessed | tf_op | source)
XLA Modules:
  0.0 50.3 jit_solution(9982678809114149489)
XLA Ops:
  0.0 2.3 %prepare.1 = (bf16[81,16,128]{2,1,0:T(8,128)(2,1)}, bf16[192,16,128]{2,1,0:T(8,128)(2,1)}, bf16[16,128]{1,0:T(8,128)(2,1)}) custom-call(s32[1,2]{1,0:T(1,128)} %offsets_ref.1, bf16[256,64,128]{2,1,0:T(8,128)(2,1)} %bitcast.18, bf16[8,16,128]{2,1,0:T(8,128)(2,1)} %bitcast.21, bf16[8,16,128]{2,1,0:T(8,128)(2,1)} %bitcast.23), custom_call_target="tpu_custom_call" | custom-call | bytes 349525 | tf_op jit(solution)/shard_map/prepare/pallas_call | solution.py:171
  2.3 1.3 %collective-permute-start = (bf16[81,16,128]{2,1,0:T(8,128)(2,1)}, bf16[81,16,128]{2,1,0:T(8,128)(2,1)S(1)}, u32[]{:S(2)}, u32[]{:S(2)}) collective-permute-start(bf16[81,16,128]{2,1,0:T(8,128)(2,1)} %get-tuple-element.29), channel_id=1, source_target_pairs={{4,0},{8,4},{12,8},{16,12},{20,16},{24,20},{28,24},{5,1},{9,5},{13... | collective-permute-start | bytes 995336 | tf_op jit(solution)/shard_map/ppermute | solution.py:34
  3.6 1.3 %collective-permute-start.2 = (bf16[256,128]{1,0:T(8,128)(2,1)S(1)}, bf16[256,128]{1,0:T(8,128)(2,1)S(1)}, u32[]{:S(2)}, u32[]{:S(2)}) collective-permute-start(bf16[256,128]{1,0:T(8,128)(2,1)S(1)} %get-tuple-element.52), channel_id=1, source_target_pairs={{8,0},{12,4},{16,8},{20,12},{24,16},{28,20},{9,1},{13,5},{17,9},{2... | collective-permute-start | bytes 196616 | tf_op jit(solution)/shard_map/ppermute | solution.py:34
  4.9 5.5 %collective-permute-start.1 = (bf16[256,128]{1,0:T(8,128)(2,1)S(1)}, bf16[256,128]{1,0:T(8,128)(2,1)S(1)}, u32[]{:S(2)}, u32[]{:S(2)}) collective-permute-start(bf16[256,128]{1,0:T(8,128)(2,1)S(1)} %get-tuple-element.52), channel_id=1, source_target_pairs={{0,4},{4,8},{8,12},{12,16},{16,20},{20,24},{24,28},{1,5},{5,9},{9,... | collective-permute-start | bytes 196616 | tf_op jit(solution)/shard_map/ppermute | solution.py:34
  10.4 1.3 %collective-permute-start.6 = (bf16[192,16,128]{2,1,0:T(8,128)(2,1)}, bf16[192,16,128]{2,1,0:T(8,128)(2,1)S(1)}, u32[]{:S(2)}, u32[]{:S(2)}) collective-permute-start(bf16[192,16,128]{2,1,0:T(8,128)(2,1)} %get-tuple-element.36), channel_id=1, source_target_pairs={{4,0},{8,4},{12,8},{16,12},{20,16},{24,20},{28,24},{5,1},{9,5},{13... | collective-permute-start | bytes 2359304 | tf_op jit(solution)/shard_map/ppermute | solution.py:34
  11.7 3.4 %collective-permute-done.head_ref.refs_0_ = bf16[81,16,128]{2,1,0:T(8,128)(2,1)S(1)} collective-permute-done((bf16[81,16,128]{2,1,0:T(8,128)(2,1)}, bf16[81,16,128]{2,1,0:T(8,128)(2,1)S(1)}, u32[]{:S(2)}, u32[]{:S(2)}) %collective-permute-start) | collective-permute-done | bytes 331808 | tf_op jit(solution)/shard_map/ppermute | solution.py:34
  15.2 2.9 %collective-permute-done.2 = bf16[256,128]{1,0:T(8,128)(2,1)S(1)} collective-permute-done((bf16[256,128]{1,0:T(8,128)(2,1)S(1)}, bf16[256,128]{1,0:T(8,128)(2,1)S(1)}, u32[]{:S(2)}, u32[]{:S(2)}) %collective-permute-start.2) | collective-permute-done | bytes 65568 | tf_op jit(solution)/shard_map/ppermute | solution.py:34
  18.1 1.6 %collective-permute-start.4 = (bf16[4,256,128]{2,1,0:T(8,128)(2,1)S(1)}, bf16[4,256,128]{2,1,0:T(8,128)(2,1)S(1)}, u32[]{:S(2)}, u32[]{:S(2)}) collective-permute-start(bf16[4,256,128]{2,1,0:T(8,128)(2,1)S(1)} %pad_maximum_fusion.refs_0_), channel_id=1, source_target_pairs={{0,2},{1,3},{2,0},{3,1},{4,6},{5,7},{6,4},{7,5},{8,10},{9,11},{10,... | collective-permute-start | bytes 786440 | tf_op jit(solution)/shard_map/ppermute | solution.py:46
  19.7 3.0 %relayout.1.rows_ref.refs_2_ = bf16[32,256,256]{2,1,0:T(8,128)(2,1)S(1)} custom-call(bf16[256,64,128]{2,1,0:T(8,128)(2,1)} %bitcast.19), custom_call_target="tpu_custom_call" | custom-call | bytes 2796202 | tf_op jit(solution)/shard_map/relayout/pallas_call | solution.py:111
  22.8 2.1 %collective-permute-done.4.refs_2_ = bf16[4,256,128]{2,1,0:T(8,128)(2,1)S(1)} collective-permute-done((bf16[4,256,128]{2,1,0:T(8,128)(2,1)S(1)}, bf16[4,256,128]{2,1,0:T(8,128)(2,1)S(1)}, u32[]{:S(2)}, u32[]{:S(2)}) %collective-permute-start.4) | collective-permute-done | bytes 262176 | tf_op jit(solution)/shard_map/ppermute | solution.py:46
  24.9 1.5 %collective-permute-done.5.refs_3_ = bf16[4,256,128]{2,1,0:T(8,128)(2,1)S(1)} collective-permute-done((bf16[4,256,128]{2,1,0:T(8,128)(2,1)S(1)}, bf16[4,256,128]{2,1,0:T(8,128)(2,1)S(1)}, u32[]{:S(2)}, u32[]{:S(2)}) %collective-permute-start.5) | collective-permute-done | bytes 262176 | tf_op jit(solution)/shard_map/ppermute | solution.py:46
  26.4 0.8 %weights.1 = (bf16[256,256]{1,0:T(8,128)(2,1)S(1)}, bf16[256,1024]{1,0:T(8,128)(2,1)S(1)}) custom-call(bf16[16,128]{1,0:T(8,128)(2,1)S(1)} %copy-done, bf16[81,16,128]{2,1,0:T(8,128)(2,1)S(1)} %collective-permute-done.head_ref.refs_0_, bf16[4,256,128]{2,1,0:T(8,128)(2,1)S(1)} %pad_maximum_fusion.refs_0_, ...), custom_call_target="tpu_custom_call" | custom-call | flops 89478488 | bytes 349525 | tf_op jit(solution)/shard_map/weights/pallas_call | solution.py:231
  27.2 2.6 %center.1 = (f32[256,256]{1,0:T(8,128)S(1)}, bf16[256,256]{1,0:T(8,128)(2,1)S(1)}) custom-call(bf16[32,256,256]{2,1,0:T(8,128)(2,1)S(1)} %relayout.1.rows_ref.refs_2_, bf16[256,256]{1,0:T(8,128)(2,1)S(1)} %get-tuple-element.33.weight_ref), custom_call_target="tpu_custom_call" | custom-call | flops 715827904 | bytes 1398101 | tf_op jit(solution)/shard_map/center/pallas_call | solution.py:268
  29.8 2.9 %collective-permute-start.10 = (bf16[256,256]{1,0:T(8,128)(2,1)S(1)}, bf16[256,256]{1,0:T(8,128)(2,1)S(1)}, u32[]{:S(2)}, u32[]{:S(2)}) collective-permute-start(bf16[256,256]{1,0:T(8,128)(2,1)S(1)} %get-tuple-element.42), channel_id=1, source_target_pairs={{0,4},{4,0},{8,12},{12,8},{16,20},{20,16},{24,28},{28,24},{1,5},{5... | collective-permute-start | bytes 393224 | tf_op jit(solution)/shard_map/ppermute | solution.py:42
  32.7 1.1 %right.2.refs_3_ = f32[256,256]{1,0:T(8,128)S(1)} custom-call(bf16[81,16,128]{2,1,0:T(8,128)(2,1)S(1)} %collective-permute-done.head_ref.refs_0_, bf16[256,1024]{1,0:T(8,128)(2,1)S(1)} %get-tuple-element.37.refs_1_, bf16[32,256,256]{2,1,0:T(8,128)(2,1)S(1)} %relayout.1.rows_ref.refs_2_), custom_call_target="tpu_custom_call" | custom-call | flops 178956976 | bytes 349525 | tf_op jit(solution)/shard_map/right/pallas_call | solution.py:343
  33.8 2.2 %right.3 = (bf16[64,256]{1,0:T(8,128)(2,1)S(1)}, bf16[64,256]{1,0:T(8,128)(2,1)S(1)}, bf16[64,256]{1,0:T(8,128)(2,1)S(1)}, bf16[64,256]{1,0:T(8,128)(2,1)S(1)}) custom-call(bf16[192,16,128]{2,1,0:T(8,128)(2,1)S(1)} %collective-permute-done.6.refs_0_, bf16[256,1024]{1,0:T(8,128)(2,1)S(1)} %get-tuple-element.37.refs_1_, ...), custom_call_target="tpu_custom_call" | custom-call | flops 536870912 | bytes 1048576 | tf_op jit(solution)/shard_map/right/pallas_call | solution.py:343
  36.0 1.6 %collective-permute-start.8 = (bf16[64,256]{1,0:T(8,128)(2,1)S(1)}, bf16[64,256]{1,0:T(8,128)(2,1)S(1)}, u32[]{:S(2)}, u32[]{:S(2)}) collective-permute-start(bf16[64,256]{1,0:T(8,128)(2,1)S(1)} %get-tuple-element.40), channel_id=1, source_target_pairs={{0,2},{1,3},{2,0},{3,1},{4,6},{5,7},{6,4},{7,5},{8,10},{9,11},{10,... | collective-permute-start | bytes 98312 | tf_op jit(solution)/shard_map/ppermute | solution.py:46
  37.9 0.7 %collective-permute-start.11 = (bf16[256,256]{1,0:T(8,128)(2,1)S(1)}, bf16[256,256]{1,0:T(8,128)(2,1)S(1)}, u32[]{:S(2)}, u32[]{:S(2)}) collective-permute-start(bf16[256,256]{1,0:T(8,128)(2,1)S(1)} %get-tuple-element.42), channel_id=1, source_target_pairs={{4,8},{8,4},{12,16},{16,12},{20,24},{24,20},{5,9},{9,5},{13,17},{1... | collective-permute-start | bytes 393224 | tf_op jit(solution)/shard_map/ppermute | solution.py:42
  38.6 1.4 %collective-permute-done.8.refs_2_ = bf16[64,256]{1,0:T(8,128)(2,1)S(1)} collective-permute-done((bf16[64,256]{1,0:T(8,128)(2,1)S(1)}, bf16[64,256]{1,0:T(8,128)(2,1)S(1)}, u32[]{:S(2)}, u32[]{:S(2)}) %collective-permute-start.8) | collective-permute-done | bytes 32800 | tf_op jit(solution)/shard_map/ppermute | solution.py:46
  40.0 1.0 %collective-permute-done.9.refs_3_ = bf16[64,256]{1,0:T(8,128)(2,1)S(1)} collective-permute-done((bf16[64,256]{1,0:T(8,128)(2,1)S(1)}, bf16[64,256]{1,0:T(8,128)(2,1)S(1)}, u32[]{:S(2)}, u32[]{:S(2)}) %collective-permute-start.9) | collective-permute-done | bytes 32800 | tf_op jit(solution)/shard_map/ppermute | solution.py:46
  41.0 4.3 %collective-permute-start.12 = (bf16[4,64,256]{2,1,0:T(8,128)(2,1)S(1)}, bf16[4,64,256]{2,1,0:T(8,128)(2,1)S(1)}, u32[]{:S(2)}, u32[]{:S(2)}) collective-permute-start(bf16[4,64,256]{2,1,0:T(8,128)(2,1)S(1)} %pad_maximum_fusion.1), channel_id=1, source_target_pairs={{0,4},{4,8},{8,12},{12,16},{16,20},{20,24},{24,28},{1,5},{5,9},{9,... | collective-permute-start | bytes 393224 | tf_op jit(solution)/shard_map/ppermute | solution.py:34
  45.3 1.7 %upper.1 = (f32[1,256,768]{2,1,0:T(8,128)}, f32[256,256]{1,0:T(8,128)S(1)}, f32[2,8,256]{2,1,0:T(8,128)S(1)}) custom-call(s32[1,3]{1,0:T(1,128)S(1)} %copy-done.1, f32[256,256]{1,0:T(8,128)S(1)} %get-tuple-element.35.center_ref, bf16[256,256]{1,0:T(8,128)(2,1)S(1)} %collective-permute-done.10.even_ref, bf16[256,256]{1,0:T(8,128)(2,1)S(1)} %collective-permute-done.11.odd_ref, ...), custom_call_target="tpu_custom_call" | custom-call | flops 89478488 | bytes 262144 | tf_op jit(solution)/shard_map/upper/pallas_call | solution.py:396
  47.0 2.2 %collective-permute-done.12.left_ref = bf16[4,64,256]{2,1,0:T(8,128)(2,1)S(1)} collective-permute-done((bf16[4,64,256]{2,1,0:T(8,128)(2,1)S(1)}, bf16[4,64,256]{2,1,0:T(8,128)(2,1)S(1)}, u32[]{:S(2)}, u32[]{:S(2)}) %collective-permute-start.12) | collective-permute-done | bytes 131104 | tf_op jit(solution)/shard_map/ppermute | solution.py:34
  49.1 1.1 %lower.1 = f32[1,256,768]{2,1,0:T(8,128)} custom-call(f32[2,8,256]{2,1,0:T(8,128)S(1)} %get-tuple-element.48.masks_ref, f32[256,256]{1,0:T(8,128)S(1)} %get-tuple-element.35.center_ref, f32[256,256]{1,0:T(8,128)S(1)} %get-tuple-element.49.middle_ref, bf16[256,256]{1,0:T(8,128)(2,1)S(1)} %collective-permute-done.10.even_ref, ...), custom_call_target="tpu_custom_call", output_to_operand_aliasing={{}: (6, {})} | custom-call | flops 55924052 | bytes 262144 | tf_op jit(solution)/shard_map/lower/pallas_call | solution.py:449
  (22 shorter events, 0.5 us)
Async XLA Ops:
  0.0 3.6 %copy-start.2 = (bf16[1,128,128]{2,1,0:T(8,128)(2,1)S(1)}, bf16[1,128,128]{2,1,0:T(8,128)(2,1)}, u32[]{:S(2)}) copy-start(bf16[1,128,128]{2,1,0:T(8,128)(2,1)} %param.6) | copy-start | bytes 98308
  0.0 3.6 %copy-start.3 = (bf16[1,128,128]{2,1,0:T(8,128)(2,1)S(1)}, bf16[1,128,128]{2,1,0:T(8,128)(2,1)}, u32[]{:S(2)}) copy-start(bf16[1,128,128]{2,1,0:T(8,128)(2,1)} %param.7) | copy-start | bytes 98308
  2.3 12.8 %collective-permute-start = (bf16[81,16,128]{2,1,0:T(8,128)(2,1)}, bf16[81,16,128]{2,1,0:T(8,128)(2,1)S(1)}, u32[]{:S(2)}, u32[]{:S(2)}) collective-permute-start(bf16[81,16,128]{2,1,0:T(8,128)(2,1)} %get-tuple-element.29), channel_id=1, source_target_pairs={{4,0},{8,4},{12,8},{16,12},{20,16},{24,20},{28,24},{5,1},{9,5},{13... | collective-permute-start | bytes 995336 | tf_op jit(solution)/shard_map/ppermute | solution.py:34
  3.6 14.4 %collective-permute-start.2 = (bf16[256,128]{1,0:T(8,128)(2,1)S(1)}, bf16[256,128]{1,0:T(8,128)(2,1)S(1)}, u32[]{:S(2)}, u32[]{:S(2)}) collective-permute-start(bf16[256,128]{1,0:T(8,128)(2,1)S(1)} %get-tuple-element.52), channel_id=1, source_target_pairs={{8,0},{12,4},{16,8},{20,12},{24,16},{28,20},{9,1},{13,5},{17,9},{2... | collective-permute-start | bytes 196616 | tf_op jit(solution)/shard_map/ppermute | solution.py:34
  4.9 13.2 %collective-permute-start.1 = (bf16[256,128]{1,0:T(8,128)(2,1)S(1)}, bf16[256,128]{1,0:T(8,128)(2,1)S(1)}, u32[]{:S(2)}, u32[]{:S(2)}) collective-permute-start(bf16[256,128]{1,0:T(8,128)(2,1)S(1)} %get-tuple-element.52), channel_id=1, source_target_pairs={{0,4},{4,8},{8,12},{12,16},{16,20},{20,24},{24,28},{1,5},{5,9},{9,... | collective-permute-start | bytes 196616 | tf_op jit(solution)/shard_map/ppermute | solution.py:34
  10.4 23.3 %collective-permute-start.6 = (bf16[192,16,128]{2,1,0:T(8,128)(2,1)}, bf16[192,16,128]{2,1,0:T(8,128)(2,1)S(1)}, u32[]{:S(2)}, u32[]{:S(2)}) collective-permute-start(bf16[192,16,128]{2,1,0:T(8,128)(2,1)} %get-tuple-element.36), channel_id=1, source_target_pairs={{4,0},{8,4},{12,8},{16,12},{20,16},{24,20},{28,24},{5,1},{9,5},{13... | collective-permute-start | bytes 2359304 | tf_op jit(solution)/shard_map/ppermute | solution.py:34
  18.1 8.3 %copy-start = (bf16[16,128]{1,0:T(8,128)(2,1)S(1)}, bf16[16,128]{1,0:T(8,128)(2,1)}, u32[]{:S(2)}) copy-start(bf16[16,128]{1,0:T(8,128)(2,1)} %get-tuple-element.28.note_ref) | copy-start | bytes 12292
  18.1 6.8 %collective-permute-start.4 = (bf16[4,256,128]{2,1,0:T(8,128)(2,1)S(1)}, bf16[4,256,128]{2,1,0:T(8,128)(2,1)S(1)}, u32[]{:S(2)}, u32[]{:S(2)}) collective-permute-start(bf16[4,256,128]{2,1,0:T(8,128)(2,1)S(1)} %pad_maximum_fusion.refs_0_), channel_id=1, source_target_pairs={{0,2},{1,3},{2,0},{3,1},{4,6},{5,7},{6,4},{7,5},{8,10},{9,11},{10,... | collective-permute-start | bytes 786440 | tf_op jit(solution)/shard_map/ppermute | solution.py:46
  22.8 2.2 %collective-permute-start.3 = (bf16[4,256,128]{2,1,0:T(8,128)(2,1)S(1)}, bf16[4,256,128]{2,1,0:T(8,128)(2,1)S(1)}, u32[]{:S(2)}, u32[]{:S(2)}) collective-permute-start(bf16[4,256,128]{2,1,0:T(8,128)(2,1)S(1)} %pad_maximum_fusion.refs_0_), channel_id=1, source_target_pairs={{0,1},{1,0},{2,3},{3,2},{4,5},{5,4},{6,7},{7,6},{8,9},{9,8},{10,11... | collective-permute-start | bytes 786440 | tf_op jit(solution)/shard_map/ppermute | solution.py:46
  24.9 1.5 %collective-permute-start.5 = (bf16[4,256,128]{2,1,0:T(8,128)(2,1)S(1)}, bf16[4,256,128]{2,1,0:T(8,128)(2,1)S(1)}, u32[]{:S(2)}, u32[]{:S(2)}) collective-permute-start(bf16[4,256,128]{2,1,0:T(8,128)(2,1)S(1)} %collective-permute-done.4.refs_2_), channel_id=1, source_target_pairs={{0,1},{1,0},{2,3},{3,2},{4,5},{5,4},{6,7},{7,6},{8,9},{9,8},{10,11... | collective-permute-start | bytes 786440 | tf_op jit(solution)/shard_map/ppermute | solution.py:46
  29.8 11.2 %collective-permute-start.10 = (bf16[256,256]{1,0:T(8,128)(2,1)S(1)}, bf16[256,256]{1,0:T(8,128)(2,1)S(1)}, u32[]{:S(2)}, u32[]{:S(2)}) collective-permute-start(bf16[256,256]{1,0:T(8,128)(2,1)S(1)} %get-tuple-element.42), channel_id=1, source_target_pairs={{0,4},{4,0},{8,12},{12,8},{16,20},{20,16},{24,28},{28,24},{1,5},{5... | collective-permute-start | bytes 393224 | tf_op jit(solution)/shard_map/ppermute | solution.py:42
  33.7 11.6 %copy-start.1 = (s32[1,3]{1,0:T(1,128)S(1)}, s32[1,3]{1,0:T(1,128)}, u32[]{:S(2)}) copy-start(s32[1,3]{1,0:T(1,128)} %pattern.1) | copy-start | bytes 40
  36.0 2.6 %collective-permute-start.7 = (bf16[64,256]{1,0:T(8,128)(2,1)S(1)}, bf16[64,256]{1,0:T(8,128)(2,1)S(1)}, u32[]{:S(2)}, u32[]{:S(2)}) collective-permute-start(bf16[64,256]{1,0:T(8,128)(2,1)S(1)} %get-tuple-element.39), channel_id=1, source_target_pairs={{0,1},{1,0},{2,3},{3,2},{4,5},{5,4},{6,7},{7,6},{8,9},{9,8},{10,11... | collective-permute-start | bytes 98312 | tf_op jit(solution)/shard_map/ppermute | solution.py:46
  36.0 4.0 %collective-permute-start.8 = (bf16[64,256]{1,0:T(8,128)(2,1)S(1)}, bf16[64,256]{1,0:T(8,128)(2,1)S(1)}, u32[]{:S(2)}, u32[]{:S(2)}) collective-permute-start(bf16[64,256]{1,0:T(8,128)(2,1)S(1)} %get-tuple-element.40), channel_id=1, source_target_pairs={{0,2},{1,3},{2,0},{3,1},{4,6},{5,7},{6,4},{7,5},{8,10},{9,11},{10,... | collective-permute-start | bytes 98312 | tf_op jit(solution)/shard_map/ppermute | solution.py:46
  37.6 3.3 %collective-permute-start.9 = (bf16[64,256]{1,0:T(8,128)(2,1)S(1)}, bf16[64,256]{1,0:T(8,128)(2,1)S(1)}, u32[]{:S(2)}, u32[]{:S(2)}) collective-permute-start(bf16[64,256]{1,0:T(8,128)(2,1)S(1)} %get-tuple-element.41), channel_id=1, source_target_pairs={{0,3},{1,2},{2,1},{3,0},{4,7},{5,6},{6,5},{7,4},{8,11},{9,10},{10,... | collective-permute-start | bytes 98312 | tf_op jit(solution)/shard_map/ppermute | solution.py:46
  37.9 7.4 %collective-permute-start.11 = (bf16[256,256]{1,0:T(8,128)(2,1)S(1)}, bf16[256,256]{1,0:T(8,128)(2,1)S(1)}, u32[]{:S(2)}, u32[]{:S(2)}) collective-permute-start(bf16[256,256]{1,0:T(8,128)(2,1)S(1)} %get-tuple-element.42), channel_id=1, source_target_pairs={{4,8},{8,4},{12,16},{16,12},{20,24},{24,20},{5,9},{9,5},{13,17},{1... | collective-permute-start | bytes 393224 | tf_op jit(solution)/shard_map/ppermute | solution.py:42
  41.0 8.1 %collective-permute-start.12 = (bf16[4,64,256]{2,1,0:T(8,128)(2,1)S(1)}, bf16[4,64,256]{2,1,0:T(8,128)(2,1)S(1)}, u32[]{:S(2)}, u32[]{:S(2)}) collective-permute-start(bf16[4,64,256]{2,1,0:T(8,128)(2,1)S(1)} %pad_maximum_fusion.1), channel_id=1, source_target_pairs={{0,4},{4,8},{8,12},{12,16},{16,20},{20,24},{24,28},{1,5},{5,9},{9,... | collective-permute-start | bytes 393224 | tf_op jit(solution)/shard_map/ppermute | solution.py:34

commit v7 on v6

--- a/solution.py
+++ b/solution.py
@@ -72,8 +72,8 @@
 def turn(source, lead, rows, lines, put):
     swap = swap_matrix(TILE)
     places = [(r, c) for r in range(0, rows, TILE) for c in range(0, lines, TILE)]
-    for at in range(0, len(places), 2):
-        pair = places[at : at + 2]
+    for at in range(0, len(places), 4):
+        pair = places[at : at + 4]
         blocks = [
             jnp.concatenate([source(lead + r + i, c) for i in range(TILE)], 0) for r, c in pair
         ]
@@ -250,7 +250,7 @@
     return mm_nt(jnp.concatenate(left, 1), right)
 
 
-def center_kernel(scale, group, rows_ref, weight_ref, out_ref, low_ref):
+def center_kernel(scale, group, rows_ref, weight_ref, out_ref, low_ref, quarters_ref):
     mus, rows, width = rows_ref.shape
     total = None
     for first in range(0, mus, group):
@@ -260,19 +260,26 @@
         part = product(rows_ref, first, group, left)
         total = part if total is None else total + part
     out_ref[...] = scale * total
-    low_ref[...] = (scale * total).astype(bf16)
+    low = (scale * total).astype(bf16)
+    half = rows // 2
+    low_ref[...] = low
+    quarters_ref[0] = low[:half, :half]
+    quarters_ref[1] = low[:half, half:]
+    quarters_ref[2] = low[half:, half:]
 
 
 def center_block(scale, turned_rows, weight, group):
     mus, rows, width = turned_rows.shape
+    half = rows // 2
     return pl.pallas_call(
         functools.partial(center_kernel, scale, group),
         out_shape=[
             jax.ShapeDtypeStruct((rows, rows), f32),
             jax.ShapeDtypeStruct((rows, rows), bf16),
+            jax.ShapeDtypeStruct((3, half, half), bf16),
         ],
         in_specs=spec_all(2),
-        out_specs=spec_all(2),
+        out_specs=spec_all(3),
         compiler_params=pltpu.CompilerParams(vmem_limit_bytes=VMEM_BYTES),
         cost_estimate=pl.CostEstimate(
             flops=2 * mus * rows * width * (width + rows) // COST,
@@ -363,6 +370,13 @@
     return high, (value - high.astype(f32)).astype(bf16)
 
 
+def whole_block(quarters):
+    first, second, last = quarters[0], quarters[1], quarters[2]
+    return jnp.concatenate(
+        [jnp.concatenate([first, second], 1), jnp.concatenate([second.T, last], 1)], 0
+    )
+
+
 def upper_kernel(n, pattern, center_ref, even_ref, odd_ref, *refs):
     pieces, (out_ref, middle_ref, masks_ref, right_t, block, sem) = refs[:n], refs[n:]
     me = lax.axis_index("tm")
@@ -372,7 +386,7 @@
         start = pl.multiple_of((me ^ i) * cols, cols)
         right_t[pl.ds(start, cols), :] = pieces[i][...]
     parity = lax.axis_index("region") % 2
-    above = jnp.where(parity == 0, even_ref[...], odd_ref[...])
+    above = jnp.where(parity == 0, whole_block(even_ref), odd_ref[...])
     mask = pattern[0, 2].astype(f32)
     upper = right_t[...].T * mask.astype(bf16)
     center = center_ref[...]
@@ -423,7 +437,7 @@
         start = pl.multiple_of((me ^ i) * cols, cols)
         left[pl.ds(start, cols), :] = left_ref[i]
     parity = lax.axis_index("region") % 2
-    below = jnp.where(parity == 0, odd_ref[...], even_ref[...])
+    below = jnp.where(parity == 0, odd_ref[...], whole_block(even_ref))
     masks = [masks_ref[e, :1, :] for e in range(2)]
     lower = left[...] * masks[0].astype(bf16)
     high, low = split(center_ref[...])
@@ -499,7 +513,7 @@
         note, far_head, 2 * blocks, [greens[i] for i in range(n)]
     )
 
-    center, center_low = center_block(scale, turned_rows, center_weight, 2)
+    center, center_low, quarters = center_block(scale, turned_rows, center_weight, 2)
 
     right_weight, center = lax.optimization_barrier((right_weight, center))
     lead = 2 * blocks + 1
@@ -515,7 +529,7 @@
     for i in range(n - 1, 0, -1):
         pieces[i] = partner(parts[i], i)
     pieces = [pieces[i] for i in range(n)]
-    even, odd = swap_pairs(center_low, 0), swap_pairs(center_low, 1)
+    even, odd = swap_pairs(quarters, 0), swap_pairs(center_low, 1)
     *pieces, even = lax.optimization_barrier((*pieces, even))
     left = shift(jnp.stack(pieces, 0), 1)
     out, middle, masks = upper_blocks(pattern, center, even, odd, pieces)

time: 50.5 us -> 50.5 us (level)
  no operation moved by 1% of the time
where the time goes in v7:
time: 50.5 us; the launch traced here: 50.3 us
  starting transfers between devices  20.8 us (41%)
  Pallas kernels  14.7 us (29%)
  waiting for transfers between devices  14.5 us (29%)
    ppermute x5, starting transfers between devices, shift(): return lax.ppermute(block, 'region', route)  13.6 us
    ppermute x5, waiting for transfers between devices, shift(): return lax.ppermute(block, 'region', route)  8.5 us
    ppermute x6, waiting for transfers between devices, partner(): lax.ppermute(block, 'tm', [(i, i ^ bit) for i in range(lax.axis_size('tm'...  5.99 us
    ppermute x6, starting transfers between devices, partner(): lax.ppermute(block, 'tm', [(i, i ^ bit) for i in range(lax.axis_size('tm'...  3.59 us
    ppermute x2, starting transfers between devices, swap_pairs(): return lax.ppermute(block, 'region', route)  3.52 us
    pallas_call x2, Pallas kernels, right_part(): pl.pallas_call(functools.partial(right_kernel, n, kb, spans, leads, group...  3.26 us
    pallas_call x1, Pallas kernels, relayout(): pl.pallas_call(functools.partial(relayout_kernel, kb, chunks), out_shape=...  3.02 us
    pallas_call x1, Pallas kernels, center_block(): pl.pallas_call(functools.partial(center_kernel, scale, group), out_shape=...  2.59 us
  transfers between devices with their start and end apart: 13, of which 7 were waited for; matrix products, arithmetic and copies ran while one was open for 0% of the time, Pallas kernels for 22%

profile of v7, /device:TPU:0, one launch (start us, length us, event | category | flops | bytes accessed | tf_op | source)
XLA Modules:
  0.0 50.3 jit_solution(576484675838114278)
XLA Ops:
  0.0 2.3 %prepare.1 = (bf16[81,16,128]{2,1,0:T(8,128)(2,1)}, bf16[192,16,128]{2,1,0:T(8,128)(2,1)}, bf16[16,128]{1,0:T(8,128)(2,1)}) custom-call(s32[1,2]{1,0:T(1,128)} %offsets_ref.1, bf16[256,64,128]{2,1,0:T(8,128)(2,1)} %bitcast.18, bf16[8,16,128]{2,1,0:T(8,128)(2,1)} %bitcast.21, bf16[8,16,128]{2,1,0:T(8,128)(2,1)} %bitcast.23), custom_call_target="tpu_custom_call" | custom-call | bytes 349525 | tf_op jit(solution)/shard_map/prepare/pallas_call | solution.py:171
  2.3 1.3 %collective-permute-start = (bf16[81,16,128]{2,1,0:T(8,128)(2,1)}, bf16[81,16,128]{2,1,0:T(8,128)(2,1)S(1)}, u32[]{:S(2)}, u32[]{:S(2)}) collective-permute-start(bf16[81,16,128]{2,1,0:T(8,128)(2,1)} %get-tuple-element.30), channel_id=1, source_target_pairs={{4,0},{8,4},{12,8},{16,12},{20,16},{24,20},{28,24},{5,1},{9,5},{13... | collective-permute-start | bytes 995336 | tf_op jit(solution)/shard_map/ppermute | solution.py:34
  3.6 1.3 %collective-permute-start.2 = (bf16[256,128]{1,0:T(8,128)(2,1)S(1)}, bf16[256,128]{1,0:T(8,128)(2,1)S(1)}, u32[]{:S(2)}, u32[]{:S(2)}) collective-permute-start(bf16[256,128]{1,0:T(8,128)(2,1)S(1)} %get-tuple-element.54), channel_id=1, source_target_pairs={{8,0},{12,4},{16,8},{20,12},{24,16},{28,20},{9,1},{13,5},{17,9},{2... | collective-permute-start | bytes 196616 | tf_op jit(solution)/shard_map/ppermute | solution.py:34
  4.9 5.5 %collective-permute-start.1 = (bf16[256,128]{1,0:T(8,128)(2,1)S(1)}, bf16[256,128]{1,0:T(8,128)(2,1)S(1)}, u32[]{:S(2)}, u32[]{:S(2)}) collective-permute-start(bf16[256,128]{1,0:T(8,128)(2,1)S(1)} %get-tuple-element.54), channel_id=1, source_target_pairs={{0,4},{4,8},{8,12},{12,16},{16,20},{20,24},{24,28},{1,5},{5,9},{9,... | collective-permute-start | bytes 196616 | tf_op jit(solution)/shard_map/ppermute | solution.py:34
  10.4 1.3 %collective-permute-start.6 = (bf16[192,16,128]{2,1,0:T(8,128)(2,1)}, bf16[192,16,128]{2,1,0:T(8,128)(2,1)S(1)}, u32[]{:S(2)}, u32[]{:S(2)}) collective-permute-start(bf16[192,16,128]{2,1,0:T(8,128)(2,1)} %get-tuple-element.37), channel_id=1, source_target_pairs={{4,0},{8,4},{12,8},{16,12},{20,16},{24,20},{28,24},{5,1},{9,5},{13... | collective-permute-start | bytes 2359304 | tf_op jit(solution)/shard_map/ppermute | solution.py:34
  11.7 3.4 %collective-permute-done.head_ref.refs_0_ = bf16[81,16,128]{2,1,0:T(8,128)(2,1)S(1)} collective-permute-done((bf16[81,16,128]{2,1,0:T(8,128)(2,1)}, bf16[81,16,128]{2,1,0:T(8,128)(2,1)S(1)}, u32[]{:S(2)}, u32[]{:S(2)}) %collective-permute-start) | collective-permute-done | bytes 331808 | tf_op jit(solution)/shard_map/ppermute | solution.py:34
  15.2 2.9 %collective-permute-done.2 = bf16[256,128]{1,0:T(8,128)(2,1)S(1)} collective-permute-done((bf16[256,128]{1,0:T(8,128)(2,1)S(1)}, bf16[256,128]{1,0:T(8,128)(2,1)S(1)}, u32[]{:S(2)}, u32[]{:S(2)}) %collective-permute-start.2) | collective-permute-done | bytes 65568 | tf_op jit(solution)/shard_map/ppermute | solution.py:34
  18.1 1.6 %collective-permute-start.4 = (bf16[4,256,128]{2,1,0:T(8,128)(2,1)S(1)}, bf16[4,256,128]{2,1,0:T(8,128)(2,1)S(1)}, u32[]{:S(2)}, u32[]{:S(2)}) collective-permute-start(bf16[4,256,128]{2,1,0:T(8,128)(2,1)S(1)} %pad_maximum_fusion.refs_0_), channel_id=1, source_target_pairs={{0,2},{1,3},{2,0},{3,1},{4,6},{5,7},{6,4},{7,5},{8,10},{9,11},{10,... | collective-permute-start | bytes 786440 | tf_op jit(solution)/shard_map/ppermute | solution.py:46
  19.7 3.0 %relayout.1.rows_ref.refs_2_ = bf16[32,256,256]{2,1,0:T(8,128)(2,1)S(1)} custom-call(bf16[256,64,128]{2,1,0:T(8,128)(2,1)} %bitcast.19), custom_call_target="tpu_custom_call" | custom-call | bytes 2796202 | tf_op jit(solution)/shard_map/relayout/pallas_call | solution.py:111
  22.8 2.1 %collective-permute-done.4.refs_2_ = bf16[4,256,128]{2,1,0:T(8,128)(2,1)S(1)} collective-permute-done((bf16[4,256,128]{2,1,0:T(8,128)(2,1)S(1)}, bf16[4,256,128]{2,1,0:T(8,128)(2,1)S(1)}, u32[]{:S(2)}, u32[]{:S(2)}) %collective-permute-start.4) | collective-permute-done | bytes 262176 | tf_op jit(solution)/shard_map/ppermute | solution.py:46
  24.9 1.5 %collective-permute-done.5.refs_3_ = bf16[4,256,128]{2,1,0:T(8,128)(2,1)S(1)} collective-permute-done((bf16[4,256,128]{2,1,0:T(8,128)(2,1)S(1)}, bf16[4,256,128]{2,1,0:T(8,128)(2,1)S(1)}, u32[]{:S(2)}, u32[]{:S(2)}) %collective-permute-start.5) | collective-permute-done | bytes 262176 | tf_op jit(solution)/shard_map/ppermute | solution.py:46
  26.4 0.8 %weights.1 = (bf16[256,256]{1,0:T(8,128)(2,1)S(1)}, bf16[256,1024]{1,0:T(8,128)(2,1)S(1)}) custom-call(bf16[16,128]{1,0:T(8,128)(2,1)S(1)} %copy-done, bf16[81,16,128]{2,1,0:T(8,128)(2,1)S(1)} %collective-permute-done.head_ref.refs_0_, bf16[4,256,128]{2,1,0:T(8,128)(2,1)S(1)} %pad_maximum_fusion.refs_0_, ...), custom_call_target="tpu_custom_call" | custom-call | flops 89478488 | bytes 349525 | tf_op jit(solution)/shard_map/weights/pallas_call | solution.py:231
  27.2 2.6 %center.1 = (f32[256,256]{1,0:T(8,128)S(1)}, bf16[256,256]{1,0:T(8,128)(2,1)S(1)}, bf16[3,128,128]{2,1,0:T(8,128)(2,1)S(1)}) custom-call(bf16[32,256,256]{2,1,0:T(8,128)(2,1)S(1)} %relayout.1.rows_ref.refs_2_, bf16[256,256]{1,0:T(8,128)(2,1)S(1)} %get-tuple-element.34.weight_ref), custom_call_target="tpu_custom_call" | custom-call | flops 715827904 | bytes 1398101 | tf_op jit(solution)/shard_map/center/pallas_call | solution.py:274
  29.8 2.9 %collective-permute-start.10 = (bf16[3,128,128]{2,1,0:T(8,128)(2,1)S(1)}, bf16[3,128,128]{2,1,0:T(8,128)(2,1)S(1)}, u32[]{:S(2)}, u32[]{:S(2)}) collective-permute-start(bf16[3,128,128]{2,1,0:T(8,128)(2,1)S(1)} %get-tuple-element.43), channel_id=1, source_target_pairs={{0,4},{4,0},{8,12},{12,8},{16,20},{20,16},{24,28},{28,24},{1,5},{5... | collective-permute-start | bytes 294920 | tf_op jit(solution)/shard_map/ppermute | solution.py:42
  32.7 1.1 %right.2.refs_3_ = f32[256,256]{1,0:T(8,128)S(1)} custom-call(bf16[81,16,128]{2,1,0:T(8,128)(2,1)S(1)} %collective-permute-done.head_ref.refs_0_, bf16[256,1024]{1,0:T(8,128)(2,1)S(1)} %get-tuple-element.38.refs_1_, bf16[32,256,256]{2,1,0:T(8,128)(2,1)S(1)} %relayout.1.rows_ref.refs_2_), custom_call_target="tpu_custom_call" | custom-call | flops 178956976 | bytes 349525 | tf_op jit(solution)/shard_map/right/pallas_call | solution.py:350
  33.8 2.2 %right.3 = (bf16[64,256]{1,0:T(8,128)(2,1)S(1)}, bf16[64,256]{1,0:T(8,128)(2,1)S(1)}, bf16[64,256]{1,0:T(8,128)(2,1)S(1)}, bf16[64,256]{1,0:T(8,128)(2,1)S(1)}) custom-call(bf16[192,16,128]{2,1,0:T(8,128)(2,1)S(1)} %collective-permute-done.6.refs_0_, bf16[256,1024]{1,0:T(8,128)(2,1)S(1)} %get-tuple-element.38.refs_1_, ...), custom_call_target="tpu_custom_call" | custom-call | flops 536870912 | bytes 1048576 | tf_op jit(solution)/shard_map/right/pallas_call | solution.py:350
  36.0 1.6 %collective-permute-start.8 = (bf16[64,256]{1,0:T(8,128)(2,1)S(1)}, bf16[64,256]{1,0:T(8,128)(2,1)S(1)}, u32[]{:S(2)}, u32[]{:S(2)}) collective-permute-start(bf16[64,256]{1,0:T(8,128)(2,1)S(1)} %get-tuple-element.41), channel_id=1, source_target_pairs={{0,2},{1,3},{2,0},{3,1},{4,6},{5,7},{6,4},{7,5},{8,10},{9,11},{10,... | collective-permute-start | bytes 98312 | tf_op jit(solution)/shard_map/ppermute | solution.py:46
  37.9 0.7 %collective-permute-start.11 = (bf16[256,256]{1,0:T(8,128)(2,1)S(1)}, bf16[256,256]{1,0:T(8,128)(2,1)S(1)}, u32[]{:S(2)}, u32[]{:S(2)}) collective-permute-start(bf16[256,256]{1,0:T(8,128)(2,1)S(1)} %get-tuple-element.45), channel_id=1, source_target_pairs={{4,8},{8,4},{12,16},{16,12},{20,24},{24,20},{5,9},{9,5},{13,17},{1... | collective-permute-start | bytes 393224 | tf_op jit(solution)/shard_map/ppermute | solution.py:42
  38.6 1.4 %collective-permute-done.8.refs_2_ = bf16[64,256]{1,0:T(8,128)(2,1)S(1)} collective-permute-done((bf16[64,256]{1,0:T(8,128)(2,1)S(1)}, bf16[64,256]{1,0:T(8,128)(2,1)S(1)}, u32[]{:S(2)}, u32[]{:S(2)}) %collective-permute-start.8) | collective-permute-done | bytes 32800 | tf_op jit(solution)/shard_map/ppermute | solution.py:46
  40.0 0.9 %collective-permute-done.9.refs_3_ = bf16[64,256]{1,0:T(8,128)(2,1)S(1)} collective-permute-done((bf16[64,256]{1,0:T(8,128)(2,1)S(1)}, bf16[64,256]{1,0:T(8,128)(2,1)S(1)}, u32[]{:S(2)}, u32[]{:S(2)}) %collective-permute-start.9) | collective-permute-done | bytes 32800 | tf_op jit(solution)/shard_map/ppermute | solution.py:46
  41.0 4.3 %collective-permute-start.12 = (bf16[4,64,256]{2,1,0:T(8,128)(2,1)S(1)}, bf16[4,64,256]{2,1,0:T(8,128)(2,1)S(1)}, u32[]{:S(2)}, u32[]{:S(2)}) collective-permute-start(bf16[4,64,256]{2,1,0:T(8,128)(2,1)S(1)} %pad_maximum_fusion.1), channel_id=1, source_target_pairs={{0,4},{4,8},{8,12},{12,16},{16,20},{20,24},{24,28},{1,5},{5,9},{9,... | collective-permute-start | bytes 393224 | tf_op jit(solution)/shard_map/ppermute | solution.py:34
  45.3 1.7 %upper.1 = (f32[1,256,768]{2,1,0:T(8,128)}, f32[256,256]{1,0:T(8,128)S(1)}, f32[2,8,256]{2,1,0:T(8,128)S(1)}) custom-call(s32[1,3]{1,0:T(1,128)S(1)} %copy-done.1, f32[256,256]{1,0:T(8,128)S(1)} %get-tuple-element.36.center_ref, bf16[3,128,128]{2,1,0:T(8,128)(2,1)S(1)} %collective-permute-done.10.even_ref, ...), custom_call_target="tpu_custom_call" | custom-call | flops 89478488 | bytes 262144 | tf_op jit(solution)/shard_map/upper/pallas_call | solution.py:410
  47.0 2.1 %collective-permute-done.12.left_ref = bf16[4,64,256]{2,1,0:T(8,128)(2,1)S(1)} collective-permute-done((bf16[4,64,256]{2,1,0:T(8,128)(2,1)S(1)}, bf16[4,64,256]{2,1,0:T(8,128)(2,1)S(1)}, u32[]{:S(2)}, u32[]{:S(2)}) %collective-permute-start.12) | collective-permute-done | bytes 131104 | tf_op jit(solution)/shard_map/ppermute | solution.py:34
  49.1 1.1 %lower.1 = f32[1,256,768]{2,1,0:T(8,128)} custom-call(f32[2,8,256]{2,1,0:T(8,128)S(1)} %get-tuple-element.50.masks_ref, f32[256,256]{1,0:T(8,128)S(1)} %get-tuple-element.36.center_ref, f32[256,256]{1,0:T(8,128)S(1)} %get-tuple-element.51.middle_ref, bf16[3,128,128]{2,1,0:T(8,128)(2,1)S(1)} %collective-permute-done.10.even_ref, ...), custom_call_target="tpu_custom_call", output_to_operand_aliasing={{}: (6, {})} | custom-call | flops 55924052 | bytes 262144 | tf_op jit(solution)/shard_map/lower/pallas_call | solution.py:463
  (22 shorter events, 0.5 us)
Async XLA Ops:
  0.0 3.6 %copy-start.2 = (bf16[1,128,128]{2,1,0:T(8,128)(2,1)S(1)}, bf16[1,128,128]{2,1,0:T(8,128)(2,1)}, u32[]{:S(2)}) copy-start(bf16[1,128,128]{2,1,0:T(8,128)(2,1)} %param.6) | copy-start | bytes 98308
  0.0 3.6 %copy-start.3 = (bf16[1,128,128]{2,1,0:T(8,128)(2,1)S(1)}, bf16[1,128,128]{2,1,0:T(8,128)(2,1)}, u32[]{:S(2)}) copy-start(bf16[1,128,128]{2,1,0:T(8,128)(2,1)} %param.7) | copy-start | bytes 98308
  2.3 12.8 %collective-permute-start = (bf16[81,16,128]{2,1,0:T(8,128)(2,1)}, bf16[81,16,128]{2,1,0:T(8,128)(2,1)S(1)}, u32[]{:S(2)}, u32[]{:S(2)}) collective-permute-start(bf16[81,16,128]{2,1,0:T(8,128)(2,1)} %get-tuple-element.30), channel_id=1, source_target_pairs={{4,0},{8,4},{12,8},{16,12},{20,16},{24,20},{28,24},{5,1},{9,5},{13... | collective-permute-start | bytes 995336 | tf_op jit(solution)/shard_map/ppermute | solution.py:34
  3.6 14.4 %collective-permute-start.2 = (bf16[256,128]{1,0:T(8,128)(2,1)S(1)}, bf16[256,128]{1,0:T(8,128)(2,1)S(1)}, u32[]{:S(2)}, u32[]{:S(2)}) collective-permute-start(bf16[256,128]{1,0:T(8,128)(2,1)S(1)} %get-tuple-element.54), channel_id=1, source_target_pairs={{8,0},{12,4},{16,8},{20,12},{24,16},{28,20},{9,1},{13,5},{17,9},{2... | collective-permute-start | bytes 196616 | tf_op jit(solution)/shard_map/ppermute | solution.py:34
  4.9 13.2 %collective-permute-start.1 = (bf16[256,128]{1,0:T(8,128)(2,1)S(1)}, bf16[256,128]{1,0:T(8,128)(2,1)S(1)}, u32[]{:S(2)}, u32[]{:S(2)}) collective-permute-start(bf16[256,128]{1,0:T(8,128)(2,1)S(1)} %get-tuple-element.54), channel_id=1, source_target_pairs={{0,4},{4,8},{8,12},{12,16},{16,20},{20,24},{24,28},{1,5},{5,9},{9,... | collective-permute-start | bytes 196616 | tf_op jit(solution)/shard_map/ppermute | solution.py:34
  10.4 23.3 %collective-permute-start.6 = (bf16[192,16,128]{2,1,0:T(8,128)(2,1)}, bf16[192,16,128]{2,1,0:T(8,128)(2,1)S(1)}, u32[]{:S(2)}, u32[]{:S(2)}) collective-permute-start(bf16[192,16,128]{2,1,0:T(8,128)(2,1)} %get-tuple-element.37), channel_id=1, source_target_pairs={{4,0},{8,4},{12,8},{16,12},{20,16},{24,20},{28,24},{5,1},{9,5},{13... | collective-permute-start | bytes 2359304 | tf_op jit(solution)/shard_map/ppermute | solution.py:34
  18.1 8.3 %copy-start = (bf16[16,128]{1,0:T(8,128)(2,1)S(1)}, bf16[16,128]{1,0:T(8,128)(2,1)}, u32[]{:S(2)}) copy-start(bf16[16,128]{1,0:T(8,128)(2,1)} %get-tuple-element.29.note_ref) | copy-start | bytes 12292
  18.1 6.8 %collective-permute-start.4 = (bf16[4,256,128]{2,1,0:T(8,128)(2,1)S(1)}, bf16[4,256,128]{2,1,0:T(8,128)(2,1)S(1)}, u32[]{:S(2)}, u32[]{:S(2)}) collective-permute-start(bf16[4,256,128]{2,1,0:T(8,128)(2,1)S(1)} %pad_maximum_fusion.refs_0_), channel_id=1, source_target_pairs={{0,2},{1,3},{2,0},{3,1},{4,6},{5,7},{6,4},{7,5},{8,10},{9,11},{10,... | collective-permute-start | bytes 786440 | tf_op jit(solution)/shard_map/ppermute | solution.py:46
  22.8 2.2 %collective-permute-start.3 = (bf16[4,256,128]{2,1,0:T(8,128)(2,1)S(1)}, bf16[4,256,128]{2,1,0:T(8,128)(2,1)S(1)}, u32[]{:S(2)}, u32[]{:S(2)}) collective-permute-start(bf16[4,256,128]{2,1,0:T(8,128)(2,1)S(1)} %pad_maximum_fusion.refs_0_), channel_id=1, source_target_pairs={{0,1},{1,0},{2,3},{3,2},{4,5},{5,4},{6,7},{7,6},{8,9},{9,8},{10,11... | collective-permute-start | bytes 786440 | tf_op jit(solution)/shard_map/ppermute | solution.py:46
  24.9 1.5 %collective-permute-start.5 = (bf16[4,256,128]{2,1,0:T(8,128)(2,1)S(1)}, bf16[4,256,128]{2,1,0:T(8,128)(2,1)S(1)}, u32[]{:S(2)}, u32[]{:S(2)}) collective-permute-start(bf16[4,256,128]{2,1,0:T(8,128)(2,1)S(1)} %collective-permute-done.4.refs_2_), channel_id=1, source_target_pairs={{0,1},{1,0},{2,3},{3,2},{4,5},{5,4},{6,7},{7,6},{8,9},{9,8},{10,11... | collective-permute-start | bytes 786440 | tf_op jit(solution)/shard_map/ppermute | solution.py:46
  29.8 11.2 %collective-permute-start.10 = (bf16[3,128,128]{2,1,0:T(8,128)(2,1)S(1)}, bf16[3,128,128]{2,1,0:T(8,128)(2,1)S(1)}, u32[]{:S(2)}, u32[]{:S(2)}) collective-permute-start(bf16[3,128,128]{2,1,0:T(8,128)(2,1)S(1)} %get-tuple-element.43), channel_id=1, source_target_pairs={{0,4},{4,0},{8,12},{12,8},{16,20},{20,16},{24,28},{28,24},{1,5},{5... | collective-permute-start | bytes 294920 | tf_op jit(solution)/shard_map/ppermute | solution.py:42
  33.7 11.6 %copy-start.1 = (s32[1,3]{1,0:T(1,128)S(1)}, s32[1,3]{1,0:T(1,128)}, u32[]{:S(2)}) copy-start(s32[1,3]{1,0:T(1,128)} %pattern.1) | copy-start | bytes 40
  36.0 2.6 %collective-permute-start.7 = (bf16[64,256]{1,0:T(8,128)(2,1)S(1)}, bf16[64,256]{1,0:T(8,128)(2,1)S(1)}, u32[]{:S(2)}, u32[]{:S(2)}) collective-permute-start(bf16[64,256]{1,0:T(8,128)(2,1)S(1)} %get-tuple-element.40), channel_id=1, source_target_pairs={{0,1},{1,0},{2,3},{3,2},{4,5},{5,4},{6,7},{7,6},{8,9},{9,8},{10,11... | collective-permute-start | bytes 98312 | tf_op jit(solution)/shard_map/ppermute | solution.py:46
  36.0 4.0 %collective-permute-start.8 = (bf16[64,256]{1,0:T(8,128)(2,1)S(1)}, bf16[64,256]{1,0:T(8,128)(2,1)S(1)}, u32[]{:S(2)}, u32[]{:S(2)}) collective-permute-start(bf16[64,256]{1,0:T(8,128)(2,1)S(1)} %get-tuple-element.41), channel_id=1, source_target_pairs={{0,2},{1,3},{2,0},{3,1},{4,6},{5,7},{6,4},{7,5},{8,10},{9,11},{10,... | collective-permute-start | bytes 98312 | tf_op jit(solution)/shard_map/ppermute | solution.py:46
  37.6 3.3 %collective-permute-start.9 = (bf16[64,256]{1,0:T(8,128)(2,1)S(1)}, bf16[64,256]{1,0:T(8,128)(2,1)S(1)}, u32[]{:S(2)}, u32[]{:S(2)}) collective-permute-start(bf16[64,256]{1,0:T(8,128)(2,1)S(1)} %get-tuple-element.42), channel_id=1, source_target_pairs={{0,3},{1,2},{2,1},{3,0},{4,7},{5,6},{6,5},{7,4},{8,11},{9,10},{10,... | collective-permute-start | bytes 98312 | tf_op jit(solution)/shard_map/ppermute | solution.py:46
  37.9 7.4 %collective-permute-start.11 = (bf16[256,256]{1,0:T(8,128)(2,1)S(1)}, bf16[256,256]{1,0:T(8,128)(2,1)S(1)}, u32[]{:S(2)}, u32[]{:S(2)}) collective-permute-start(bf16[256,256]{1,0:T(8,128)(2,1)S(1)} %get-tuple-element.45), channel_id=1, source_target_pairs={{4,8},{8,4},{12,16},{16,12},{20,24},{24,20},{5,9},{9,5},{13,17},{1... | collective-permute-start | bytes 393224 | tf_op jit(solution)/shard_map/ppermute | solution.py:42
  41.0 8.2 %collective-permute-start.12 = (bf16[4,64,256]{2,1,0:T(8,128)(2,1)S(1)}, bf16[4,64,256]{2,1,0:T(8,128)(2,1)S(1)}, u32[]{:S(2)}, u32[]{:S(2)}) collective-permute-start(bf16[4,64,256]{2,1,0:T(8,128)(2,1)S(1)} %pad_maximum_fusion.1), channel_id=1, source_target_pairs={{0,4},{4,8},{8,12},{12,16},{16,20},{20,24},{24,28},{1,5},{5,9},{9,... | collective-permute-start | bytes 393224 | tf_op jit(solution)/shard_map/ppermute | solution.py:34
